TPU v7x, 32 devices: a whole 2x2x4 slice. The times are simulated.
32 devices in a mesh: day: 4 (over x, core), year: 4 (over z), region: 2 (over y).
Axes of the slice: x: 2, y: 2, z: 4, core: 2. Of those that a mesh axis runs over, the one named last changes fastest.
Arguments:
- samples: bfloat16 [92, 8, 2000, 256], P('day', 'year', 'region'), parts along dimension 2, may hold values from -24 to 24, as said below
- counts: int32 [2, 92, 8], P('region', 'day', 'year'), parts along dimension 0, may hold values from 500 to 1000, as said below
Outputs:
- covariance: float32 [2, 92, 256, 256], P('region', 'day', 'year'), parts along dimension 0
- window_mean: float32 [2, 92, 256], P('region', 'day', 'year'), parts along dimension 0
There are 2 independent parts, one for each index of `region`. A program takes and returns all parts, laid end to end along the dimension named above; each array names one. Nothing has to cross between parts.
Inputs may be any that keep to these rules, and one draw needn't show every extreme that they name: `counts`: every entry lies between 500 and 1000; both ends are taken in every draw. `samples`: finite profile values.
All inputs are finite; a program needn't handle non-finite values.
Results may differ from a plain program's by a relative error of at most 0.0003.
Values sent between devices are 32-bit elements; how exact they have to be, the bound alone decides.
No kernel may reach another device: no remote copies, remote signals or barrier semaphores. Data moves between devices by JAX's collectives and lax.ppermute only.
A program may use at most 128 MiB of HBM per device.

v0:
```python
import jax
import jax.numpy as jnp
from jax import lax
from jax.sharding import PartitionSpec as P

HALF = 7


def extended(cells, sides, width):
    for axis, dim in sides:
        count = lax.axis_size(axis)
        head = lax.slice_in_dim(cells, 0, width, axis=dim)
        tail = lax.slice_in_dim(cells, cells.shape[dim] - width, cells.shape[dim], axis=dim)
        cells = jnp.concatenate(
            [
                lax.ppermute(tail, axis, [(i, (i + 1) % count) for i in range(count)]),
                cells,
                lax.ppermute(head, axis, [((i + 1) % count, i) for i in range(count)]),
            ],
            axis=dim,
        )
    return cells


def window_total(padded, days):
    total = padded[0:days]
    for offset in range(1, 2 * HALF + 1):
        total = total + padded[offset : offset + days]
    return total


def shards(samples, counts):
    days, groups, slots, width = samples.shape
    parts_year = lax.axis_size("year")
    share = width // parts_year
    slot_index = lax.broadcasted_iota(jnp.int32, (days, groups, slots), 2)
    valid = slot_index < counts[0][:, :, None]
    masked = jnp.where(valid[..., None], samples, jnp.zeros_like(samples))
    day_gram = jnp.einsum("dgsf,dgsh->dfh", masked, masked, preferred_element_type=jnp.float32)
    day_sum = jnp.sum(masked, axis=(1, 2), dtype=jnp.float32)
    day_count = jnp.sum(counts[0], axis=1).astype(jnp.float32)
    extra = jnp.zeros((days, 8, width), jnp.float32)
    extra = extra.at[:, 0, :].set(day_sum)
    extra = extra.at[:, 1, :].set(jnp.broadcast_to(day_count[:, None], (days, width)))
    blocks = day_gram.reshape(days, parts_year, share, width)
    extra_all = jnp.broadcast_to(extra[:, None], (days, parts_year, 8, width))
    stacked = jnp.concatenate([blocks, extra_all], axis=2).reshape(
        days, parts_year * (share + 8), width
    )
    summed = lax.psum_scatter(stacked, "year", scatter_dimension=1, tiled=True)
    padded = extended(summed, (("day", 0),), HALF)
    merged = window_total(padded, days)
    win_gram = merged[:, :share, :]
    win_sum = merged[:, share, :]
    win_count = merged[:, share + 1, 0]
    full_mean = win_sum / win_count[:, None]
    start = lax.axis_index("year") * share
    own_mean = lax.dynamic_slice_in_dim(full_mean, start, share, 1)
    outer = win_count[:, None, None] * own_mean[:, :, None] * full_mean[:, None, :]
    covariance = (win_gram - outer) / (win_count - 1.0)[:, None, None]
    return (covariance[None], own_mean[None])


def solution(mesh):
    placed = (P("day", "year", "region", None), P("region", "day", "year"))
    return jax.shard_map(
        shards,
        mesh=mesh,
        in_specs=placed,
        out_specs=(P("region", "day", "year", None), P("region", "day", "year")),
        check_vma=False,
    )
```

profile of v0, /device:TPU:1, one launch (start us, length us, event | category | flops | bytes accessed | tf_op | source)
XLA Modules:
  0.0 215.9 jit_solution(6066490630283557537)
XLA Ops:
  7.2 0.0 reduce-scatter.2.cloned.1.call-start
  7.2 0.8 copy.5
  8.0 0.2 iota_compare_fusion
  8.2 0.0 copy-start
  8.2 16.5 %broadcast_select_fusion.6 = bf16[23,2,1000,256]{3,2,1,0:T(8,128)(2,1)} fusion(bf16[23,2,1000,256]{3,2,1,0:T(8,128)(2,1)} %param.6, pred[23,2,1000]{2,1,0:T(4,128)(4,1)S(1)} %iota_compare_fusion), kind=kLoop, calls=%fused_computation.1.clone.1.clone.2 | loop fusion | flops 11776000 | bytes 47150000 | tf_op jit(solution)/shard_map/dgsf,dgsh->dfh/dot_general | solution.py:39
  24.6 6.6 %copy-done = bf16[23,2,1000,256]{3,2,1,0:T(8,128)(2,1)S(1)} copy-done((bf16[23,2,1000,256]{3,2,1,0:T(8,128)(2,1)S(1)}, bf16[23,2,1000,256]{3,2,1,0:T(8,128)(2,1)}, u32[]{:S(2)}) %copy-start) | copy-done | bytes 23552024
  31.2 11.0 %convert_reduce_fusion = f32[23,256]{1,0:T(8,128)S(1)} fusion(bf16[23,2,1000,256]{3,2,1,0:T(8,128)(2,1)S(1)} %copy-done, pred[23,2,1000]{2,1,0:T(4,128)(4,1)S(1)} %iota_compare_fusion), kind=kLoop, calls=%fused_computation | loop fusion | flops 35322112 | bytes 23621552 | tf_op jit(solution)/shard_map/reduce_sum | solution.py:40
  42.2 0.0 copy-start.2
  42.2 19.4 %fusion = f32[23,256,256,1]{2,1,3,0:T(8,128)} fusion(bf16[23,2,1000,256]{3,2,1,0:T(8,128)(2,1)} %broadcast_select_fusion.6), kind=kOutput, calls=%fused_computation.2 | convolution fusion | flops 6029312000 | bytes 29581312 | tf_op jit(solution)/shard_map/dgsf,dgsh->dfh/dot_general | solution.py:39
  61.7 0.0 copy-done.2
  61.7 0.1 broadcast_in_dim.20
  61.8 0.1 scatter.9
  61.9 0.1 broadcast_in_dim.21
  62.0 6.3 %pad_maximum_fusion = f32[23,4,72,256]{3,2,1,0:T(8,128)} fusion(f32[23,4,8,256]{3,2,1,0:T(8,128)S(1)} %broadcast_in_dim.21, f32[23,4,64,256]{3,2,1,0:T(8,128)} %bitcast.13), kind=kLoop, calls=%fused_computation.4 | loop fusion | flops 1695744 | bytes 13565952 | tf_op jit(solution)/shard_map/concatenate | solution.py:47
  68.3 0.0 reduce-scatter.2.cloned.1.call-update
  68.3 121.0 %reduce-scatter.2.cloned.1.call-done = f32[23,72,256]{2,1,0:T(8,128)} async-done(((f32[23,288,256]{2,1,0:T(8,128)}), f32[23,72,256]{2,1,0:T(8,128)}) %reduce-scatter.2.cloned.1.call-update) | async-done | bytes 1695760 | tf_op jit(solution)/shard_map/reduce_scatter | solution.py:50
  189.4 0.0 copy-start.1
  189.4 1.4 fusion.7
  190.8 1.7 collective-permute-start
  192.5 0.0 collective-permute-start.1
  192.5 10.7 %collective-permute-done = f32[7,72,256]{2,1,0:T(8,128)} collective-permute-done((f32[7,72,256]{2,1,0:T(8,128)S(1)}, f32[7,72,256]{2,1,0:T(8,128)}, u32[]{:S(2)}, u32[]{:S(2)}) %collective-permute-start) | collective-permute-done | bytes 516128 | tf_op jit(solution)/shard_map/ppermute | solution.py:16
  203.2 1.1 constant_dynamic-update-slice_fusion.1
  204.3 0.0 copy-done.1
  204.3 0.2 constant_dynamic-update-slice_fusion
  204.5 0.3 collective-permute-done.1
  204.8 1.7 slice_add_fusion
  206.6 0.3 slice_reduce_fusion
  206.8 0.1 fusion.6
  206.9 0.1 broadcast_multiply_fusion
  207.0 0.6 broadcast_in_dim.39
  207.6 1.5 fusion.4
  (6 shorter events, 0.1 us)
Async XLA Ops:
  7.2 182.2 %reduce-scatter.2.cloned.1.call-start = ((), (), s32[]{:S(2)}) async-start(), calls=%async_computation.1 | async-start | bytes 8478720 | tf_op jit(solution)/shard_map/reduce_scatter | solution.py:50
  8.2 23.1 %copy-start = (bf16[23,2,1000,256]{3,2,1,0:T(8,128)(2,1)S(1)}, bf16[23,2,1000,256]{3,2,1,0:T(8,128)(2,1)}, u32[]{:S(2)}) copy-start(bf16[23,2,1000,256]{3,2,1,0:T(8,128)(2,1)} %param.6) | copy-start | bytes 70656000
  42.2 19.5 %copy-start.2 = (s32[1,23,2]{1,2,0:T(2,128)S(1)}, s32[1,23,2]{1,2,0:T(2,128)}, u32[]{:S(2)}) copy-start(s32[1,23,2]{1,2,0:T(2,128)} %param.7) | copy-start | bytes 556
  189.4 14.9 %copy-start.1 = (f32[23,72,256]{2,1,0:T(8,128)S(1)}, f32[23,72,256]{2,1,0:T(8,128)}, u32[]{:S(2)}) copy-start(f32[23,72,256]{2,1,0:T(8,128)} %reduce-scatter.2.cloned.1.call-done) | copy-start | bytes 5087236
  190.8 12.4 %collective-permute-start = (f32[7,72,256]{2,1,0:T(8,128)S(1)}, f32[7,72,256]{2,1,0:T(8,128)}, u32[]{:S(2)}, u32[]{:S(2)}) collective-permute-start(f32[7,72,256]{2,1,0:T(8,128)S(1)} %get-tuple-element.34), channel_id=1, source_target_pairs={{0,8},{8,16},{16,24},{24,0},{1,9},{9,17},{17,25},{25,1},{2,10},{10... | collective-permute-start | bytes 1548296 | tf_op jit(solution)/shard_map/ppermute | solution.py:16
  192.5 12.3 %collective-permute-start.1 = (f32[7,72,256]{2,1,0:T(8,128)S(1)}, f32[7,72,256]{2,1,0:T(8,128)S(1)}, u32[]{:S(2)}, u32[]{:S(2)}) collective-permute-start(f32[7,72,256]{2,1,0:T(8,128)S(1)} %get-tuple-element.35), channel_id=1, source_target_pairs={{8,0},{16,8},{24,16},{0,24},{9,1},{17,9},{25,17},{1,25},{10,2},{18... | collective-permute-start | bytes 1548296 | tf_op jit(solution)/shard_map/ppermute | solution.py:18
Sparse Core Ops, SparseCore 0:
  68.5 120.8 reduce-scatter.1
where the time goes:
time: 216 us
  waiting for transfers between devices  132 us (61%)
  other arithmetic  37.6 us (17%)
  matrix products  19.4 us (9%)
  between operations  14.2 us (7%)
  local copies, waits for them, and re-layouts  11 us (5%)
    reduce_scatter x1, waiting for transfers between devices, shards(): summed = lax.psum_scatter(stacked, 'year', scatter_dimension=1, tiled=True)  121 us
    dot_general x1, matrix products, shards(): jnp.einsum('dgsf,dgsh->dfh', masked, masked, preferred_element_type=jnp.f...  19.4 us
    dot_general x1, other arithmetic, shards(): jnp.einsum('dgsf,dgsh->dfh', masked, masked, preferred_element_type=jnp.f...  16.5 us
    reduce_sum x1, other arithmetic, shards(): day_sum = jnp.sum(masked, axis=(1, 2), dtype=jnp.float32)  11 us
    ppermute x1, waiting for transfers between devices, extended(): lax.ppermute(tail, axis, [(i, (i + 1) % count) for i in range(count)])  10.7 us
    unnamed x8, local copies, waits for them, and re-layouts  7.67 us
    concatenate x1, other arithmetic, shards(): jnp.concatenate([blocks, extra_all], axis=2)  6.31 us
  transfers between devices with their start and end apart: 3, of which 3 were waited for; matrix products, arithmetic and copies ran while one was open for 1% of the time, Pallas kernels for 0%

commit v1 on v0

v1 whole, which is shorter than its diff:
```python
import functools

import jax
import jax.numpy as jnp
from jax import lax
from jax.experimental import pallas as pl
from jax.experimental.pallas import tpu as pltpu
from jax.sharding import PartitionSpec as P

HALF = 7
LANES = 128
BLOCK = 64
SUBLANES = 8
FULL, CROSS, OWN = 4 * BLOCK, 3 * BLOCK, 2 * BLOCK
SMALL = 3
TOKEN = (SUBLANES, LANES)
SCALARS = pl.BlockSpec(memory_space=pltpu.SMEM)
INSIDE = pl.BlockSpec(memory_space=pltpu.VMEM)
ANYWHERE = pl.BlockSpec(memory_space=pl.ANY)


def small_rows(days):
    return -(-(SMALL * days + 1) // SUBLANES) * SUBLANES


def length(runs):
    return sum(size for _, size in runs)


def call(kernel, args, specs, shapes, scratch, flops, moved, mebibytes=16, outs=None):
    results = pl.pallas_call(
        kernel,
        in_specs=list(specs),
        out_specs=(list(outs) if outs else [INSIDE] * len(shapes)) + [INSIDE],
        out_shape=[jax.ShapeDtypeStruct(shape, jnp.float32) for shape in list(shapes) + [TOKEN]],
        scratch_shapes=scratch,
        cost_estimate=pl.CostEstimate(flops=flops, bytes_accessed=moved, transcendentals=0),
        compiler_params=pltpu.CompilerParams(vmem_limit_bytes=mebibytes * 1024 * 1024),
    )(*args)
    return results[:-1], results[-1]


def iotas(shape):
    return lax.broadcasted_iota(jnp.int32, shape, 0), lax.broadcasted_iota(jnp.int32, shape, 1)


def swap(block):
    return pltpu.roll(block, BLOCK, 1)


def pack_quadrant(quadrant):
    top, bottom = quadrant[:BLOCK], swap(quadrant[BLOCK:])
    row, lane = iotas((BLOCK, LANES))
    packed = jnp.where((lane < BLOCK) & (row > lane), bottom, top)
    diagonal = jnp.sum(jnp.where(row == lane, bottom, 0.0), axis=0, keepdims=True)
    return packed, diagonal


def gram_kernel(parts, counts_ref, samples_ref, after_ref, *refs):
    outs, token_ref, held, arrived = refs[: len(parts)], *refs[len(parts) :]
    groups, slots, width = held.shape[1:]
    lane = lax.broadcasted_iota(jnp.int32, (1, LANES), 1)
    rank = lax.broadcasted_iota(jnp.int32, (2 * SUBLANES, slots), 1)
    token_ref[...] = jnp.zeros_like(token_ref)

    def copies(day, slot):
        return [
            pltpu.make_async_copy(samples_ref.at[day, g], held.at[slot, g], arrived.at[slot, g])
            for g in range(groups)
        ]

    slot = 0
    for runs in parts:
        for start, number in runs:
            for i in range(number):
                for copy in copies(start + i, slot + i):
                    copy.start()
            slot += number
    slot = 0
    for runs, out_ref in zip(parts, outs):
        days = length(runs)
        small = days * FULL
        out_ref[small:] = jnp.zeros((small_rows(days), LANES), jnp.float32)
        numbers = jnp.zeros((1, LANES), jnp.int32)
        at = 0
        for start, number in runs:

            def day(i, numbers, start=start, at=at, slot=slot, out_ref=out_ref, small=small):
                gram = jnp.zeros((width, width), jnp.float32)
                total = jnp.zeros((1, width), jnp.float32)
                for g, copy in enumerate(copies(start + i, slot + i)):
                    copy.wait()
                    count = counts_ref[0, g, start + i]
                    numbers += jnp.where(lane == at + i, count, 0)
                    block = held[slot + i, g]
                    left = jnp.concatenate([block.T, jnp.ones(rank.shape, block.dtype)], axis=0)
                    left = jnp.where(rank[:1] < count, left, jnp.zeros_like(left))
                    product = jnp.dot(left, block, preferred_element_type=jnp.float32)
                    gram += product[:width]
                    total += product[width : width + 1]
                base = pl.multiple_of((at + i) * FULL, FULL)
                low, diagonal_low = pack_quadrant(gram[:LANES, :LANES])
                high, diagonal_high = pack_quadrant(gram[LANES:, LANES:])
                out_ref[pl.ds(base, LANES)] = gram[:LANES, LANES:]
                out_ref[pl.ds(base + LANES, BLOCK)] = low
                out_ref[pl.ds(base + LANES + BLOCK, BLOCK)] = high
                row = small + SMALL * (at + i)
                out_ref[pl.ds(row, 1)] = diagonal_high + swap(diagonal_low)
                out_ref[pl.ds(row + 1, 1)] = total[:, :LANES]
                out_ref[pl.ds(row + 2, 1)] = total[:, LANES:]
                return numbers

            numbers = lax.fori_loop(0, number, day, numbers)
            at += number
            slot += number
        last = small + SMALL * days
        out_ref[last : last + 1] = numbers.astype(jnp.float32)


def gram(samples, counts, parts, after):
    _, groups, slots, width = samples.shape
    days = sum(length(runs) for runs in parts)
    rows = [length(runs) * FULL + small_rows(length(runs)) for runs in parts]
    outs, token = call(
        functools.partial(gram_kernel, parts),
        (counts, samples, after),
        (SCALARS, ANYWHERE, ANYWHERE),
        [(size, LANES) for size in rows],
        [
            pltpu.VMEM((days, groups, slots, width), samples.dtype),
            pltpu.SemaphoreType.DMA((days, groups)),
        ],
        2 * days * groups * slots * width * width,
        2 * days * groups * slots * width + 4 * sum(rows) * LANES,
        44,
    )
    return outs, token


def inner_kernel(days, year_ref, mine_ref, came_ref, after_ref, send_ref, keep_ref, token_ref):
    low_half = year_ref[0] < 2
    token_ref[...] = jnp.zeros_like(token_ref)

    def day(i, carry):
        src = pl.multiple_of(i * FULL, FULL)
        dst = pl.multiple_of(i * CROSS, CROSS)
        own = pl.multiple_of(i * BLOCK, BLOCK)
        q = pl.ds(src, LANES)
        send_ref[pl.ds(dst, LANES)] = mine_ref[q] + came_ref[q]
        low = pl.ds(src + LANES, BLOCK)
        high = pl.ds(src + LANES + BLOCK, BLOCK)
        low_sum = mine_ref[low] + came_ref[low]
        high_sum = mine_ref[high] + came_ref[high]
        send_ref[pl.ds(dst + LANES, BLOCK)] = jnp.where(low_half, high_sum, low_sum)
        keep_ref[pl.ds(own, BLOCK)] = jnp.where(low_half, low_sum, high_sum)
        return carry

    lax.fori_loop(0, days, day, 0)
    send_ref[days * CROSS :] = mine_ref[days * FULL :] + came_ref[days * FULL :]


def inner(year, mine, came, days, after):
    rows = days * CROSS + small_rows(days)
    (send, keep), token = call(
        functools.partial(inner_kernel, days),
        (year, mine, came, after),
        (SCALARS, INSIDE, INSIDE, ANYWHERE),
        [(rows, LANES), (days * BLOCK, LANES)],
        [],
        days * FULL * LANES,
        3 * 4 * days * FULL * LANES,
    )
    return send, keep, token


def cross_kernel(days, year_ref, mine_ref, keep_ref, came_ref, after_ref, send_ref, own_ref, token_ref):
    low_half = year_ref[0] < 2
    token_ref[...] = jnp.zeros_like(token_ref)
    _, lane = iotas((BLOCK, LANES))

    def day(i, carry):
        src = pl.multiple_of(i * CROSS, CROSS)
        own = pl.multiple_of(i * BLOCK, BLOCK)
        dst = pl.multiple_of(i * OWN, OWN)
        top = mine_ref[pl.ds(src, BLOCK)] + came_ref[pl.ds(src, BLOCK)]
        bottom = mine_ref[pl.ds(src + BLOCK, BLOCK)] + came_ref[pl.ds(src + BLOCK, BLOCK)]
        packed = keep_ref[pl.ds(own, BLOCK)] + came_ref[pl.ds(src + LANES, BLOCK)]
        first = jnp.where(lane < BLOCK, top, swap(bottom))
        second = jnp.where(lane < BLOCK, swap(top), bottom)
        send_ref[pl.ds(dst, BLOCK)] = packed
        own_ref[pl.ds(dst, BLOCK)] = packed
        send_ref[pl.ds(dst + BLOCK, BLOCK)] = jnp.where(low_half, top, second)
        own_ref[pl.ds(dst + BLOCK, BLOCK)] = jnp.where(low_half, bottom, first)
        return carry

    lax.fori_loop(0, days, day, 0)
    small = mine_ref[days * CROSS :] + came_ref[days * CROSS :]
    send_ref[days * OWN :] = small
    own_ref[days * OWN :] = small


def cross(year, mine, keep, came, days, after):
    rows = days * OWN + small_rows(days)
    (send, own), token = call(
        functools.partial(cross_kernel, days),
        (year, mine, keep, came, after),
        (SCALARS, INSIDE, INSIDE, INSIDE, ANYWHERE),
        [(rows, LANES)] * 2,
        [],
        days * CROSS * LANES,
        3 * 4 * days * CROSS * LANES,
    )
    return send, own, token


def is_outer(year):
    return (year == 0) | (year == 3)


def pick_kernel(runs, year_ref, own_ref, came_ref, after_ref, *refs):
    outs, token_ref = refs[:-1], refs[-1]
    outer = is_outer(year_ref[0])
    token_ref[...] = jnp.zeros_like(token_ref)

    def pick(start, size):
        return jnp.where(outer, came_ref[start : start + size], own_ref[start : start + size])

    small = length(runs) * OWN
    at = 0
    for (_, number), out_ref in zip(runs, outs):
        out_ref[: number * OWN] = pick(at * OWN, number * OWN)
        row = number * OWN
        out_ref[row : row + SMALL * number] = pick(small + SMALL * at, SMALL * number)
        counts = pick(small + SMALL * length(runs), 1)
        row += SMALL * number
        out_ref[row : row + 1] = pltpu.roll(counts, (LANES - at) % LANES, 1)
        at += number


def pick(year, own, came, runs, after):
    return call(
        functools.partial(pick_kernel, runs),
        (year, own, came, after),
        (SCALARS, INSIDE, INSIDE, ANYWHERE),
        [(size * OWN + small_rows(size), LANES) for _, size in runs],
        [],
        0,
        2 * 4 * own.size,
    )


def unpack(year, rows, diagonal):
    odd = lax.rem(year, 2) == 1
    low_half = year < 2
    row, lane = iotas((BLOCK, LANES))
    turned = rows.T
    top, bottom = rows[:BLOCK], rows[BLOCK:]
    top_turned, bottom_turned = turned[:BLOCK], turned[BLOCK:]
    upper = jnp.where(lane < BLOCK, jnp.where(row <= lane, top, top_turned), top)
    lower = swap(jnp.where(row > lane, top, top_turned))
    diagonal = jnp.where(low_half, diagonal, swap(diagonal))
    lower = jnp.where(row == lane - BLOCK, diagonal, lower)
    lower = jnp.where(lane < BLOCK, bottom_turned, lower)
    packed = jnp.where(odd, lower, upper)
    across = jnp.where(lane < BLOCK, swap(top_turned), bottom_turned)
    return jnp.where(low_half, packed, across), jnp.where(low_half, bottom, packed)


def windows_kernel(places, days, year_ref, *refs):
    parts = refs[: len(places)]
    win_ref, small_ref, token_ref, packed_ref = refs[len(places) + 1 :]
    token_ref[...] = jnp.zeros_like(token_ref)
    year = year_ref[0]
    extended = days + 2 * HALF
    where = {}
    for (place, number), ref in zip(places, parts):
        for i in range(number):
            where[place + i] = (ref, i, number * OWN)

    def sums(load, store):
        def add(a, b):
            return b if a is None else a if b is None else a + b

        def level(table, hop):
            return [add(table[k], table[k + hop]) for k in range(len(table) - hop)]

        ones = [load(*where[k]) if k in where else None for k in range(extended)]
        twos = level(ones, 1)
        fours = level(twos, 2)
        eights = level(fours, 4)
        for d in range(days):
            store(d, add(add(eights[d], fours[d + 8]), add(twos[d + 12], ones[d + 14])))

    def strip(s, carry):
        at = pl.multiple_of(s * SUBLANES, SUBLANES)

        def store(d, value):
            packed_ref[d, pl.ds(at, SUBLANES)] = value

        sums(lambda ref, i, small: ref[pl.ds(i * OWN + at, SUBLANES)], store)
        return carry

    lax.fori_loop(0, OWN // SUBLANES, strip, 0)

    for row in range(SMALL):

        def store_row(d, value):
            small_ref[row, d : d + 1] = value

        sums(lambda ref, i, small: ref[small + SMALL * i + row : small + SMALL * i + row + 1], store_row)

    lane = lax.broadcasted_iota(jnp.int32, (1, LANES), 1)

    def load_count(ref, i, small):
        last = small + SMALL * (small // OWN)
        count = jnp.sum(jnp.where(lane == i, ref[last : last + 1], 0.0), axis=1, keepdims=True)
        return jnp.broadcast_to(count, (1, LANES))

    def store_count(d, value):
        small_ref[SMALL, d : d + 1] = value

    sums(load_count, store_count)

    def day(d, carry):
        left, right = unpack(year, packed_ref[d], small_ref[0, pl.ds(d, 1)])
        win_ref[d, :, :LANES] = left
        win_ref[d, :, LANES:] = right
        return carry

    lax.fori_loop(0, days, day, 0)


def windows(year, parts, places, days, after):
    (win, small), token = call(
        functools.partial(windows_kernel, places, days),
        (year, *parts, after),
        [SCALARS] + [INSIDE] * len(parts) + [ANYWHERE],
        [(days, BLOCK, 2 * LANES), (SMALL + 1, days, LANES)],
        [pltpu.VMEM((days, OWN, LANES), jnp.float32)],
        6 * days * BLOCK * 2 * LANES,
        8 * days * BLOCK * 2 * LANES,
    )
    return win, small, token


def finish_kernel(places, pieces, year_ref, win_ref, small_ref, *refs):
    pairs, (after_ref, cov_ref, mean_ref, token_ref, formed, sent) = refs[: 2 * len(places)], refs[2 * len(places) :]
    token_ref[...] = jnp.zeros_like(token_ref)
    year = year_ref[0]
    outer = is_outer(year)
    days = win_ref.shape[0]
    lane = lax.broadcasted_iota(jnp.int32, (1, LANES), 1)
    day_of = lax.broadcasted_iota(jnp.int32, (days, LANES), 0)
    low, high, count = small_ref[1], small_ref[2], small_ref[SMALL]
    extras = []
    for p, (place, number) in enumerate(places):
        own_ref, came_ref = pairs[2 * p : 2 * p + 2]

        def pick(start, size):
            return jnp.where(outer, came_ref[start : start + size], own_ref[start : start + size])

        small = number * OWN
        numbers = pick(small + SMALL * number, 1)
        for i in range(number):
            inside = jnp.abs(day_of - (place + i)) <= HALF
            low += jnp.where(inside, pick(small + SMALL * i + 1, 1), 0.0)
            high += jnp.where(inside, pick(small + SMALL * i + 2, 1), 0.0)
            extra = jnp.sum(jnp.where(lane == i, numbers, 0.0), axis=1, keepdims=True)
            count += jnp.where(inside, extra, 0.0)
            extras.append((place + i, unpack(year, pick(i * OWN, OWN), pick(small + SMALL * i, 1))))
    low = low / count
    high = high / count
    own = jnp.where(year < 2, low, high)
    own = jnp.where(lax.rem(year, 2) == 1, swap(own), own)
    mean_ref[:, 0] = own[:, :BLOCK]
    turned = jnp.concatenate([own, jnp.zeros((LANES - days, LANES), jnp.float32)], axis=0).T
    scale = 1.0 / (count - 1.0)
    low = low * (count * scale)
    high = high * (count * scale)
    copies = []
    for first, size in pieces:
        for d in range(first, first + size):
            left, right = win_ref[d, :, :LANES], win_ref[d, :, LANES:]
            for at, (more_left, more_right) in extras:
                if abs(d - at) <= HALF:
                    left, right = left + more_left, right + more_right
            column = turned[:BLOCK, d : d + 1]
            factor = scale[d : d + 1]
            formed[d, :, :LANES] = left * factor - column * low[d : d + 1]
            formed[d, :, LANES:] = right * factor - column * high[d : d + 1]
        piece = pl.ds(first, size)
        copy = pltpu.make_async_copy(formed.at[piece], cov_ref.at[0, piece], sent.at[len(copies)])
        copy.start()
        copies.append(copy)
    for copy in copies:
        copy.wait()


def finish(year, win, small, pairs, places, after):
    days, _, width = win.shape
    size = -(-days // 3)
    pieces = tuple((first, min(size, days - first)) for first in range(0, days, size))
    flat = [array for pair in pairs for array in pair]
    (covariance, mean), _ = call(
        functools.partial(finish_kernel, places, pieces),
        (year, win, small, *flat, after),
        [SCALARS] + [INSIDE] * (2 + len(flat)) + [ANYWHERE],
        [(1, days, BLOCK, width), (days, 1, BLOCK)],
        [pltpu.VMEM((days, BLOCK, width), jnp.float32), pltpu.SemaphoreType.DMA((len(pieces),))],
        6 * days * BLOCK * width,
        8 * days * BLOCK * width,
        outs=[ANYWHERE, INSIDE],
    )
    return covariance, mean


def plan(days):
    near = min(5, HALF)
    rest = HALF - near
    parts = [((0, near),), ((days - near, near),), ((near, rest), (days - HALF, rest))]
    at, left = HALF, days - 2 * HALF
    for size in (left - 5, 3, 2):
        parts.append(((at, size),))
        at += size
    return parts


def shards(samples, counts):
    days = samples.shape[0]
    day_size = lax.axis_size("day")
    position = lax.axis_index("year")
    year = position.astype(jnp.int32)[None]
    inward = [(0, 1), (3, 2)]
    between = [(1, 2), (2, 1)]
    outward = [(1, 0), (2, 3)]
    right = [(i, (i + 1) % day_size) for i in range(day_size)]
    left = [((i + 1) % day_size, i) for i in range(day_size)]
    counts = jnp.transpose(counts, (0, 2, 1))
    parts = plan(days)
    token = jnp.zeros(TOKEN, jnp.float32)
    mine, sums, rows = {}, {}, {}
    totals, places = [], []

    def gram_step(*ks):
        nonlocal token
        outs, token = gram(samples, counts, tuple(parts[k] for k in ks), token)
        for k, out in zip(ks, outs):
            mine[k] = (out, lax.ppermute(out, "year", inward))

    def inner_step(k):
        nonlocal token
        send, keep, token = inner(year, *mine[k], length(parts[k]), token)
        sums[k] = (send, keep, lax.ppermute(send, "year", between))

    def cross_step(k):
        nonlocal token
        send, own, token = cross(year, *sums[k], length(parts[k]), token)
        rows[k] = (own, lax.ppermute(send, "year", outward))

    def pick_step(k):
        nonlocal token
        outs, token = pick(year, *rows[k], parts[k], token)
        for (start, size), out in zip(parts[k], outs):
            totals.append(out)
            places.append((start + HALF, size))
            if start < HALF:
                totals.append(lax.ppermute(out, "day", left))
                places.append((start + HALF + days, size))
            elif start >= days - HALF:
                totals.append(lax.ppermute(out, "day", right))
                places.append((start + HALF - days, size))

    gram_step(0)
    gram_step(1, 2)
    inner_step(0)
    gram_step(3, 4, 5)
    inner_step(1)
    cross_step(0)
    inner_step(2)
    pick_step(0)
    cross_step(1)
    inner_step(3)
    pick_step(1)
    cross_step(2)
    inner_step(4)
    pick_step(2)
    cross_step(3)
    inner_step(5)
    cross_step(4)
    pick_step(3)
    win, small, token = windows(year, totals, tuple(places), days, token)
    cross_step(5)
    last = tuple((parts[k][0][0], parts[k][0][1]) for k in (4, 5))
    covariance, mean = finish(year, win, small, (rows[4], rows[5]), last, token)
    return covariance, jnp.transpose(mean, (1, 0, 2))


def solution(mesh):
    placed = (P("day", "year", "region", None), P("region", "day", "year"))
    return jax.shard_map(
        shards,
        mesh=mesh,
        in_specs=placed,
        out_specs=(P("region", "day", "year", None), P("region", "day", "year")),
        check_vma=False,
    )
```

time: 216 us -> 106 us (0.49)
  waiting for transfers between devices: 132 us -> 15.9 us
  starting transfers between devices: 1.77 us -> 48.7 us
  Pallas kernels: 0 us -> 38.3 us
  other arithmetic: 37.6 us -> 0 us
  matrix products: 19.4 us -> 0 us
  between operations: 14.2 us -> 0.98 us
  local copies, waits for them, and re-layouts: 11 us -> 0.68 us
    reduce_scatter x1 -> x0, waiting for transfers between devices: 121 us -> none  [shards(): summed = lax.psum_scatter(stacked, 'year', scatter_dimension=1, tiled=True)]
    ppermute x2 -> x22, starting transfers between devices: 1.73 us -> 48.7 us  [the longest x6 27.3 us: gram_step(): mine[k] = (out, lax.ppermute(out, 'year', inward))]
    pallas_call x0 -> x21, Pallas kernels: none -> 38.3 us  [call(): pl.pallas_call(kernel, in_specs=list(specs), out_specs=(list(outs) if out...]
    dot_general x1 -> x0, matrix products: 19.4 us -> none  [shards(): jnp.einsum('dgsf,dgsh->dfh', masked, masked, preferred_element_type=jnp.f...]
    dot_general x1 -> x0, other arithmetic: 16.5 us -> none  [shards(): jnp.einsum('dgsf,dgsh->dfh', masked, masked, preferred_element_type=jnp.f...]
    reduce_sum x2 -> x0, other arithmetic: 11 us -> none  [the longest x1 11 us: shards(): day_sum = jnp.sum(masked, axis=(1, 2), dtype=jnp.float32)]
    unnamed x8 -> x4, local copies, waits for them, and re-layouts: 7.67 us -> 0.68 us
    concatenate x1 -> x0, other arithmetic: 6.31 us -> none  [shards(): jnp.concatenate([blocks, extra_all], axis=2)]
  transfers between devices with their start and end apart: 3 -> 22, of which waited for: 3 -> 10; matrix products, arithmetic and copies ran while one was open for 1% -> 0% of each run, Pallas kernels for 0% -> 28%
where the time goes in v1:
time: 106 us; the launch traced here: 104 us
  starting transfers between devices  48.7 us (46%)
  Pallas kernels  38.3 us (36%)
  waiting for transfers between devices  15.9 us (15%)
    pallas_call x21, Pallas kernels, call(): pl.pallas_call(kernel, in_specs=list(specs), out_specs=(list(outs) if out...  38.3 us
    ppermute x6, starting transfers between devices, gram_step(): mine[k] = (out, lax.ppermute(out, 'year', inward))  27.3 us
    ppermute x6, waiting for transfers between devices, cross_step(): rows[k] = (own, lax.ppermute(send, 'year', outward))  11 us
    ppermute x6, starting transfers between devices, cross_step(): rows[k] = (own, lax.ppermute(send, 'year', outward))  7.74 us
    ppermute x2, starting transfers between devices, pick_step(): totals.append(lax.ppermute(out, 'day', left))  5.23 us
    ppermute x2, starting transfers between devices, pick_step(): totals.append(lax.ppermute(out, 'day', right))  4.23 us
    ppermute x6, starting transfers between devices, inner_step(): sums[k] = (send, keep, lax.ppermute(send, 'year', between))  4.11 us
    ppermute x2, waiting for transfers between devices, pick_step(): totals.append(lax.ppermute(out, 'day', left))  2.42 us
  transfers between devices with their start and end apart: 22, of which 10 were waited for; matrix products, arithmetic and copies ran while one was open for 0% of the time, Pallas kernels for 28%

profile of v1, /device:TPU:1, one launch (start us, length us, event | category | flops | bytes accessed | tf_op | source)
XLA Modules:
  0.0 104.5 jit_solution(13383058286794295339)
XLA Ops:
  0.6 0.0 copy-start
  0.7 0.7 copy-done
  1.3 6.8 %shard_map.41 = (f32[1296,128]{1,0:T(8,128)S(1)}, f32[8,128]{1,0:T(8,128)S(1)}) custom-call(s32[1,2,23]{2,1,0:T(2,128)S(1)} %bitcast.3, bf16[23,2,1000,256]{3,2,1,0:T(8,128)(2,1)} %samples_ref.5, f32[8,128]{1,0:T(8,128)S(1)} %broadcast_in_dim.7.after_ref), custom_call_target="tpu_custom_call" | custom-call | flops 1310720000 | bytes 5783552 | tf_op jit(solution)/shard_map/pallas_call | solution.py:31
  8.1 4.1 %collective-permute-start = (f32[1296,128]{1,0:T(8,128)S(1)}, f32[1296,128]{1,0:T(8,128)S(1)}, u32[]{:S(2)}, u32[]{:S(2)}) collective-permute-start(f32[1296,128]{1,0:T(8,128)S(1)} %get-tuple-element.61.mine_ref), channel_id=1, source_target_pairs={{0,2},{6,4},{1,3},{7,5},{8,10},{14,12},{9,11},{15,13},{16,18},{22,... | collective-permute-start | bytes 1990664 | tf_op jit(solution)/shard_map/ppermute | solution.py:448
  12.2 0.0 copy-start.1
  12.2 11.0 %shard_map.42 = (f32[1296,128]{1,0:T(8,128)S(1)}, f32[1040,128]{1,0:T(8,128)S(1)}, f32[8,128]{1,0:T(8,128)S(1)}) custom-call(s32[1,2,23]{2,1,0:T(2,128)S(1)} %bitcast.4, bf16[23,2,1000,256]{3,2,1,0:T(8,128)(2,1)} %samples_ref.5, f32[8,128]{1,0:T(8,128)S(1)} %get-tuple-element.62.after_ref), custom_call_target="tpu_custom_call" | custom-call | flops 2359296000 | bytes 10412032 | tf_op jit(solution)/shard_map/pallas_call | solution.py:31
  23.2 1.3 %collective-permute-start.2 = (f32[1296,128]{1,0:T(8,128)S(1)}, f32[1296,128]{1,0:T(8,128)S(1)}, u32[]{:S(2)}, u32[]{:S(2)}) collective-permute-start(f32[1296,128]{1,0:T(8,128)S(1)} %get-tuple-element.66.mine_ref), channel_id=1, source_target_pairs={{0,2},{6,4},{1,3},{7,5},{8,10},{14,12},{9,11},{15,13},{16,18},{22,... | collective-permute-start | bytes 1990664 | tf_op jit(solution)/shard_map/ppermute | solution.py:448
  24.5 1.2 %collective-permute-done.came_ref = f32[1296,128]{1,0:T(8,128)S(1)} collective-permute-done((f32[1296,128]{1,0:T(8,128)S(1)}, f32[1296,128]{1,0:T(8,128)S(1)}, u32[]{:S(2)}, u32[]{:S(2)}) %collective-permute-start) | collective-permute-done | bytes 663584 | tf_op jit(solution)/shard_map/ppermute | solution.py:448
  25.7 0.1 shard_map.43
  25.8 0.7 collective-permute-start.1
  26.5 6.7 %collective-permute-start.4 = (f32[1040,128]{1,0:T(8,128)S(1)}, f32[1040,128]{1,0:T(8,128)S(1)}, u32[]{:S(2)}, u32[]{:S(2)}) collective-permute-start(f32[1040,128]{1,0:T(8,128)S(1)} %get-tuple-element.72.mine_ref), channel_id=1, source_target_pairs={{0,2},{6,4},{1,3},{7,5},{8,10},{14,12},{9,11},{15,13},{16,18},{22,... | collective-permute-start | bytes 1597448 | tf_op jit(solution)/shard_map/ppermute | solution.py:448
  33.2 11.0 %shard_map.44 = (f32[1040,128]{1,0:T(8,128)S(1)}, f32[784,128]{1,0:T(8,128)S(1)}, f32[520,128]{1,0:T(8,128)S(1)}, f32[8,128]{1,0:T(8,128)S(1)}) custom-call(s32[1,2,23]{2,1,0:T(2,128)S(1)} %bitcast.5, bf16[23,2,1000,256]{3,2,1,0:T(8,128)(2,1)} %samples_ref.5, f32[8,128]{1,0:T(8,128)S(1)} %get-tuple-element.67.after_ref), custom_call_target="tpu_custom_call" | custom-call | flops 2359296000 | bytes 10416128 | tf_op jit(solution)/shard_map/pallas_call | solution.py:31
  44.1 0.0 collective-permute-done.2.came_ref
  44.1 0.1 shard_map.45
  44.2 0.7 collective-permute-start.6
  44.9 0.0 collective-permute-done.1.came_ref
  45.0 0.5 shard_map.46
  45.4 1.3 %collective-permute-start.3 = (f32[656,128]{1,0:T(8,128)S(1)}, f32[656,128]{1,0:T(8,128)S(1)}, u32[]{:S(2)}, u32[]{:S(2)}) collective-permute-start(f32[656,128]{1,0:T(8,128)S(1)} %get-tuple-element.71), channel_id=1, source_target_pairs={{2,0},{4,6},{3,1},{5,7},{10,8},{12,14},{11,9},{13,15},{18,16},{20,... | collective-permute-start | bytes 1007624 | tf_op jit(solution)/shard_map/ppermute | solution.py:458
  46.7 4.0 %collective-permute-start.8 = (f32[1040,128]{1,0:T(8,128)S(1)}, f32[1040,128]{1,0:T(8,128)S(1)}, u32[]{:S(2)}, u32[]{:S(2)}) collective-permute-start(f32[1040,128]{1,0:T(8,128)S(1)} %get-tuple-element.81.mine_ref), channel_id=1, source_target_pairs={{0,2},{6,4},{1,3},{7,5},{8,10},{14,12},{9,11},{15,13},{16,18},{22,... | collective-permute-start | bytes 1597448 | tf_op jit(solution)/shard_map/ppermute | solution.py:448
  50.8 0.6 collective-permute-done.4.came_ref
  51.3 0.1 shard_map.47
  51.4 0.7 collective-permute-start.10
  52.1 1.2 %collective-permute-done.3.came_ref = f32[656,128]{1,0:T(8,128)S(1)} collective-permute-done((f32[656,128]{1,0:T(8,128)S(1)}, f32[656,128]{1,0:T(8,128)S(1)}, u32[]{:S(2)}, u32[]{:S(2)}) %collective-permute-start.3) | collective-permute-done | bytes 335904 | tf_op jit(solution)/shard_map/ppermute | solution.py:458
  53.4 0.0 collective-permute-done.6.came_ref
  53.4 0.5 shard_map.49
  53.9 1.3 %collective-permute-start.7 = (f32[656,128]{1,0:T(8,128)S(1)}, f32[656,128]{1,0:T(8,128)S(1)}, u32[]{:S(2)}, u32[]{:S(2)}) collective-permute-start(f32[656,128]{1,0:T(8,128)S(1)} %get-tuple-element.80), channel_id=1, source_target_pairs={{2,0},{4,6},{3,1},{5,7},{10,8},{12,14},{11,9},{13,15},{18,16},{20,... | collective-permute-start | bytes 1007624 | tf_op jit(solution)/shard_map/ppermute | solution.py:458
  55.2 5.5 %collective-permute-start.12 = (f32[784,128]{1,0:T(8,128)S(1)}, f32[784,128]{1,0:T(8,128)S(1)}, u32[]{:S(2)}, u32[]{:S(2)}) collective-permute-start(f32[784,128]{1,0:T(8,128)S(1)} %get-tuple-element.90.mine_ref), channel_id=1, source_target_pairs={{0,2},{6,4},{1,3},{7,5},{8,10},{14,12},{9,11},{15,13},{16,18},{22,... | collective-permute-start | bytes 1204232 | tf_op jit(solution)/shard_map/ppermute | solution.py:448
  60.6 0.5 collective-permute-done.8.came_ref
  61.1 0.1 shard_map.50
  61.2 0.7 collective-permute-start.15
  61.9 1.7 %collective-permute-done.7.came_ref = f32[656,128]{1,0:T(8,128)S(1)} collective-permute-done((f32[656,128]{1,0:T(8,128)S(1)}, f32[656,128]{1,0:T(8,128)S(1)}, u32[]{:S(2)}, u32[]{:S(2)}) %collective-permute-start.7) | collective-permute-done | bytes 335904 | tf_op jit(solution)/shard_map/ppermute | solution.py:458
  63.6 0.0 collective-permute-done.10.came_ref
  63.6 0.4 shard_map.52
  64.0 1.3 %collective-permute-start.11 = (f32[528,128]{1,0:T(8,128)S(1)}, f32[528,128]{1,0:T(8,128)S(1)}, u32[]{:S(2)}, u32[]{:S(2)}) collective-permute-start(f32[528,128]{1,0:T(8,128)S(1)} %get-tuple-element.89), channel_id=1, source_target_pairs={{2,0},{4,6},{3,1},{5,7},{10,8},{12,14},{11,9},{13,15},{18,16},{20,... | collective-permute-start | bytes 811016 | tf_op jit(solution)/shard_map/ppermute | solution.py:458
  65.3 4.4 %collective-permute-start.5 = (f32[656,128]{1,0:T(8,128)S(1)}, f32[656,128]{1,0:T(8,128)S(1)}, u32[]{:S(2)}, u32[]{:S(2)}) collective-permute-start(f32[656,128]{1,0:T(8,128)S(1)} %get-tuple-element.75.refs_0_), channel_id=1, source_target_pairs={{8,0},{16,8},{24,16},{0,24},{9,1},{17,9},{25,17},{1,25},{10,2},{18... | collective-permute-start | bytes 1007624 | tf_op jit(solution)/shard_map/ppermute | solution.py:467
  69.7 5.8 %collective-permute-start.18 = (f32[520,128]{1,0:T(8,128)S(1)}, f32[520,128]{1,0:T(8,128)S(1)}, u32[]{:S(2)}, u32[]{:S(2)}) collective-permute-start(f32[520,128]{1,0:T(8,128)S(1)} %get-tuple-element.102.mine_ref), channel_id=1, source_target_pairs={{0,2},{6,4},{1,3},{7,5},{8,10},{14,12},{9,11},{15,13},{16,18},{22,... | collective-permute-start | bytes 798728 | tf_op jit(solution)/shard_map/ppermute | solution.py:448
  75.5 0.0 collective-permute-done.12.came_ref
  75.5 0.1 shard_map.53
  75.6 0.7 collective-permute-start.17
  76.2 0.0 collective-permute-done.11.came_ref
  76.3 0.1 shard_map.54
  76.3 0.0 collective-permute-done.15.came_ref
  76.3 0.4 shard_map.55
  76.7 1.3 %collective-permute-start.16 = (f32[528,128]{1,0:T(8,128)S(1)}, f32[528,128]{1,0:T(8,128)S(1)}, u32[]{:S(2)}, u32[]{:S(2)}) collective-permute-start(f32[528,128]{1,0:T(8,128)S(1)} %get-tuple-element.99), channel_id=1, source_target_pairs={{2,0},{4,6},{3,1},{5,7},{10,8},{12,14},{11,9},{13,15},{18,16},{20,... | collective-permute-start | bytes 811016 | tf_op jit(solution)/shard_map/ppermute | solution.py:458
  78.0 3.1 %collective-permute-start.9 = (f32[656,128]{1,0:T(8,128)S(1)}, f32[656,128]{1,0:T(8,128)S(1)}, u32[]{:S(2)}, u32[]{:S(2)}) collective-permute-start(f32[656,128]{1,0:T(8,128)S(1)} %get-tuple-element.84.refs_2_), channel_id=1, source_target_pairs={{0,8},{8,16},{16,24},{24,0},{1,9},{9,17},{17,25},{25,1},{2,10},{10... | collective-permute-start | bytes 1007624 | tf_op jit(solution)/shard_map/ppermute | solution.py:470
  81.1 0.2 collective-permute-done.18.came_ref
  81.3 0.7 collective-permute-start.20
  82.0 0.0 collective-permute-done.5.refs_1_
  82.0 0.9 collective-permute-start.13
  82.8 0.0 collective-permute-done.17.came_ref
  82.8 1.2 %collective-permute-start.14 = (f32[264,128]{1,0:T(8,128)S(1)}, f32[264,128]{1,0:T(8,128)S(1)}, u32[]{:S(2)}, u32[]{:S(2)}) collective-permute-start(f32[264,128]{1,0:T(8,128)S(1)} %get-tuple-element.94.refs_6_), channel_id=1, source_target_pairs={{0,8},{8,16},{16,24},{24,0},{1,9},{9,17},{17,25},{25,1},{2,10},{10... | collective-permute-start | bytes 405512 | tf_op jit(solution)/shard_map/ppermute | solution.py:470
  84.0 0.3 shard_map.57
  84.3 0.4 collective-permute-done.16.came_ref
  84.7 1.3 %collective-permute-start.19 = (f32[400,128]{1,0:T(8,128)S(1)}, f32[400,128]{1,0:T(8,128)S(1)}, u32[]{:S(2)}, u32[]{:S(2)}) collective-permute-start(f32[400,128]{1,0:T(8,128)S(1)} %get-tuple-element.111), channel_id=1, source_target_pairs={{2,0},{4,6},{3,1},{5,7},{10,8},{12,14},{11,9},{13,15},{18,16},{20,... | collective-permute-start | bytes 614408 | tf_op jit(solution)/shard_map/ppermute | solution.py:458
  86.0 0.0 collective-permute-done.9.refs_3_
  86.0 2.4 %collective-permute-done.13.refs_5_ = f32[264,128]{1,0:T(8,128)S(1)} collective-permute-done((f32[264,128]{1,0:T(8,128)S(1)}, f32[264,128]{1,0:T(8,128)S(1)}, u32[]{:S(2)}, u32[]{:S(2)}) %collective-permute-start.13) | collective-permute-done | bytes 135200 | tf_op jit(solution)/shard_map/ppermute | solution.py:467
  88.4 0.0 collective-permute-done.14.refs_7_
  88.4 4.4 %shard_map.59 = (f32[23,64,256]{2,1,0:T(8,128)S(1)}, f32[4,23,128]{2,1,0:T(8,128)S(1)}, f32[8,128]{1,0:T(8,128)S(1)}) custom-call(s32[1]{0:T(128)} %bitcast.year_ref, f32[656,128]{1,0:T(8,128)S(1)} %get-tuple-element.75.refs_0_, f32[656,128]{1,0:T(8,128)S(1)} %collective-permute-done.5.refs_1_, f32[656,128]{1,0:T(8,128)S(1)} %get-tuple-element.84.refs_2_, ...), custom_call_target="tpu_custom_call" | custom-call | flops 2260992 | bytes 3014656 | tf_op jit(solution)/shard_map/pallas_call | solution.py:31
  92.8 0.0 collective-permute-done.20.came_ref
  92.8 0.2 shard_map.60
  93.0 1.3 %collective-permute-start.21 = (f32[264,128]{1,0:T(8,128)S(1)}, f32[264,128]{1,0:T(8,128)S(1)}, u32[]{:S(2)}, u32[]{:S(2)}) collective-permute-start(f32[264,128]{1,0:T(8,128)S(1)} %get-tuple-element.116), channel_id=1, source_target_pairs={{2,0},{4,6},{3,1},{5,7},{10,8},{12,14},{11,9},{13,15},{18,16},{20,... | collective-permute-start | bytes 405512 | tf_op jit(solution)/shard_map/ppermute | solution.py:458
  94.3 1.2 %collective-permute-done.19.refs_1_ = f32[400,128]{1,0:T(8,128)S(1)} collective-permute-done((f32[400,128]{1,0:T(8,128)S(1)}, f32[400,128]{1,0:T(8,128)S(1)}, u32[]{:S(2)}, u32[]{:S(2)}) %collective-permute-start.19) | collective-permute-done | bytes 204832 | tf_op jit(solution)/shard_map/ppermute | solution.py:458
  95.5 6.5 %collective-permute-done.21.refs_3_ = f32[264,128]{1,0:T(8,128)S(1)} collective-permute-done((f32[264,128]{1,0:T(8,128)S(1)}, f32[264,128]{1,0:T(8,128)S(1)}, u32[]{:S(2)}, u32[]{:S(2)}) %collective-permute-start.21) | collective-permute-done | bytes 135200 | tf_op jit(solution)/shard_map/ppermute | solution.py:458
  102.0 2.4 %shard_map.61 = (f32[1,23,64,256]{3,2,1,0:T(8,128)}, f32[23,1,64]{2,1,0:T(1,128)}, f32[8,128]{1,0:T(8,128)}) custom-call(s32[1]{0:T(128)} %bitcast.year_ref, f32[23,64,256]{2,1,0:T(8,128)S(1)} %get-tuple-element.108.win_ref, f32[4,23,128]{2,1,0:T(8,128)S(1)} %get-tuple-element.109.small_ref, f32[400,128]{1,0:T(8,128)S(1)} %get-tuple-element.110.refs_0_, ...), custom_call_target="tpu_custom_call" | custom-call | flops 2260992 | bytes 3014656 | tf_op jit(solution)/shard_map/pallas_call | solution.py:31
  (6 shorter events, 0.2 us)
Async XLA Ops:
  0.6 0.7 copy-start
  8.1 17.6 %collective-permute-start = (f32[1296,128]{1,0:T(8,128)S(1)}, f32[1296,128]{1,0:T(8,128)S(1)}, u32[]{:S(2)}, u32[]{:S(2)}) collective-permute-start(f32[1296,128]{1,0:T(8,128)S(1)} %get-tuple-element.61.mine_ref), channel_id=1, source_target_pairs={{0,2},{6,4},{1,3},{7,5},{8,10},{14,12},{9,11},{15,13},{16,18},{22,... | collective-permute-start | bytes 1990664 | tf_op jit(solution)/shard_map/ppermute | solution.py:448
  12.2 21.0 %copy-start.1 = (s32[1,23,2]{1,2,0:T(2,128)S(1)}, s32[1,23,2]{1,2,0:T(2,128)}, u32[]{:S(2)}) copy-start(s32[1,23,2]{1,2,0:T(2,128)} %param.3) | copy-start | bytes 556
  23.2 21.0 %collective-permute-start.2 = (f32[1296,128]{1,0:T(8,128)S(1)}, f32[1296,128]{1,0:T(8,128)S(1)}, u32[]{:S(2)}, u32[]{:S(2)}) collective-permute-start(f32[1296,128]{1,0:T(8,128)S(1)} %get-tuple-element.66.mine_ref), channel_id=1, source_target_pairs={{0,2},{6,4},{1,3},{7,5},{8,10},{14,12},{9,11},{15,13},{16,18},{22,... | collective-permute-start | bytes 1990664 | tf_op jit(solution)/shard_map/ppermute | solution.py:448
  25.8 19.1 %collective-permute-start.1 = (f32[976,128]{1,0:T(8,128)S(1)}, f32[976,128]{1,0:T(8,128)S(1)}, u32[]{:S(2)}, u32[]{:S(2)}) collective-permute-start(f32[976,128]{1,0:T(8,128)S(1)} %get-tuple-element.64.mine_ref), channel_id=1, source_target_pairs={{2,4},{4,2},{3,5},{5,3},{10,12},{12,10},{11,13},{13,11},{18,20},{2... | collective-permute-start | bytes 1499144 | tf_op jit(solution)/shard_map/ppermute | solution.py:453
  26.5 24.8 %collective-permute-start.4 = (f32[1040,128]{1,0:T(8,128)S(1)}, f32[1040,128]{1,0:T(8,128)S(1)}, u32[]{:S(2)}, u32[]{:S(2)}) collective-permute-start(f32[1040,128]{1,0:T(8,128)S(1)} %get-tuple-element.72.mine_ref), channel_id=1, source_target_pairs={{0,2},{6,4},{1,3},{7,5},{8,10},{14,12},{9,11},{15,13},{16,18},{22,... | collective-permute-start | bytes 1597448 | tf_op jit(solution)/shard_map/ppermute | solution.py:448
  44.2 9.1 %collective-permute-start.6 = (f32[976,128]{1,0:T(8,128)S(1)}, f32[976,128]{1,0:T(8,128)S(1)}, u32[]{:S(2)}, u32[]{:S(2)}) collective-permute-start(f32[976,128]{1,0:T(8,128)S(1)} %get-tuple-element.76.mine_ref), channel_id=1, source_target_pairs={{2,4},{4,2},{3,5},{5,3},{10,12},{12,10},{11,13},{13,11},{18,20},{2... | collective-permute-start | bytes 1499144 | tf_op jit(solution)/shard_map/ppermute | solution.py:453
  45.4 7.9 %collective-permute-start.3 = (f32[656,128]{1,0:T(8,128)S(1)}, f32[656,128]{1,0:T(8,128)S(1)}, u32[]{:S(2)}, u32[]{:S(2)}) collective-permute-start(f32[656,128]{1,0:T(8,128)S(1)} %get-tuple-element.71), channel_id=1, source_target_pairs={{2,0},{4,6},{3,1},{5,7},{10,8},{12,14},{11,9},{13,15},{18,16},{20,... | collective-permute-start | bytes 1007624 | tf_op jit(solution)/shard_map/ppermute | solution.py:458
  46.7 14.4 %collective-permute-start.8 = (f32[1040,128]{1,0:T(8,128)S(1)}, f32[1040,128]{1,0:T(8,128)S(1)}, u32[]{:S(2)}, u32[]{:S(2)}) collective-permute-start(f32[1040,128]{1,0:T(8,128)S(1)} %get-tuple-element.81.mine_ref), channel_id=1, source_target_pairs={{0,2},{6,4},{1,3},{7,5},{8,10},{14,12},{9,11},{15,13},{16,18},{22,... | collective-permute-start | bytes 1597448 | tf_op jit(solution)/shard_map/ppermute | solution.py:448
  51.4 12.2 %collective-permute-start.10 = (f32[784,128]{1,0:T(8,128)S(1)}, f32[784,128]{1,0:T(8,128)S(1)}, u32[]{:S(2)}, u32[]{:S(2)}) collective-permute-start(f32[784,128]{1,0:T(8,128)S(1)} %get-tuple-element.85.mine_ref), channel_id=1, source_target_pairs={{2,4},{4,2},{3,5},{5,3},{10,12},{12,10},{11,13},{13,11},{18,20},{2... | collective-permute-start | bytes 1204232 | tf_op jit(solution)/shard_map/ppermute | solution.py:453
  53.9 9.7 %collective-permute-start.7 = (f32[656,128]{1,0:T(8,128)S(1)}, f32[656,128]{1,0:T(8,128)S(1)}, u32[]{:S(2)}, u32[]{:S(2)}) collective-permute-start(f32[656,128]{1,0:T(8,128)S(1)} %get-tuple-element.80), channel_id=1, source_target_pairs={{2,0},{4,6},{3,1},{5,7},{10,8},{12,14},{11,9},{13,15},{18,16},{20,... | collective-permute-start | bytes 1007624 | tf_op jit(solution)/shard_map/ppermute | solution.py:458
  55.2 20.3 %collective-permute-start.12 = (f32[784,128]{1,0:T(8,128)S(1)}, f32[784,128]{1,0:T(8,128)S(1)}, u32[]{:S(2)}, u32[]{:S(2)}) collective-permute-start(f32[784,128]{1,0:T(8,128)S(1)} %get-tuple-element.90.mine_ref), channel_id=1, source_target_pairs={{0,2},{6,4},{1,3},{7,5},{8,10},{14,12},{9,11},{15,13},{16,18},{22,... | collective-permute-start | bytes 1204232 | tf_op jit(solution)/shard_map/ppermute | solution.py:448
  61.2 15.2 %collective-permute-start.15 = (f32[784,128]{1,0:T(8,128)S(1)}, f32[784,128]{1,0:T(8,128)S(1)}, u32[]{:S(2)}, u32[]{:S(2)}) collective-permute-start(f32[784,128]{1,0:T(8,128)S(1)} %get-tuple-element.95.mine_ref), channel_id=1, source_target_pairs={{2,4},{4,2},{3,5},{5,3},{10,12},{12,10},{11,13},{13,11},{18,20},{2... | collective-permute-start | bytes 1204232 | tf_op jit(solution)/shard_map/ppermute | solution.py:453
  64.0 12.3 %collective-permute-start.11 = (f32[528,128]{1,0:T(8,128)S(1)}, f32[528,128]{1,0:T(8,128)S(1)}, u32[]{:S(2)}, u32[]{:S(2)}) collective-permute-start(f32[528,128]{1,0:T(8,128)S(1)} %get-tuple-element.89), channel_id=1, source_target_pairs={{2,0},{4,6},{3,1},{5,7},{10,8},{12,14},{11,9},{13,15},{18,16},{20,... | collective-permute-start | bytes 811016 | tf_op jit(solution)/shard_map/ppermute | solution.py:458
  65.3 16.7 %collective-permute-start.5 = (f32[656,128]{1,0:T(8,128)S(1)}, f32[656,128]{1,0:T(8,128)S(1)}, u32[]{:S(2)}, u32[]{:S(2)}) collective-permute-start(f32[656,128]{1,0:T(8,128)S(1)} %get-tuple-element.75.refs_0_), channel_id=1, source_target_pairs={{8,0},{16,8},{24,16},{0,24},{9,1},{17,9},{25,17},{1,25},{10,2},{18... | collective-permute-start | bytes 1007624 | tf_op jit(solution)/shard_map/ppermute | solution.py:467
  69.7 11.6 %collective-permute-start.18 = (f32[520,128]{1,0:T(8,128)S(1)}, f32[520,128]{1,0:T(8,128)S(1)}, u32[]{:S(2)}, u32[]{:S(2)}) collective-permute-start(f32[520,128]{1,0:T(8,128)S(1)} %get-tuple-element.102.mine_ref), channel_id=1, source_target_pairs={{0,2},{6,4},{1,3},{7,5},{8,10},{14,12},{9,11},{15,13},{16,18},{22,... | collective-permute-start | bytes 798728 | tf_op jit(solution)/shard_map/ppermute | solution.py:448
  75.6 7.3 %collective-permute-start.17 = (f32[592,128]{1,0:T(8,128)S(1)}, f32[592,128]{1,0:T(8,128)S(1)}, u32[]{:S(2)}, u32[]{:S(2)}) collective-permute-start(f32[592,128]{1,0:T(8,128)S(1)} %get-tuple-element.100.mine_ref), channel_id=1, source_target_pairs={{2,4},{4,2},{3,5},{5,3},{10,12},{12,10},{11,13},{13,11},{18,20},{2... | collective-permute-start | bytes 909320 | tf_op jit(solution)/shard_map/ppermute | solution.py:453
  76.7 7.9 %collective-permute-start.16 = (f32[528,128]{1,0:T(8,128)S(1)}, f32[528,128]{1,0:T(8,128)S(1)}, u32[]{:S(2)}, u32[]{:S(2)}) collective-permute-start(f32[528,128]{1,0:T(8,128)S(1)} %get-tuple-element.99), channel_id=1, source_target_pairs={{2,0},{4,6},{3,1},{5,7},{10,8},{12,14},{11,9},{13,15},{18,16},{20,... | collective-permute-start | bytes 811016 | tf_op jit(solution)/shard_map/ppermute | solution.py:458
  78.0 8.0 %collective-permute-start.9 = (f32[656,128]{1,0:T(8,128)S(1)}, f32[656,128]{1,0:T(8,128)S(1)}, u32[]{:S(2)}, u32[]{:S(2)}) collective-permute-start(f32[656,128]{1,0:T(8,128)S(1)} %get-tuple-element.84.refs_2_), channel_id=1, source_target_pairs={{0,8},{8,16},{16,24},{24,0},{1,9},{9,17},{17,25},{25,1},{2,10},{10... | collective-permute-start | bytes 1007624 | tf_op jit(solution)/shard_map/ppermute | solution.py:470
  81.3 11.6 %collective-permute-start.20 = (f32[392,128]{1,0:T(8,128)S(1)}, f32[392,128]{1,0:T(8,128)S(1)}, u32[]{:S(2)}, u32[]{:S(2)}) collective-permute-start(f32[392,128]{1,0:T(8,128)S(1)} %get-tuple-element.112.mine_ref), channel_id=1, source_target_pairs={{2,4},{4,2},{3,5},{5,3},{10,12},{12,10},{11,13},{13,11},{18,20},{2... | collective-permute-start | bytes 602120 | tf_op jit(solution)/shard_map/ppermute | solution.py:453
  82.0 6.5 %collective-permute-start.13 = (f32[264,128]{1,0:T(8,128)S(1)}, f32[264,128]{1,0:T(8,128)S(1)}, u32[]{:S(2)}, u32[]{:S(2)}) collective-permute-start(f32[264,128]{1,0:T(8,128)S(1)} %get-tuple-element.93.refs_4_), channel_id=1, source_target_pairs={{8,0},{16,8},{24,16},{0,24},{9,1},{17,9},{25,17},{1,25},{10,2},{18... | collective-permute-start | bytes 405512 | tf_op jit(solution)/shard_map/ppermute | solution.py:467
  82.8 5.6 %collective-permute-start.14 = (f32[264,128]{1,0:T(8,128)S(1)}, f32[264,128]{1,0:T(8,128)S(1)}, u32[]{:S(2)}, u32[]{:S(2)}) collective-permute-start(f32[264,128]{1,0:T(8,128)S(1)} %get-tuple-element.94.refs_6_), channel_id=1, source_target_pairs={{0,8},{8,16},{16,24},{24,0},{1,9},{9,17},{17,25},{25,1},{2,10},{10... | collective-permute-start | bytes 405512 | tf_op jit(solution)/shard_map/ppermute | solution.py:470
  84.7 10.8 %collective-permute-start.19 = (f32[400,128]{1,0:T(8,128)S(1)}, f32[400,128]{1,0:T(8,128)S(1)}, u32[]{:S(2)}, u32[]{:S(2)}) collective-permute-start(f32[400,128]{1,0:T(8,128)S(1)} %get-tuple-element.111), channel_id=1, source_target_pairs={{2,0},{4,6},{3,1},{5,7},{10,8},{12,14},{11,9},{13,15},{18,16},{20,... | collective-permute-start | bytes 614408 | tf_op jit(solution)/shard_map/ppermute | solution.py:458
  93.0 9.0 %collective-permute-start.21 = (f32[264,128]{1,0:T(8,128)S(1)}, f32[264,128]{1,0:T(8,128)S(1)}, u32[]{:S(2)}, u32[]{:S(2)}) collective-permute-start(f32[264,128]{1,0:T(8,128)S(1)} %get-tuple-element.116), channel_id=1, source_target_pairs={{2,0},{4,6},{3,1},{5,7},{10,8},{12,14},{11,9},{13,15},{18,16},{20,... | collective-permute-start | bytes 405512 | tf_op jit(solution)/shard_map/ppermute | solution.py:458

commit v2 on v1

--- a/solution.py
+++ b/solution.py
@@ -34,7 +34,7 @@
         out_specs=(list(outs) if outs else [INSIDE] * len(shapes)) + [INSIDE],
         out_shape=[jax.ShapeDtypeStruct(shape, jnp.float32) for shape in list(shapes) + [TOKEN]],
         scratch_shapes=scratch,
-        cost_estimate=pl.CostEstimate(flops=flops, bytes_accessed=moved, transcendentals=0),
+        cost_estimate=pl.CostEstimate(flops=0, bytes_accessed=0, transcendentals=0),
         compiler_params=pltpu.CompilerParams(vmem_limit_bytes=mebibytes * 1024 * 1024),
     )(*args)
     return results[:-1], results[-1]
@@ -60,7 +60,7 @@
     outs, token_ref, held, arrived = refs[: len(parts)], *refs[len(parts) :]
     groups, slots, width = held.shape[1:]
     lane = lax.broadcasted_iota(jnp.int32, (1, LANES), 1)
-    rank = lax.broadcasted_iota(jnp.int32, (2 * SUBLANES, slots), 1)
+    rank = lax.broadcasted_iota(jnp.int32, (1, slots), 1)
     token_ref[...] = jnp.zeros_like(token_ref)
 
     def copies(day, slot):
@@ -88,13 +88,14 @@
             def day(i, numbers, start=start, at=at, slot=slot, out_ref=out_ref, small=small):
                 gram = jnp.zeros((width, width), jnp.float32)
                 total = jnp.zeros((1, width), jnp.float32)
-                for g, copy in enumerate(copies(start + i, slot + i)):
+                for copy in copies(start + i, slot + i):
                     copy.wait()
+                for g in range(groups):
                     count = counts_ref[0, g, start + i]
                     numbers += jnp.where(lane == at + i, count, 0)
                     block = held[slot + i, g]
-                    left = jnp.concatenate([block.T, jnp.ones(rank.shape, block.dtype)], axis=0)
-                    left = jnp.where(rank[:1] < count, left, jnp.zeros_like(left))
+                    left = jnp.concatenate([block.T, jnp.ones((2 * SUBLANES, slots), block.dtype)], axis=0)
+                    left = jnp.where(rank < count, left, jnp.zeros_like(left))
                     product = jnp.dot(left, block, preferred_element_type=jnp.float32)
                     gram += product[:width]
                     total += product[width : width + 1]
@@ -327,7 +328,7 @@
         win_ref[d, :, LANES:] = right
         return carry
 
-    lax.fori_loop(0, days, day, 0)
+    lax.fori_loop(0, days, day, 0, unroll=True)
 
 
 def windows(year, parts, places, days, after):
@@ -415,14 +416,37 @@
 
 
 def plan(days):
-    near = min(5, HALF)
-    rest = HALF - near
-    parts = [((0, near),), ((days - near, near),), ((near, rest), (days - HALF, rest))]
+    parts = [((0, 4),), ((days - 5, 5),), ((4, HALF - 4), (days - HALF, HALF - 5))]
     at, left = HALF, days - 2 * HALF
     for size in (left - 5, 3, 2):
         parts.append(((at, size),))
         at += size
     return parts
+
+
+ORDER = (
+    ("gram", 0),
+    ("gram", 1),
+    ("gram", 2, 3, 4, 5),
+    ("inner", 0),
+    ("inner", 1),
+    ("cross", 0),
+    ("inner", 2),
+    ("pick", 0),
+    ("cross", 1),
+    ("inner", 3),
+    ("pick", 1),
+    ("cross", 2),
+    ("inner", 4),
+    ("cross", 3),
+    ("inner", 5),
+    ("pick", 2),
+    ("cross", 4),
+    ("pick", 3),
+    ("cross", 5),
+    ("windows",),
+    ("finish", 4, 5),
+)
 
 
 def shards(samples, counts):
@@ -470,28 +494,28 @@
                 totals.append(lax.ppermute(out, "day", right))
                 places.append((start + HALF - days, size))
 
-    gram_step(0)
-    gram_step(1, 2)
-    inner_step(0)
-    gram_step(3, 4, 5)
-    inner_step(1)
-    cross_step(0)
-    inner_step(2)
-    pick_step(0)
-    cross_step(1)
-    inner_step(3)
-    pick_step(1)
-    cross_step(2)
-    inner_step(4)
-    pick_step(2)
-    cross_step(3)
-    inner_step(5)
-    cross_step(4)
-    pick_step(3)
-    win, small, token = windows(year, totals, tuple(places), days, token)
-    cross_step(5)
-    last = tuple((parts[k][0][0], parts[k][0][1]) for k in (4, 5))
-    covariance, mean = finish(year, win, small, (rows[4], rows[5]), last, token)
+    def windows_step():
+        nonlocal token
+        win, small, token = windows(year, totals, tuple(places), days, token)
+        return win, small
+
+    def finish_step(*ks):
+        last = tuple(parts[k][0] for k in ks)
+        return finish(year, *held, [rows[k] for k in ks], last, token)
+
+    steps = {
+        "gram": gram_step,
+        "inner": inner_step,
+        "cross": cross_step,
+        "pick": pick_step,
+        "windows": windows_step,
+        "finish": finish_step,
+    }
+    held = None
+    for name, *ks in ORDER:
+        result = steps[name](*ks)
+        held = result if result else held
+    covariance, mean = held
     return covariance, jnp.transpose(mean, (1, 0, 2))
 
 

time: 106 us -> 97.8 us (0.923); the launches traced: 104 us -> 97.3 us
  Pallas kernels: 38.3 us -> 28.3 us
  waiting for transfers between devices: 15.9 us -> 17.2 us
    pallas_call x21, Pallas kernels: 38.3 us -> 28.3 us  [call(): pl.pallas_call(kernel, in_specs=list(specs), out_specs=(list(outs) if out...]
    ppermute x6, waiting for transfers between devices: 2.41 us -> 10.6 us  [gram_step(): mine[k] = (out, lax.ppermute(out, 'year', inward))]
    ppermute x6, waiting for transfers between devices: 11 us -> 6.1 us  [cross_step(): rows[k] = (own, lax.ppermute(send, 'year', outward))]
    ppermute x2, starting transfers between devices: 4.23 us -> 7.15 us  [pick_step(): totals.append(lax.ppermute(out, 'day', right))]
    ppermute x2, waiting for transfers between devices: 2.42 us -> 0.01 us  [pick_step(): totals.append(lax.ppermute(out, 'day', left))]
    ppermute x2, starting transfers between devices: 5.23 us -> 3.32 us  [pick_step(): totals.append(lax.ppermute(out, 'day', left))]
  transfers between devices with their start and end apart: 22 -> 22, of which waited for: 10 -> 7; matrix products, arithmetic and copies ran while one was open for 0% -> 0% of each run, Pallas kernels for 28% -> 21%
where the time goes in v2:
time: 97.8 us; the launch traced here: 97.3 us
  starting transfers between devices  49.5 us (51%)
  Pallas kernels  28.3 us (29%)
  waiting for transfers between devices  17.2 us (18%)
  local copies, waits for them, and re-layouts  1.43 us (1%)
  between operations  1.02 us (1%)
    pallas_call x21, Pallas kernels, call(): pl.pallas_call(kernel, in_specs=list(specs), out_specs=(list(outs) if out...  28.3 us
    ppermute x6, starting transfers between devices, gram_step(): mine[k] = (out, lax.ppermute(out, 'year', inward))  27 us
    ppermute x6, waiting for transfers between devices, gram_step(): mine[k] = (out, lax.ppermute(out, 'year', inward))  10.6 us
    ppermute x6, starting transfers between devices, cross_step(): rows[k] = (own, lax.ppermute(send, 'year', outward))  7.74 us
    ppermute x2, starting transfers between devices, pick_step(): totals.append(lax.ppermute(out, 'day', right))  7.15 us
    ppermute x6, waiting for transfers between devices, cross_step(): rows[k] = (own, lax.ppermute(send, 'year', outward))  6.1 us
    ppermute x6, starting transfers between devices, inner_step(): sums[k] = (send, keep, lax.ppermute(send, 'year', between))  4.24 us
    ppermute x2, starting transfers between devices, pick_step(): totals.append(lax.ppermute(out, 'day', left))  3.32 us
  transfers between devices with their start and end apart: 22, of which 7 were waited for; matrix products, arithmetic and copies ran while one was open for 0% of the time, Pallas kernels for 21%

profile of v2, /device:TPU:1, one launch (start us, length us, event | category | flops | bytes accessed | tf_op | source)
XLA Modules:
  0.0 97.3 jit_solution(11287650532115139083)
XLA Ops:
  0.6 0.0 copy-start.2
  0.7 0.7 copy-done.2
  1.3 5.0 %shard_map.41 = (f32[1040,128]{1,0:T(8,128)}, f32[8,128]{1,0:T(8,128)S(1)}) custom-call(s32[1,2,23]{2,1,0:T(2,128)S(1)} %bitcast.3, bf16[23,2,1000,256]{3,2,1,0:T(8,128)(2,1)} %samples_ref.5, f32[8,128]{1,0:T(8,128)S(1)} %broadcast_in_dim.7.after_ref), custom_call_target="tpu_custom_call" | custom-call | tf_op jit(solution)/shard_map/pallas_call | solution.py:31
  6.4 4.8 %collective-permute-start = (f32[1040,128]{1,0:T(8,128)}, f32[1040,128]{1,0:T(8,128)}, u32[]{:S(2)}, u32[]{:S(2)}) collective-permute-start(f32[1040,128]{1,0:T(8,128)} %get-tuple-element.61.mine_ref), channel_id=1, source_target_pairs={{0,2},{6,4},{1,3},{7,5},{8,10},{14,12},{9,11},{15,13},{16,18},{22,... | collective-permute-start | bytes 1597448 | tf_op jit(solution)/shard_map/ppermute | solution.py:472
  11.2 4.9 %shard_map.42 = (f32[1296,128]{1,0:T(8,128)S(1)}, f32[8,128]{1,0:T(8,128)S(1)}) custom-call(s32[1,2,23]{2,1,0:T(2,128)S(1)} %bitcast.4, bf16[23,2,1000,256]{3,2,1,0:T(8,128)(2,1)} %samples_ref.5, f32[8,128]{1,0:T(8,128)S(1)} %get-tuple-element.62.after_ref), custom_call_target="tpu_custom_call" | custom-call | tf_op jit(solution)/shard_map/pallas_call | solution.py:31
  16.1 1.3 %collective-permute-start.2 = (f32[1296,128]{1,0:T(8,128)S(1)}, f32[1296,128]{1,0:T(8,128)S(1)}, u32[]{:S(2)}, u32[]{:S(2)}) collective-permute-start(f32[1296,128]{1,0:T(8,128)S(1)} %get-tuple-element.67.mine_ref), channel_id=1, source_target_pairs={{0,2},{6,4},{1,3},{7,5},{8,10},{14,12},{9,11},{15,13},{16,18},{22,... | collective-permute-start | bytes 1990664 | tf_op jit(solution)/shard_map/ppermute | solution.py:472
  17.4 10.5 %shard_map.43 = (f32[1296,128]{1,0:T(8,128)S(1)}, f32[1040,128]{1,0:T(8,128)S(1)}, f32[784,128]{1,0:T(8,128)S(1)}, f32[520,128]{1,0:T(8,128)S(1)}, f32[8,128]{1,0:T(8,128)S(1)}) custom-call(s32[1,2,23]{2,1,0:T(2,128)S(1)} %bitcast.5, bf16[23,2,1000,256]{3,2,1,0:T(8,128)(2,1)} %samples_ref.5, f32[8,128]{1,0:T(8,128)S(1)} %get-tuple-element.63.after_ref), custom_call_target="tpu_custom_call" | custom-call | tf_op jit(solution)/shard_map/pallas_call | solution.py:31
  28.0 0.7 copy-done
  28.7 1.3 %collective-permute-start.4 = (f32[1296,128]{1,0:T(8,128)S(1)}, f32[1296,128]{1,0:T(8,128)S(1)}, u32[]{:S(2)}, u32[]{:S(2)}) collective-permute-start(f32[1296,128]{1,0:T(8,128)S(1)} %get-tuple-element.72.mine_ref), channel_id=1, source_target_pairs={{0,2},{6,4},{1,3},{7,5},{8,10},{14,12},{9,11},{15,13},{16,18},{22,... | collective-permute-start | bytes 1990664 | tf_op jit(solution)/shard_map/ppermute | solution.py:472
  30.0 0.0 collective-permute-done.came_ref
  30.1 1.3 %shard_map.44 = (f32[784,128]{1,0:T(8,128)S(1)}, f32[256,128]{1,0:T(8,128)S(1)}, f32[8,128]{1,0:T(8,128)S(1)}) custom-call(s32[1]{0:T(128)} %bitcast.year_ref, f32[1040,128]{1,0:T(8,128)} %get-tuple-element.61.mine_ref, f32[1040,128]{1,0:T(8,128)} %collective-permute-done.came_ref, f32[8,128]{1,0:T(8,128)S(1)} %get-tuple-element.64.after_ref), custom_call_target="tpu_custom_call" | custom-call | tf_op jit(solution)/shard_map/pallas_call | solution.py:31
  31.3 0.7 collective-permute-start.1
  32.0 3.5 %collective-permute-done.2.came_ref = f32[1296,128]{1,0:T(8,128)S(1)} collective-permute-done((f32[1296,128]{1,0:T(8,128)S(1)}, f32[1296,128]{1,0:T(8,128)S(1)}, u32[]{:S(2)}, u32[]{:S(2)}) %collective-permute-start.2) | collective-permute-done | bytes 663584 | tf_op jit(solution)/shard_map/ppermute | solution.py:472
  35.6 0.1 shard_map.45
  35.7 0.7 collective-permute-start.6
  36.4 6.7 %collective-permute-start.8 = (f32[1040,128]{1,0:T(8,128)S(1)}, f32[1040,128]{1,0:T(8,128)S(1)}, u32[]{:S(2)}, u32[]{:S(2)}) collective-permute-start(f32[1040,128]{1,0:T(8,128)S(1)} %get-tuple-element.81.mine_ref), channel_id=1, source_target_pairs={{0,2},{6,4},{1,3},{7,5},{8,10},{14,12},{9,11},{15,13},{16,18},{22,... | collective-permute-start | bytes 1597448 | tf_op jit(solution)/shard_map/ppermute | solution.py:472
  43.0 0.0 collective-permute-done.1.came_ref
  43.1 0.4 shard_map.46
  43.4 1.3 %collective-permute-start.3 = (f32[528,128]{1,0:T(8,128)S(1)}, f32[528,128]{1,0:T(8,128)S(1)}, u32[]{:S(2)}, u32[]{:S(2)}) collective-permute-start(f32[528,128]{1,0:T(8,128)S(1)} %get-tuple-element.71), channel_id=1, source_target_pairs={{2,0},{4,6},{3,1},{5,7},{10,8},{12,14},{11,9},{13,15},{18,16},{20,... | collective-permute-start | bytes 811016 | tf_op jit(solution)/shard_map/ppermute | solution.py:482
  44.7 5.1 %collective-permute-done.4.came_ref = f32[1296,128]{1,0:T(8,128)S(1)} collective-permute-done((f32[1296,128]{1,0:T(8,128)S(1)}, f32[1296,128]{1,0:T(8,128)S(1)}, u32[]{:S(2)}, u32[]{:S(2)}) %collective-permute-start.4) | collective-permute-done | bytes 663584 | tf_op jit(solution)/shard_map/ppermute | solution.py:472
  49.8 0.1 shard_map.47
  49.9 0.8 collective-permute-start.10
  50.7 0.0 collective-permute-done.3.came_ref
  50.8 0.0 collective-permute-done.6.came_ref
  50.8 0.5 shard_map.49
  51.3 1.3 %collective-permute-start.7 = (f32[656,128]{1,0:T(8,128)S(1)}, f32[656,128]{1,0:T(8,128)S(1)}, u32[]{:S(2)}, u32[]{:S(2)}) collective-permute-start(f32[656,128]{1,0:T(8,128)S(1)} %get-tuple-element.80), channel_id=1, source_target_pairs={{2,0},{4,6},{3,1},{5,7},{10,8},{12,14},{11,9},{13,15},{18,16},{20,... | collective-permute-start | bytes 1007624 | tf_op jit(solution)/shard_map/ppermute | solution.py:482
  52.6 6.7 %collective-permute-start.14 = (f32[784,128]{1,0:T(8,128)S(1)}, f32[784,128]{1,0:T(8,128)S(1)}, u32[]{:S(2)}, u32[]{:S(2)}) collective-permute-start(f32[784,128]{1,0:T(8,128)S(1)} %copy-done.1), channel_id=1, source_target_pairs={{0,2},{6,4},{1,3},{7,5},{8,10},{14,12},{9,11},{15,13},{16,18},{22,... | collective-permute-start | bytes 1204232 | tf_op jit(solution)/shard_map/ppermute | solution.py:472
  59.3 1.9 %collective-permute-done.8.came_ref = f32[1040,128]{1,0:T(8,128)S(1)} collective-permute-done((f32[1040,128]{1,0:T(8,128)S(1)}, f32[1040,128]{1,0:T(8,128)S(1)}, u32[]{:S(2)}, u32[]{:S(2)}) %collective-permute-start.8) | collective-permute-done | bytes 532512 | tf_op jit(solution)/shard_map/ppermute | solution.py:472
  61.2 0.1 shard_map.50
  61.3 0.7 collective-permute-start.13
  62.0 0.5 collective-permute-done.7.came_ref
  62.5 0.0 collective-permute-done.10.came_ref
  62.5 0.5 shard_map.52
  63.0 1.3 %collective-permute-start.11 = (f32[656,128]{1,0:T(8,128)S(1)}, f32[656,128]{1,0:T(8,128)S(1)}, u32[]{:S(2)}, u32[]{:S(2)}) collective-permute-start(f32[656,128]{1,0:T(8,128)S(1)} %get-tuple-element.89), channel_id=1, source_target_pairs={{2,0},{4,6},{3,1},{5,7},{10,8},{12,14},{11,9},{13,15},{18,16},{20,... | collective-permute-start | bytes 1007624 | tf_op jit(solution)/shard_map/ppermute | solution.py:482
  64.3 6.2 %collective-permute-start.12 = (f32[520,128]{1,0:T(8,128)S(1)}, f32[520,128]{1,0:T(8,128)S(1)}, u32[]{:S(2)}, u32[]{:S(2)}) collective-permute-start(f32[520,128]{1,0:T(8,128)S(1)} %get-tuple-element.90.mine_ref), channel_id=1, source_target_pairs={{0,2},{6,4},{1,3},{7,5},{8,10},{14,12},{9,11},{15,13},{16,18},{22,... | collective-permute-start | bytes 798728 | tf_op jit(solution)/shard_map/ppermute | solution.py:472
  70.5 0.0 collective-permute-done.14.came_ref
  70.5 0.1 shard_map.53
  70.6 0.7 collective-permute-start.18
  71.3 0.0 collective-permute-done.13.came_ref
  71.3 0.4 shard_map.54
  71.6 1.3 %collective-permute-start.17 = (f32[528,128]{1,0:T(8,128)S(1)}, f32[528,128]{1,0:T(8,128)S(1)}, u32[]{:S(2)}, u32[]{:S(2)}) collective-permute-start(f32[528,128]{1,0:T(8,128)S(1)} %get-tuple-element.101), channel_id=1, source_target_pairs={{2,0},{4,6},{3,1},{5,7},{10,8},{12,14},{11,9},{13,15},{18,16},{20,... | collective-permute-start | bytes 811016 | tf_op jit(solution)/shard_map/ppermute | solution.py:482
  72.9 3.3 %collective-permute-start.5 = (f32[528,128]{1,0:T(8,128)S(1)}, f32[528,128]{1,0:T(8,128)S(1)}, u32[]{:S(2)}, u32[]{:S(2)}) collective-permute-start(f32[528,128]{1,0:T(8,128)S(1)} %get-tuple-element.75.refs_0_), channel_id=1, source_target_pairs={{8,0},{16,8},{24,16},{0,24},{9,1},{17,9},{25,17},{1,25},{10,2},{18... | collective-permute-start | bytes 811016 | tf_op jit(solution)/shard_map/ppermute | solution.py:491
  76.2 0.0 collective-permute-done.12.came_ref
  76.3 0.7 collective-permute-start.19
  77.0 0.0 collective-permute-done.11.came_ref
  77.0 2.5 %collective-permute-start.9 = (f32[656,128]{1,0:T(8,128)S(1)}, f32[656,128]{1,0:T(8,128)S(1)}, u32[]{:S(2)}, u32[]{:S(2)}) collective-permute-start(f32[656,128]{1,0:T(8,128)S(1)} %get-tuple-element.84.refs_2_), channel_id=1, source_target_pairs={{0,8},{8,16},{16,24},{24,0},{1,9},{9,17},{17,25},{25,1},{2,10},{10... | collective-permute-start | bytes 1007624 | tf_op jit(solution)/shard_map/ppermute | solution.py:494
  79.5 0.1 shard_map.56
  79.6 0.0 collective-permute-done.18.came_ref
  79.6 0.0 collective-permute-start.15
  79.6 0.3 shard_map.57
  79.9 1.2 %collective-permute-done.17.came_ref = f32[528,128]{1,0:T(8,128)S(1)} collective-permute-done((f32[528,128]{1,0:T(8,128)S(1)}, f32[528,128]{1,0:T(8,128)S(1)}, u32[]{:S(2)}, u32[]{:S(2)}) %collective-permute-start.17) | collective-permute-done | bytes 270368 | tf_op jit(solution)/shard_map/ppermute | solution.py:482
  81.1 1.3 %collective-permute-start.20 = (f32[400,128]{1,0:T(8,128)S(1)}, f32[400,128]{1,0:T(8,128)S(1)}, u32[]{:S(2)}, u32[]{:S(2)}) collective-permute-start(f32[400,128]{1,0:T(8,128)S(1)} %get-tuple-element.114), channel_id=1, source_target_pairs={{2,0},{4,6},{3,1},{5,7},{10,8},{12,14},{11,9},{13,15},{18,16},{20,... | collective-permute-start | bytes 614408 | tf_op jit(solution)/shard_map/ppermute | solution.py:482
  82.4 0.0 collective-permute-done.19.came_ref
  82.4 4.6 %collective-permute-start.16 = (f32[264,128]{1,0:T(8,128)S(1)}, f32[264,128]{1,0:T(8,128)S(1)}, u32[]{:S(2)}, u32[]{:S(2)}) collective-permute-start(f32[264,128]{1,0:T(8,128)S(1)} %get-tuple-element.99.refs_6_), channel_id=1, source_target_pairs={{0,8},{8,16},{16,24},{24,0},{1,9},{9,17},{17,25},{25,1},{2,10},{10... | collective-permute-start | bytes 405512 | tf_op jit(solution)/shard_map/ppermute | solution.py:494
  87.1 0.2 shard_map.59
  87.2 0.0 collective-permute-done.5.refs_1_
  87.3 1.3 %collective-permute-start.21 = (f32[264,128]{1,0:T(8,128)S(1)}, f32[264,128]{1,0:T(8,128)S(1)}, u32[]{:S(2)}, u32[]{:S(2)}) collective-permute-start(f32[264,128]{1,0:T(8,128)S(1)} %get-tuple-element.116), channel_id=1, source_target_pairs={{2,0},{4,6},{3,1},{5,7},{10,8},{12,14},{11,9},{13,15},{18,16},{20,... | collective-permute-start | bytes 405512 | tf_op jit(solution)/shard_map/ppermute | solution.py:482
  88.6 0.0 collective-permute-done.9.refs_3_
  88.6 0.5 collective-permute-done.16.refs_7_
  89.0 0.0 collective-permute-done.15.refs_5_
  89.0 1.4 %shard_map.60 = (f32[23,64,256]{2,1,0:T(8,128)S(1)}, f32[4,23,128]{2,1,0:T(8,128)S(1)}, f32[8,128]{1,0:T(8,128)S(1)}) custom-call(s32[1]{0:T(128)} %bitcast.year_ref, f32[528,128]{1,0:T(8,128)S(1)} %get-tuple-element.75.refs_0_, f32[528,128]{1,0:T(8,128)S(1)} %collective-permute-done.5.refs_1_, f32[656,128]{1,0:T(8,128)S(1)} %get-tuple-element.84.refs_2_, ...), custom_call_target="tpu_custom_call" | custom-call | tf_op jit(solution)/shard_map/pallas_call | solution.py:31
  90.5 4.4 %collective-permute-done.21.refs_3_ = f32[264,128]{1,0:T(8,128)S(1)} collective-permute-done((f32[264,128]{1,0:T(8,128)S(1)}, f32[264,128]{1,0:T(8,128)S(1)}, u32[]{:S(2)}, u32[]{:S(2)}) %collective-permute-start.21) | collective-permute-done | bytes 135200 | tf_op jit(solution)/shard_map/ppermute | solution.py:482
  94.9 0.0 collective-permute-done.20.refs_1_
  94.9 2.4 %shard_map.61 = (f32[1,23,64,256]{3,2,1,0:T(8,128)}, f32[23,1,64]{2,1,0:T(1,128)}, f32[8,128]{1,0:T(8,128)}) custom-call(s32[1]{0:T(128)} %bitcast.year_ref, f32[23,64,256]{2,1,0:T(8,128)S(1)} %get-tuple-element.111.win_ref, f32[4,23,128]{2,1,0:T(8,128)S(1)} %get-tuple-element.112.small_ref, f32[400,128]{1,0:T(8,128)S(1)} %get-tuple-element.113.refs_0_, ...), custom_call_target="tpu_custom_call" | custom-call | tf_op jit(solution)/shard_map/pallas_call | solution.py:31
  (8 shorter events, 0.1 us)
Async XLA Ops:
  0.6 0.7 copy-start.2
  6.4 23.7 %collective-permute-start = (f32[1040,128]{1,0:T(8,128)}, f32[1040,128]{1,0:T(8,128)}, u32[]{:S(2)}, u32[]{:S(2)}) collective-permute-start(f32[1040,128]{1,0:T(8,128)} %get-tuple-element.61.mine_ref), channel_id=1, source_target_pairs={{0,2},{6,4},{1,3},{7,5},{8,10},{14,12},{9,11},{15,13},{16,18},{22,... | collective-permute-start | bytes 1597448 | tf_op jit(solution)/shard_map/ppermute | solution.py:472
  16.1 19.5 %collective-permute-start.2 = (f32[1296,128]{1,0:T(8,128)S(1)}, f32[1296,128]{1,0:T(8,128)S(1)}, u32[]{:S(2)}, u32[]{:S(2)}) collective-permute-start(f32[1296,128]{1,0:T(8,128)S(1)} %get-tuple-element.67.mine_ref), channel_id=1, source_target_pairs={{0,2},{6,4},{1,3},{7,5},{8,10},{14,12},{9,11},{15,13},{16,18},{22,... | collective-permute-start | bytes 1990664 | tf_op jit(solution)/shard_map/ppermute | solution.py:472
  28.0 0.8 copy-start
  28.7 21.1 %collective-permute-start.4 = (f32[1296,128]{1,0:T(8,128)S(1)}, f32[1296,128]{1,0:T(8,128)S(1)}, u32[]{:S(2)}, u32[]{:S(2)}) collective-permute-start(f32[1296,128]{1,0:T(8,128)S(1)} %get-tuple-element.72.mine_ref), channel_id=1, source_target_pairs={{0,2},{6,4},{1,3},{7,5},{8,10},{14,12},{9,11},{15,13},{16,18},{22,... | collective-permute-start | bytes 1990664 | tf_op jit(solution)/shard_map/ppermute | solution.py:472
  31.3 11.7 %collective-permute-start.1 = (f32[784,128]{1,0:T(8,128)S(1)}, f32[784,128]{1,0:T(8,128)S(1)}, u32[]{:S(2)}, u32[]{:S(2)}) collective-permute-start(f32[784,128]{1,0:T(8,128)S(1)} %get-tuple-element.65.mine_ref), channel_id=1, source_target_pairs={{2,4},{4,2},{3,5},{5,3},{10,12},{12,10},{11,13},{13,11},{18,20},{2... | collective-permute-start | bytes 1204232 | tf_op jit(solution)/shard_map/ppermute | solution.py:477
  35.7 15.1 %collective-permute-start.6 = (f32[976,128]{1,0:T(8,128)S(1)}, f32[976,128]{1,0:T(8,128)S(1)}, u32[]{:S(2)}, u32[]{:S(2)}) collective-permute-start(f32[976,128]{1,0:T(8,128)S(1)} %get-tuple-element.76.mine_ref), channel_id=1, source_target_pairs={{2,4},{4,2},{3,5},{5,3},{10,12},{12,10},{11,13},{13,11},{18,20},{2... | collective-permute-start | bytes 1499144 | tf_op jit(solution)/shard_map/ppermute | solution.py:477
  36.4 24.8 %collective-permute-start.8 = (f32[1040,128]{1,0:T(8,128)S(1)}, f32[1040,128]{1,0:T(8,128)S(1)}, u32[]{:S(2)}, u32[]{:S(2)}) collective-permute-start(f32[1040,128]{1,0:T(8,128)S(1)} %get-tuple-element.81.mine_ref), channel_id=1, source_target_pairs={{0,2},{6,4},{1,3},{7,5},{8,10},{14,12},{9,11},{15,13},{16,18},{22,... | collective-permute-start | bytes 1597448 | tf_op jit(solution)/shard_map/ppermute | solution.py:472
  43.4 7.3 %collective-permute-start.3 = (f32[528,128]{1,0:T(8,128)S(1)}, f32[528,128]{1,0:T(8,128)S(1)}, u32[]{:S(2)}, u32[]{:S(2)}) collective-permute-start(f32[528,128]{1,0:T(8,128)S(1)} %get-tuple-element.71), channel_id=1, source_target_pairs={{2,0},{4,6},{3,1},{5,7},{10,8},{12,14},{11,9},{13,15},{18,16},{20,... | collective-permute-start | bytes 811016 | tf_op jit(solution)/shard_map/ppermute | solution.py:482
  49.8 2.8 %copy-start.1 = (f32[784,128]{1,0:T(8,128)S(1)}, f32[784,128]{1,0:T(8,128)}, u32[]{:S(2)}) copy-start(f32[784,128]{1,0:T(8,128)} %copy-done) | copy-start | bytes 1204228
  49.9 12.6 %collective-permute-start.10 = (f32[976,128]{1,0:T(8,128)S(1)}, f32[976,128]{1,0:T(8,128)S(1)}, u32[]{:S(2)}, u32[]{:S(2)}) collective-permute-start(f32[976,128]{1,0:T(8,128)S(1)} %get-tuple-element.85.mine_ref), channel_id=1, source_target_pairs={{2,4},{4,2},{3,5},{5,3},{10,12},{12,10},{11,13},{13,11},{18,20},{2... | collective-permute-start | bytes 1499144 | tf_op jit(solution)/shard_map/ppermute | solution.py:477
  51.3 11.2 %collective-permute-start.7 = (f32[656,128]{1,0:T(8,128)S(1)}, f32[656,128]{1,0:T(8,128)S(1)}, u32[]{:S(2)}, u32[]{:S(2)}) collective-permute-start(f32[656,128]{1,0:T(8,128)S(1)} %get-tuple-element.80), channel_id=1, source_target_pairs={{2,0},{4,6},{3,1},{5,7},{10,8},{12,14},{11,9},{13,15},{18,16},{20,... | collective-permute-start | bytes 1007624 | tf_op jit(solution)/shard_map/ppermute | solution.py:482
  52.6 17.9 %collective-permute-start.14 = (f32[784,128]{1,0:T(8,128)S(1)}, f32[784,128]{1,0:T(8,128)S(1)}, u32[]{:S(2)}, u32[]{:S(2)}) collective-permute-start(f32[784,128]{1,0:T(8,128)S(1)} %copy-done.1), channel_id=1, source_target_pairs={{0,2},{6,4},{1,3},{7,5},{8,10},{14,12},{9,11},{15,13},{16,18},{22,... | collective-permute-start | bytes 1204232 | tf_op jit(solution)/shard_map/ppermute | solution.py:472
  61.3 10.0 %collective-permute-start.13 = (f32[784,128]{1,0:T(8,128)S(1)}, f32[784,128]{1,0:T(8,128)S(1)}, u32[]{:S(2)}, u32[]{:S(2)}) collective-permute-start(f32[784,128]{1,0:T(8,128)S(1)} %get-tuple-element.91.mine_ref), channel_id=1, source_target_pairs={{2,4},{4,2},{3,5},{5,3},{10,12},{12,10},{11,13},{13,11},{18,20},{2... | collective-permute-start | bytes 1204232 | tf_op jit(solution)/shard_map/ppermute | solution.py:477
  63.0 14.0 %collective-permute-start.11 = (f32[656,128]{1,0:T(8,128)S(1)}, f32[656,128]{1,0:T(8,128)S(1)}, u32[]{:S(2)}, u32[]{:S(2)}) collective-permute-start(f32[656,128]{1,0:T(8,128)S(1)} %get-tuple-element.89), channel_id=1, source_target_pairs={{2,0},{4,6},{3,1},{5,7},{10,8},{12,14},{11,9},{13,15},{18,16},{20,... | collective-permute-start | bytes 1007624 | tf_op jit(solution)/shard_map/ppermute | solution.py:482
  64.3 11.9 %collective-permute-start.12 = (f32[520,128]{1,0:T(8,128)S(1)}, f32[520,128]{1,0:T(8,128)S(1)}, u32[]{:S(2)}, u32[]{:S(2)}) collective-permute-start(f32[520,128]{1,0:T(8,128)S(1)} %get-tuple-element.90.mine_ref), channel_id=1, source_target_pairs={{0,2},{6,4},{1,3},{7,5},{8,10},{14,12},{9,11},{15,13},{16,18},{22,... | collective-permute-start | bytes 798728 | tf_op jit(solution)/shard_map/ppermute | solution.py:472
  70.6 9.0 %collective-permute-start.18 = (f32[592,128]{1,0:T(8,128)S(1)}, f32[592,128]{1,0:T(8,128)S(1)}, u32[]{:S(2)}, u32[]{:S(2)}) collective-permute-start(f32[592,128]{1,0:T(8,128)S(1)} %get-tuple-element.102.mine_ref), channel_id=1, source_target_pairs={{2,4},{4,2},{3,5},{5,3},{10,12},{12,10},{11,13},{13,11},{18,20},{2... | collective-permute-start | bytes 909320 | tf_op jit(solution)/shard_map/ppermute | solution.py:477
  71.6 9.5 %collective-permute-start.17 = (f32[528,128]{1,0:T(8,128)S(1)}, f32[528,128]{1,0:T(8,128)S(1)}, u32[]{:S(2)}, u32[]{:S(2)}) collective-permute-start(f32[528,128]{1,0:T(8,128)S(1)} %get-tuple-element.101), channel_id=1, source_target_pairs={{2,0},{4,6},{3,1},{5,7},{10,8},{12,14},{11,9},{13,15},{18,16},{20,... | collective-permute-start | bytes 811016 | tf_op jit(solution)/shard_map/ppermute | solution.py:482
  72.9 14.3 %collective-permute-start.5 = (f32[528,128]{1,0:T(8,128)S(1)}, f32[528,128]{1,0:T(8,128)S(1)}, u32[]{:S(2)}, u32[]{:S(2)}) collective-permute-start(f32[528,128]{1,0:T(8,128)S(1)} %get-tuple-element.75.refs_0_), channel_id=1, source_target_pairs={{8,0},{16,8},{24,16},{0,24},{9,1},{17,9},{25,17},{1,25},{10,2},{18... | collective-permute-start | bytes 811016 | tf_op jit(solution)/shard_map/ppermute | solution.py:491
  76.3 6.1 %collective-permute-start.19 = (f32[392,128]{1,0:T(8,128)S(1)}, f32[392,128]{1,0:T(8,128)S(1)}, u32[]{:S(2)}, u32[]{:S(2)}) collective-permute-start(f32[392,128]{1,0:T(8,128)S(1)} %get-tuple-element.107.mine_ref), channel_id=1, source_target_pairs={{2,4},{4,2},{3,5},{5,3},{10,12},{12,10},{11,13},{13,11},{18,20},{2... | collective-permute-start | bytes 602120 | tf_op jit(solution)/shard_map/ppermute | solution.py:477
  77.0 11.6 %collective-permute-start.9 = (f32[656,128]{1,0:T(8,128)S(1)}, f32[656,128]{1,0:T(8,128)S(1)}, u32[]{:S(2)}, u32[]{:S(2)}) collective-permute-start(f32[656,128]{1,0:T(8,128)S(1)} %get-tuple-element.84.refs_2_), channel_id=1, source_target_pairs={{0,8},{8,16},{16,24},{24,0},{1,9},{9,17},{17,25},{25,1},{2,10},{10... | collective-permute-start | bytes 1007624 | tf_op jit(solution)/shard_map/ppermute | solution.py:494
  79.6 9.4 %collective-permute-start.15 = (f32[400,128]{1,0:T(8,128)S(1)}, f32[400,128]{1,0:T(8,128)S(1)}, u32[]{:S(2)}, u32[]{:S(2)}) collective-permute-start(f32[400,128]{1,0:T(8,128)S(1)} %get-tuple-element.98.refs_4_), channel_id=1, source_target_pairs={{8,0},{16,8},{24,16},{0,24},{9,1},{17,9},{25,17},{1,25},{10,2},{18... | collective-permute-start | bytes 614408 | tf_op jit(solution)/shard_map/ppermute | solution.py:491
  81.1 13.8 %collective-permute-start.20 = (f32[400,128]{1,0:T(8,128)S(1)}, f32[400,128]{1,0:T(8,128)S(1)}, u32[]{:S(2)}, u32[]{:S(2)}) collective-permute-start(f32[400,128]{1,0:T(8,128)S(1)} %get-tuple-element.114), channel_id=1, source_target_pairs={{2,0},{4,6},{3,1},{5,7},{10,8},{12,14},{11,9},{13,15},{18,16},{20,... | collective-permute-start | bytes 614408 | tf_op jit(solution)/shard_map/ppermute | solution.py:482
  82.4 6.6 %collective-permute-start.16 = (f32[264,128]{1,0:T(8,128)S(1)}, f32[264,128]{1,0:T(8,128)S(1)}, u32[]{:S(2)}, u32[]{:S(2)}) collective-permute-start(f32[264,128]{1,0:T(8,128)S(1)} %get-tuple-element.99.refs_6_), channel_id=1, source_target_pairs={{0,8},{8,16},{16,24},{24,0},{1,9},{9,17},{17,25},{25,1},{2,10},{10... | collective-permute-start | bytes 405512 | tf_op jit(solution)/shard_map/ppermute | solution.py:494
  87.3 7.6 %collective-permute-start.21 = (f32[264,128]{1,0:T(8,128)S(1)}, f32[264,128]{1,0:T(8,128)S(1)}, u32[]{:S(2)}, u32[]{:S(2)}) collective-permute-start(f32[264,128]{1,0:T(8,128)S(1)} %get-tuple-element.116), channel_id=1, source_target_pairs={{2,0},{4,6},{3,1},{5,7},{10,8},{12,14},{11,9},{13,15},{18,16},{20,... | collective-permute-start | bytes 405512 | tf_op jit(solution)/shard_map/ppermute | solution.py:482

commit v3 on v2

--- a/solution.py
+++ b/solution.py
@@ -12,6 +12,7 @@
 BLOCK = 64
 SUBLANES = 8
 FULL, CROSS, OWN = 4 * BLOCK, 3 * BLOCK, 2 * BLOCK
+PAIR = BLOCK + BLOCK // 2
 SMALL = 3
 TOKEN = (SUBLANES, LANES)
 SCALARS = pl.BlockSpec(memory_space=pltpu.SMEM)
@@ -28,16 +29,21 @@
 
 
 def call(kernel, args, specs, shapes, scratch, flops, moved, mebibytes=16, outs=None):
+    *args, (after, *others) = args
     results = pl.pallas_call(
-        kernel,
-        in_specs=list(specs),
+        lambda *refs: kernel(*refs[len(others) :]),
+        in_specs=[ANYWHERE] * len(others) + list(specs),
         out_specs=(list(outs) if outs else [INSIDE] * len(shapes)) + [INSIDE],
         out_shape=[jax.ShapeDtypeStruct(shape, jnp.float32) for shape in list(shapes) + [TOKEN]],
         scratch_shapes=scratch,
         cost_estimate=pl.CostEstimate(flops=0, bytes_accessed=0, transcendentals=0),
         compiler_params=pltpu.CompilerParams(vmem_limit_bytes=mebibytes * 1024 * 1024),
-    )(*args)
-    return results[:-1], results[-1]
+    )(*others, *args, after)
+    return results[:-1], results[-1:]
+
+
+def sent_rows(days):
+    return days * CROSS + days // 2 * PAIR + days % 2 * BLOCK
 
 
 def iotas(shape):
@@ -56,8 +62,55 @@
     return packed, diagonal
 
 
-def gram_kernel(parts, counts_ref, samples_ref, after_ref, *refs):
-    outs, token_ref, held, arrived = refs[: len(parts)], *refs[len(parts) :]
+def own_side(row, lane, low_half):
+    ahead = jnp.where(low_half, lane - row, row - lane - 1)
+    return (lane < BLOCK) & (ahead >= 0)
+
+
+def half_rows(ref, i, low_half):
+    return ref[pl.ds(pl.multiple_of(i * FULL + LANES + jnp.where(low_half, 0, BLOCK), BLOCK), BLOCK)]
+
+
+def pack_sent(days, low_half, mine_ref, sent_ref):
+    row, lane = iotas((BLOCK, LANES))
+    own = own_side(row, lane, low_half)
+    small, at = days * FULL, sent_rows(days)
+    sent_ref[at:] = mine_ref[small:]
+
+    def day(i, carry):
+        src = pl.multiple_of(i * FULL, FULL)
+        dst = pl.multiple_of(i * CROSS, CROSS)
+        sent_ref[pl.ds(dst, LANES)] = mine_ref[pl.ds(src, LANES)]
+        sent_ref[pl.ds(dst + LANES, BLOCK)] = half_rows(mine_ref, i, ~low_half)
+        diagonal = jnp.sum(jnp.where(row == lane, half_rows(mine_ref, i, low_half), 0.0), axis=0, keepdims=True)
+        kept = mine_ref[pl.ds(small + SMALL * i, 1)]
+        sent_ref[pl.ds(at + SMALL * i, 1)] = jnp.where(low_half | (lane[:1] >= BLOCK), kept, diagonal)
+        return carry
+
+    lax.fori_loop(0, days, day, 0)
+
+    def pair(p, carry):
+        first, second = half_rows(mine_ref, 2 * p, low_half), half_rows(mine_ref, 2 * p + 1, low_half)
+        turned = jnp.concatenate([first, second], axis=0).T[:BLOCK]
+        below = jnp.where(low_half, first, turned)
+        above = jnp.where(low_half, swap(turned), second)
+        triangles = jnp.where(row > lane, below, above)
+        dst = pl.multiple_of(days * CROSS + p * PAIR, PAIR // 3)
+        sent_ref[pl.ds(dst, BLOCK)] = jnp.where(lane < BLOCK, swap(first), second)
+        rest = jnp.where(lane[: BLOCK // 2] < BLOCK, triangles[: BLOCK // 2], swap(triangles[BLOCK // 2 :]))
+        sent_ref[pl.ds(dst + BLOCK, BLOCK // 2)] = rest
+        return carry
+
+    lax.fori_loop(0, days // 2, pair, 0)
+    if days % 2:
+        last = days * CROSS + days // 2 * PAIR
+        sent_ref[last : last + BLOCK] = jnp.where(own, 0.0, half_rows(mine_ref, days - 1, low_half))
+
+
+def gram_kernel(parts, counts_ref, year_ref, samples_ref, after_ref, *refs):
+    outs, sents = refs[: len(parts)], refs[len(parts) : 2 * len(parts)]
+    token_ref, held, arrived = refs[2 * len(parts) :]
+    low_half = year_ref[0] < 2
     groups, slots, width = held.shape[1:]
     lane = lax.broadcasted_iota(jnp.int32, (1, LANES), 1)
     rank = lax.broadcasted_iota(jnp.int32, (1, slots), 1)
@@ -77,7 +130,7 @@
                     copy.start()
             slot += number
     slot = 0
-    for runs, out_ref in zip(parts, outs):
+    for runs, out_ref, sent_ref in zip(parts, outs, sents):
         days = length(runs)
         small = days * FULL
         out_ref[small:] = jnp.zeros((small_rows(days), LANES), jnp.float32)
@@ -116,16 +169,18 @@
             slot += number
         last = small + SMALL * days
         out_ref[last : last + 1] = numbers.astype(jnp.float32)
-
-
-def gram(samples, counts, parts, after):
+        pack_sent(days, low_half, out_ref, sent_ref)
+
+
+def gram(samples, counts, year, parts, after):
     _, groups, slots, width = samples.shape
     days = sum(length(runs) for runs in parts)
     rows = [length(runs) * FULL + small_rows(length(runs)) for runs in parts]
+    rows += [sent_rows(length(runs)) + small_rows(length(runs)) for runs in parts]
     outs, token = call(
         functools.partial(gram_kernel, parts),
-        (counts, samples, after),
-        (SCALARS, ANYWHERE, ANYWHERE),
+        (counts, year, samples, after),
+        (SCALARS, SCALARS, ANYWHERE, ANYWHERE),
         [(size, LANES) for size in rows],
         [
             pltpu.VMEM((days, groups, slots, width), samples.dtype),
@@ -135,29 +190,50 @@
         2 * days * groups * slots * width + 4 * sum(rows) * LANES,
         44,
     )
-    return outs, token
+    return list(zip(outs[: len(parts)], outs[len(parts) :])), token
 
 
 def inner_kernel(days, year_ref, mine_ref, came_ref, after_ref, send_ref, keep_ref, token_ref):
     low_half = year_ref[0] < 2
     token_ref[...] = jnp.zeros_like(token_ref)
+    row, lane = iotas((BLOCK, LANES))
+    at = sent_rows(days)
 
     def day(i, carry):
         src = pl.multiple_of(i * FULL, FULL)
         dst = pl.multiple_of(i * CROSS, CROSS)
-        own = pl.multiple_of(i * BLOCK, BLOCK)
-        q = pl.ds(src, LANES)
-        send_ref[pl.ds(dst, LANES)] = mine_ref[q] + came_ref[q]
-        low = pl.ds(src + LANES, BLOCK)
-        high = pl.ds(src + LANES + BLOCK, BLOCK)
-        low_sum = mine_ref[low] + came_ref[low]
-        high_sum = mine_ref[high] + came_ref[high]
-        send_ref[pl.ds(dst + LANES, BLOCK)] = jnp.where(low_half, high_sum, low_sum)
-        keep_ref[pl.ds(own, BLOCK)] = jnp.where(low_half, low_sum, high_sum)
+        send_ref[pl.ds(dst, LANES)] = mine_ref[pl.ds(src, LANES)] + came_ref[pl.ds(dst, LANES)]
+        other = pl.ds(dst + LANES, BLOCK)
+        send_ref[other] = half_rows(mine_ref, i, ~low_half) + came_ref[other]
         return carry
 
     lax.fori_loop(0, days, day, 0)
-    send_ref[days * CROSS :] = mine_ref[days * FULL :] + came_ref[days * FULL :]
+
+    def pair(p, carry):
+        src = pl.multiple_of(days * CROSS + p * PAIR, PAIR // 3)
+        blocks = came_ref[pl.ds(src, BLOCK)]
+        rest = came_ref[pl.ds(src + BLOCK, BLOCK // 2)]
+        triangles = jnp.concatenate([rest, swap(rest)], axis=0)
+        turned = jnp.concatenate([triangles, jnp.zeros_like(triangles)], axis=0).T[:BLOCK]
+        side = jnp.where(low_half, row - lane, lane - row)
+        for k, block in enumerate((swap(blocks), blocks)):
+            i = 2 * p + k
+            triangle = jnp.where(low_half, (triangles, turned)[k], (turned, triangles)[k])
+            diagonal = jnp.where(low_half, 0.0, came_ref[pl.ds(at + SMALL * i, 1)])
+            triangle = jnp.where(side > 0, triangle, jnp.where(side == 0, diagonal, 0.0))
+            keep_ref[pl.ds(pl.multiple_of(i * BLOCK, BLOCK), BLOCK)] = half_rows(mine_ref, i, low_half) + jnp.where(
+                lane < BLOCK, triangle, block
+            )
+        return carry
+
+    lax.fori_loop(0, days // 2, pair, 0)
+    if days % 2:
+        last = at - BLOCK
+        keep_ref[(days - 1) * BLOCK :] = half_rows(mine_ref, days - 1, low_half) + came_ref[last:at]
+    row, lane = iotas((small_rows(days), LANES))
+    diagonals = (lax.rem(row, SMALL) == 0) & (row < SMALL * days) & (lane < BLOCK)
+    came = jnp.where(diagonals & ~low_half, 0.0, came_ref[at:])
+    send_ref[days * CROSS :] = mine_ref[days * FULL :] + came
 
 
 def inner(year, mine, came, days, after):
@@ -218,31 +294,50 @@
     return (year == 0) | (year == 3)
 
 
-def pick_kernel(runs, year_ref, own_ref, came_ref, after_ref, *refs):
+def day_rows(year, number, i, mine_ref, own_ref, came_ref):
+    outer, low_half = is_outer(year), year < 2
+    row, lane = iotas((BLOCK, LANES))
+    alone = jnp.where(own_side(row, lane, low_half), half_rows(mine_ref, i, low_half), 0.0)
+    start = i * OWN
+    top = jnp.where(outer, came_ref[start : start + BLOCK] + alone, own_ref[start : start + BLOCK])
+    middle = start + BLOCK
+    bottom = jnp.where(outer, came_ref[middle : middle + BLOCK], own_ref[middle : middle + BLOCK])
+    at = number * OWN + SMALL * i
+    small = jnp.where(outer, came_ref[at : at + SMALL], own_ref[at : at + SMALL])
+    kept = mine_ref[number * FULL + SMALL * i : number * FULL + SMALL * i + 1]
+    diagonal = small[:1] + jnp.where(outer & ~low_half & (lane[:1] < BLOCK), kept, 0.0)
+    return jnp.concatenate([top, bottom], axis=0), diagonal, small[1:2], small[2:3]
+
+
+def day_counts(year, number, own_ref, came_ref):
+    at = number * OWN + SMALL * number
+    return jnp.where(is_outer(year), came_ref[at : at + 1], own_ref[at : at + 1])
+
+
+def pick_kernel(runs, year_ref, mine_ref, own_ref, came_ref, after_ref, *refs):
     outs, token_ref = refs[:-1], refs[-1]
-    outer = is_outer(year_ref[0])
+    year = year_ref[0]
     token_ref[...] = jnp.zeros_like(token_ref)
-
-    def pick(start, size):
-        return jnp.where(outer, came_ref[start : start + size], own_ref[start : start + size])
-
-    small = length(runs) * OWN
+    days = length(runs)
+    counts = day_counts(year, days, own_ref, came_ref)
     at = 0
     for (_, number), out_ref in zip(runs, outs):
-        out_ref[: number * OWN] = pick(at * OWN, number * OWN)
-        row = number * OWN
-        out_ref[row : row + SMALL * number] = pick(small + SMALL * at, SMALL * number)
-        counts = pick(small + SMALL * length(runs), 1)
-        row += SMALL * number
-        out_ref[row : row + 1] = pltpu.roll(counts, (LANES - at) % LANES, 1)
+        small = number * OWN
+        for i in range(number):
+            rows, *lines = day_rows(year, days, at + i, mine_ref, own_ref, came_ref)
+            out_ref[i * OWN : (i + 1) * OWN] = rows
+            for k, line in enumerate(lines):
+                out_ref[small + SMALL * i + k : small + SMALL * i + k + 1] = line
+        last = small + SMALL * number
+        out_ref[last : last + 1] = pltpu.roll(counts, (LANES - at) % LANES, 1)
         at += number
 
 
-def pick(year, own, came, runs, after):
+def pick(year, mine, own, came, runs, after):
     return call(
         functools.partial(pick_kernel, runs),
-        (year, own, came, after),
-        (SCALARS, INSIDE, INSIDE, ANYWHERE),
+        (year, mine, own, came, after),
+        (SCALARS, INSIDE, INSIDE, INSIDE, ANYWHERE),
         [(size * OWN + small_rows(size), LANES) for _, size in runs],
         [],
         0,
@@ -345,30 +440,25 @@
 
 
 def finish_kernel(places, pieces, year_ref, win_ref, small_ref, *refs):
-    pairs, (after_ref, cov_ref, mean_ref, token_ref, formed, sent) = refs[: 2 * len(places)], refs[2 * len(places) :]
+    held, (after_ref, cov_ref, mean_ref, token_ref, formed, sent) = refs[: 3 * len(places)], refs[3 * len(places) :]
     token_ref[...] = jnp.zeros_like(token_ref)
     year = year_ref[0]
-    outer = is_outer(year)
     days = win_ref.shape[0]
     lane = lax.broadcasted_iota(jnp.int32, (1, LANES), 1)
     day_of = lax.broadcasted_iota(jnp.int32, (days, LANES), 0)
     low, high, count = small_ref[1], small_ref[2], small_ref[SMALL]
     extras = []
     for p, (place, number) in enumerate(places):
-        own_ref, came_ref = pairs[2 * p : 2 * p + 2]
-
-        def pick(start, size):
-            return jnp.where(outer, came_ref[start : start + size], own_ref[start : start + size])
-
-        small = number * OWN
-        numbers = pick(small + SMALL * number, 1)
+        arrays = held[3 * p : 3 * p + 3]
+        numbers = day_counts(year, number, *arrays[1:])
         for i in range(number):
+            rows, diagonal, more_low, more_high = day_rows(year, number, i, *arrays)
             inside = jnp.abs(day_of - (place + i)) <= HALF
-            low += jnp.where(inside, pick(small + SMALL * i + 1, 1), 0.0)
-            high += jnp.where(inside, pick(small + SMALL * i + 2, 1), 0.0)
+            low += jnp.where(inside, more_low, 0.0)
+            high += jnp.where(inside, more_high, 0.0)
             extra = jnp.sum(jnp.where(lane == i, numbers, 0.0), axis=1, keepdims=True)
             count += jnp.where(inside, extra, 0.0)
-            extras.append((place + i, unpack(year, pick(i * OWN, OWN), pick(small + SMALL * i, 1))))
+            extras.append((place + i, unpack(year, rows, diagonal)))
     low = low / count
     high = high / count
     own = jnp.where(year < 2, low, high)
@@ -397,11 +487,11 @@
         copy.wait()
 
 
-def finish(year, win, small, pairs, places, after):
+def finish(year, win, small, held, places, after):
     days, _, width = win.shape
     size = -(-days // 3)
     pieces = tuple((first, min(size, days - first)) for first in range(0, days, size))
-    flat = [array for pair in pairs for array in pair]
+    flat = [array for arrays in held for array in arrays]
     (covariance, mean), _ = call(
         functools.partial(finish_kernel, places, pieces),
         (year, win, small, *flat, after),
@@ -461,15 +551,15 @@
     left = [((i + 1) % day_size, i) for i in range(day_size)]
     counts = jnp.transpose(counts, (0, 2, 1))
     parts = plan(days)
-    token = jnp.zeros(TOKEN, jnp.float32)
+    token = [jnp.zeros(TOKEN, jnp.float32)]
     mine, sums, rows = {}, {}, {}
-    totals, places = [], []
+    totals, places, halos = [], [], {}
 
     def gram_step(*ks):
         nonlocal token
-        outs, token = gram(samples, counts, tuple(parts[k] for k in ks), token)
-        for k, out in zip(ks, outs):
-            mine[k] = (out, lax.ppermute(out, "year", inward))
+        outs, token = gram(samples, counts, year, tuple(parts[k] for k in ks), token)
+        for k, (out, sent) in zip(ks, outs):
+            mine[k] = (out, lax.ppermute(sent, "year", inward))
 
     def inner_step(k):
         nonlocal token
@@ -479,7 +569,7 @@
     def cross_step(k):
         nonlocal token
         send, own, token = cross(year, *sums[k], length(parts[k]), token)
-        rows[k] = (own, lax.ppermute(send, "year", outward))
+        rows[k] = (mine[k][0], own, lax.ppermute(send, "year", outward))
 
     def pick_step(k):
         nonlocal token
@@ -490,9 +580,15 @@
             if start < HALF:
                 totals.append(lax.ppermute(out, "day", left))
                 places.append((start + HALF + days, size))
+                halos.setdefault(k, []).append(totals[-1])
             elif start >= days - HALF:
                 totals.append(lax.ppermute(out, "day", right))
                 places.append((start + HALF - days, size))
+                halos.setdefault(k, []).append(totals[-1])
+
+    def halo_step(k):
+        nonlocal token
+        token = [*token, *halos[k]]
 
     def windows_step():
         nonlocal token
@@ -508,6 +604,7 @@
         "inner": inner_step,
         "cross": cross_step,
         "pick": pick_step,
+        "halo": halo_step,
         "windows": windows_step,
         "finish": finish_step,
     }

time: 97.8 us -> 94.4 us (0.965)
  waiting for transfers between devices: 17.2 us -> 14.6 us
  starting transfers between devices: 49.5 us -> 47.3 us
  Pallas kernels: 28.3 us -> 30.3 us
    ppermute x12, waiting for transfers between devices: 16.7 us -> 14.1 us  [the longest x6 7.45 us: gram_step(): mine[k] = (out, lax.ppermute(sent, 'year', inward))]
    ppermute x12, starting transfers between devices: 34.8 us -> 32.7 us  [the longest x6 24.9 us: gram_step(): mine[k] = (out, lax.ppermute(sent, 'year', inward))]
    pallas_call x21, Pallas kernels: 28.3 us -> 30.3 us  [call(): pl.pallas_call(lambda *refs: kernel(*refs[len(others):]), in_specs=[ANYWH...]
  transfers between devices with their start and end apart: 22 -> 22, of which waited for: 7 -> 8; matrix products, arithmetic and copies ran while one was open for 0% -> 0% of each run, Pallas kernels for 21% -> 25%
where the time goes in v3:
time: 94.4 us; the launch traced here: 93.9 us
  starting transfers between devices  47.3 us (50%)
  Pallas kernels  30.3 us (32%)
  waiting for transfers between devices  14.6 us (15%)
  between operations  1.01 us (1%)
    pallas_call x21, Pallas kernels, call(): pl.pallas_call(lambda *refs: kernel(*refs[len(others):]), in_specs=[ANYWH...  30.3 us
    ppermute x6, starting transfers between devices, gram_step(): mine[k] = (out, lax.ppermute(sent, 'year', inward))  24.9 us
    ppermute x6, starting transfers between devices, cross_step(): rows[k] = (mine[k][0], own, lax.ppermute(send, 'year', outward))  7.74 us
    ppermute x6, waiting for transfers between devices, gram_step(): mine[k] = (out, lax.ppermute(sent, 'year', inward))  7.45 us
    ppermute x2, starting transfers between devices, pick_step(): totals.append(lax.ppermute(out, 'day', right))  7.13 us
    ppermute x6, waiting for transfers between devices, cross_step(): rows[k] = (mine[k][0], own, lax.ppermute(send, 'year', outward))  6.65 us
    ppermute x6, starting transfers between devices, inner_step(): sums[k] = (send, keep, lax.ppermute(send, 'year', between))  4.11 us
    ppermute x2, starting transfers between devices, pick_step(): totals.append(lax.ppermute(out, 'day', left))  3.35 us
  transfers between devices with their start and end apart: 22, of which 8 were waited for; matrix products, arithmetic and copies ran while one was open for 0% of the time, Pallas kernels for 25%

profile of v3, /device:TPU:1, one launch (start us, length us, event | category | flops | bytes accessed | tf_op | source)
XLA Modules:
  0.0 93.9 jit_solution(13258459776251933020)
XLA Ops:
  0.6 0.0 copy-start
  0.7 0.7 copy-done
  1.3 4.8 %shard_map.41 = (f32[1040,128]{1,0:T(8,128)S(1)}, f32[976,128]{1,0:T(8,128)S(1)}, f32[8,128]{1,0:T(8,128)S(1)}) custom-call(s32[1,2,23]{2,1,0:T(2,128)S(1)} %bitcast.3, s32[1]{0:T(128)} %bitcast.refs_1_.refs_0_, bf16[23,2,1000,256]{3,2,1,0:T(8,128)(2,1)} %refs_2_.5, f32[8,128]{1,0:T(8,128)S(1)} %broadcast_in_dim.7.refs_3_), custom_call_target="tpu_custom_call" | custom-call | tf_op jit(solution)/shard_map/pallas_call | solution.py:33
  6.1 4.1 %collective-permute-start = (f32[976,128]{1,0:T(8,128)S(1)}, f32[976,128]{1,0:T(8,128)S(1)}, u32[]{:S(2)}, u32[]{:S(2)}) collective-permute-start(f32[976,128]{1,0:T(8,128)S(1)} %get-tuple-element.68), channel_id=1, source_target_pairs={{0,2},{6,4},{1,3},{7,5},{8,10},{14,12},{9,11},{15,13},{16,18},{22,... | collective-permute-start | bytes 1499144 | tf_op jit(solution)/shard_map/ppermute | solution.py:562
  10.2 5.4 %shard_map.42 = (f32[1296,128]{1,0:T(8,128)S(1)}, f32[1232,128]{1,0:T(8,128)S(1)}, f32[8,128]{1,0:T(8,128)S(1)}) custom-call(s32[1,2,23]{2,1,0:T(2,128)S(1)} %bitcast.4, s32[1]{0:T(128)} %bitcast.refs_1_.refs_0_, bf16[23,2,1000,256]{3,2,1,0:T(8,128)(2,1)} %refs_2_.5, f32[8,128]{1,0:T(8,128)S(1)} %get-tuple-element.69.refs_3_), custom_call_target="tpu_custom_call" | custom-call | tf_op jit(solution)/shard_map/pallas_call | solution.py:33
  15.6 1.3 %collective-permute-start.2 = (f32[1232,128]{1,0:T(8,128)S(1)}, f32[1232,128]{1,0:T(8,128)S(1)}, u32[]{:S(2)}, u32[]{:S(2)}) collective-permute-start(f32[1232,128]{1,0:T(8,128)S(1)} %get-tuple-element.75), channel_id=1, source_target_pairs={{0,2},{6,4},{1,3},{7,5},{8,10},{14,12},{9,11},{15,13},{16,18},{22,... | collective-permute-start | bytes 1892360 | tf_op jit(solution)/shard_map/ppermute | solution.py:562
  16.9 12.1 %shard_map.43 = (f32[1296,128]{1,0:T(8,128)S(1)}, f32[1040,128]{1,0:T(8,128)S(1)}, f32[784,128]{1,0:T(8,128)S(1)}, f32[520,128]{1,0:T(8,128)S(1)}, f32[1232,128]...) custom-call(s32[1,2,23]{2,1,0:T(2,128)S(1)} %bitcast.5, ...), custom_call_target="tpu_custom_call" | custom-call | tf_op jit(solution)/shard_map/pallas_call | solution.py:33
  29.1 1.3 %collective-permute-start.4 = (f32[1232,128]{1,0:T(8,128)S(1)}, f32[1232,128]{1,0:T(8,128)S(1)}, u32[]{:S(2)}, u32[]{:S(2)}) collective-permute-start(f32[1232,128]{1,0:T(8,128)S(1)} %get-tuple-element.81), channel_id=1, source_target_pairs={{0,2},{6,4},{1,3},{7,5},{8,10},{14,12},{9,11},{15,13},{16,18},{22,... | collective-permute-start | bytes 1892360 | tf_op jit(solution)/shard_map/ppermute | solution.py:562
  30.4 0.0 collective-permute-done.refs_2_
  30.4 0.4 shard_map.44
  30.8 0.7 collective-permute-start.1
  31.5 2.2 %collective-permute-done.2.refs_2_ = f32[1232,128]{1,0:T(8,128)S(1)} collective-permute-done((f32[1232,128]{1,0:T(8,128)S(1)}, f32[1232,128]{1,0:T(8,128)S(1)}, u32[]{:S(2)}, u32[]{:S(2)}) %collective-permute-start.2) | collective-permute-done | bytes 630816 | tf_op jit(solution)/shard_map/ppermute | solution.py:562
  33.7 0.4 shard_map.45
  34.1 0.7 collective-permute-start.6
  34.8 6.7 %collective-permute-start.8 = (f32[976,128]{1,0:T(8,128)S(1)}, f32[976,128]{1,0:T(8,128)S(1)}, u32[]{:S(2)}, u32[]{:S(2)}) collective-permute-start(f32[976,128]{1,0:T(8,128)S(1)} %get-tuple-element.91), channel_id=1, source_target_pairs={{0,2},{6,4},{1,3},{7,5},{8,10},{14,12},{9,11},{15,13},{16,18},{22,... | collective-permute-start | bytes 1499144 | tf_op jit(solution)/shard_map/ppermute | solution.py:562
  41.4 0.0 collective-permute-done.1.refs_3_
  41.4 0.4 shard_map.46
  41.8 1.3 %collective-permute-start.3 = (f32[528,128]{1,0:T(8,128)S(1)}, f32[528,128]{1,0:T(8,128)S(1)}, u32[]{:S(2)}, u32[]{:S(2)}) collective-permute-start(f32[528,128]{1,0:T(8,128)S(1)} %get-tuple-element.79), channel_id=1, source_target_pairs={{2,0},{4,6},{3,1},{5,7},{10,8},{12,14},{11,9},{13,15},{18,16},{20,... | collective-permute-start | bytes 811016 | tf_op jit(solution)/shard_map/ppermute | solution.py:572
  43.1 4.1 %collective-permute-done.4.refs_2_ = f32[1232,128]{1,0:T(8,128)S(1)} collective-permute-done((f32[1232,128]{1,0:T(8,128)S(1)}, f32[1232,128]{1,0:T(8,128)S(1)}, u32[]{:S(2)}, u32[]{:S(2)}) %collective-permute-start.4) | collective-permute-done | bytes 630816 | tf_op jit(solution)/shard_map/ppermute | solution.py:562
  47.2 0.4 shard_map.47
  47.6 0.7 collective-permute-start.10
  48.3 0.7 collective-permute-done.3.refs_3_
  49.1 0.0 collective-permute-done.6.refs_3_
  49.1 0.5 shard_map.49
  49.6 1.3 %collective-permute-start.7 = (f32[656,128]{1,0:T(8,128)S(1)}, f32[656,128]{1,0:T(8,128)S(1)}, u32[]{:S(2)}, u32[]{:S(2)}) collective-permute-start(f32[656,128]{1,0:T(8,128)S(1)} %get-tuple-element.89), channel_id=1, source_target_pairs={{2,0},{4,6},{3,1},{5,7},{10,8},{12,14},{11,9},{13,15},{18,16},{20,... | collective-permute-start | bytes 1007624 | tf_op jit(solution)/shard_map/ppermute | solution.py:572
  50.9 5.9 %collective-permute-start.14 = (f32[752,128]{1,0:T(8,128)S(1)}, f32[752,128]{1,0:T(8,128)S(1)}, u32[]{:S(2)}, u32[]{:S(2)}) collective-permute-start(f32[752,128]{1,0:T(8,128)S(1)} %get-tuple-element.105), channel_id=1, source_target_pairs={{0,2},{6,4},{1,3},{7,5},{8,10},{14,12},{9,11},{15,13},{16,18},{22,... | collective-permute-start | bytes 1155080 | tf_op jit(solution)/shard_map/ppermute | solution.py:562
  56.8 1.1 %collective-permute-done.8.refs_2_ = f32[976,128]{1,0:T(8,128)S(1)} collective-permute-done((f32[976,128]{1,0:T(8,128)S(1)}, f32[976,128]{1,0:T(8,128)S(1)}, u32[]{:S(2)}, u32[]{:S(2)}) %collective-permute-start.8) | collective-permute-done | bytes 499744 | tf_op jit(solution)/shard_map/ppermute | solution.py:562
  57.9 0.3 shard_map.50
  58.3 0.7 collective-permute-start.13
  59.0 1.1 %collective-permute-done.7.refs_3_ = f32[656,128]{1,0:T(8,128)S(1)} collective-permute-done((f32[656,128]{1,0:T(8,128)S(1)}, f32[656,128]{1,0:T(8,128)S(1)}, u32[]{:S(2)}, u32[]{:S(2)}) %collective-permute-start.7) | collective-permute-done | bytes 335904 | tf_op jit(solution)/shard_map/ppermute | solution.py:572
  60.1 0.1 shard_map.51
  60.1 0.0 collective-permute-done.10.refs_3_
  60.1 0.5 shard_map.52
  60.6 1.3 %collective-permute-start.11 = (f32[656,128]{1,0:T(8,128)S(1)}, f32[656,128]{1,0:T(8,128)S(1)}, u32[]{:S(2)}, u32[]{:S(2)}) collective-permute-start(f32[656,128]{1,0:T(8,128)S(1)} %get-tuple-element.99), channel_id=1, source_target_pairs={{2,0},{4,6},{3,1},{5,7},{10,8},{12,14},{11,9},{13,15},{18,16},{20,... | collective-permute-start | bytes 1007624 | tf_op jit(solution)/shard_map/ppermute | solution.py:572
  61.9 5.6 %collective-permute-start.12 = (f32[488,128]{1,0:T(8,128)S(1)}, f32[488,128]{1,0:T(8,128)S(1)}, u32[]{:S(2)}, u32[]{:S(2)}) collective-permute-start(f32[488,128]{1,0:T(8,128)S(1)} %get-tuple-element.101), channel_id=1, source_target_pairs={{0,2},{6,4},{1,3},{7,5},{8,10},{14,12},{9,11},{15,13},{16,18},{22,... | collective-permute-start | bytes 749576 | tf_op jit(solution)/shard_map/ppermute | solution.py:562
  67.5 0.0 collective-permute-done.14.refs_2_
  67.5 0.2 shard_map.53
  67.7 0.7 collective-permute-start.18
  68.4 0.0 collective-permute-done.13.refs_3_
  68.4 0.4 shard_map.54
  68.8 1.3 %collective-permute-start.17 = (f32[528,128]{1,0:T(8,128)S(1)}, f32[528,128]{1,0:T(8,128)S(1)}, u32[]{:S(2)}, u32[]{:S(2)}) collective-permute-start(f32[528,128]{1,0:T(8,128)S(1)} %get-tuple-element.113), channel_id=1, source_target_pairs={{2,0},{4,6},{3,1},{5,7},{10,8},{12,14},{11,9},{13,15},{18,16},{20,... | collective-permute-start | bytes 811016 | tf_op jit(solution)/shard_map/ppermute | solution.py:572
  70.1 3.3 %collective-permute-start.5 = (f32[528,128]{1,0:T(8,128)S(1)}, f32[528,128]{1,0:T(8,128)S(1)}, u32[]{:S(2)}, u32[]{:S(2)}) collective-permute-start(f32[528,128]{1,0:T(8,128)S(1)} %get-tuple-element.84.refs_1_), channel_id=1, source_target_pairs={{8,0},{16,8},{24,16},{0,24},{9,1},{17,9},{25,17},{1,25},{10,2},{18... | collective-permute-start | bytes 811016 | tf_op jit(solution)/shard_map/ppermute | solution.py:581
  73.4 0.0 collective-permute-done.12.refs_2_
  73.4 0.2 shard_map.55
  73.6 0.7 collective-permute-start.19
  74.3 0.0 collective-permute-done.11.refs_3_
  74.3 2.2 %collective-permute-start.9 = (f32[656,128]{1,0:T(8,128)S(1)}, f32[656,128]{1,0:T(8,128)S(1)}, u32[]{:S(2)}, u32[]{:S(2)}) collective-permute-start(f32[656,128]{1,0:T(8,128)S(1)} %get-tuple-element.94.refs_3_), channel_id=1, source_target_pairs={{0,8},{8,16},{16,24},{24,0},{1,9},{9,17},{17,25},{25,1},{2,10},{10... | collective-permute-start | bytes 1007624 | tf_op jit(solution)/shard_map/ppermute | solution.py:585
  76.5 0.1 shard_map.56
  76.6 0.0 collective-permute-done.18.refs_3_
  76.6 0.0 collective-permute-start.15
  76.6 0.3 shard_map.57
  76.9 0.4 collective-permute-done.17.refs_3_
  77.3 1.3 %collective-permute-start.20 = (f32[400,128]{1,0:T(8,128)S(1)}, f32[400,128]{1,0:T(8,128)S(1)}, u32[]{:S(2)}, u32[]{:S(2)}) collective-permute-start(f32[400,128]{1,0:T(8,128)S(1)} %get-tuple-element.126), channel_id=1, source_target_pairs={{2,0},{4,6},{3,1},{5,7},{10,8},{12,14},{11,9},{13,15},{18,16},{20,... | collective-permute-start | bytes 614408 | tf_op jit(solution)/shard_map/ppermute | solution.py:572
  78.6 0.1 shard_map.58
  78.7 0.0 collective-permute-done.19.refs_3_
  78.7 4.9 %collective-permute-start.16 = (f32[264,128]{1,0:T(8,128)S(1)}, f32[264,128]{1,0:T(8,128)S(1)}, u32[]{:S(2)}, u32[]{:S(2)}) collective-permute-start(f32[264,128]{1,0:T(8,128)S(1)} %get-tuple-element.111.refs_7_), channel_id=1, source_target_pairs={{0,8},{8,16},{16,24},{24,0},{1,9},{9,17},{17,25},{25,1},{2,10},{10... | collective-permute-start | bytes 405512 | tf_op jit(solution)/shard_map/ppermute | solution.py:585
  83.6 0.2 shard_map.59
  83.8 0.0 collective-permute-done.5.refs_2_
  83.8 1.3 %collective-permute-start.21 = (f32[264,128]{1,0:T(8,128)S(1)}, f32[264,128]{1,0:T(8,128)S(1)}, u32[]{:S(2)}, u32[]{:S(2)}) collective-permute-start(f32[264,128]{1,0:T(8,128)S(1)} %get-tuple-element.128), channel_id=1, source_target_pairs={{2,0},{4,6},{3,1},{5,7},{10,8},{12,14},{11,9},{13,15},{18,16},{20,... | collective-permute-start | bytes 405512 | tf_op jit(solution)/shard_map/ppermute | solution.py:572
  85.1 0.5 collective-permute-done.16.refs_8_
  85.6 0.0 collective-permute-done.15.refs_6_
  85.6 1.4 %shard_map.60 = (f32[23,64,256]{2,1,0:T(8,128)S(1)}, f32[4,23,128]{2,1,0:T(8,128)S(1)}, f32[8,128]{1,0:T(8,128)S(1)}) custom-call(s32[1]{0:T(128)} %bitcast.refs_1_.refs_0_, f32[528,128]{1,0:T(8,128)S(1)} %get-tuple-element.84.refs_1_, f32[528,128]{1,0:T(8,128)S(1)} %collective-permute-done.5.refs_2_, f32[656,128]{1,0:T(8,128)S(1)} %get-tuple-element.94.refs_3_, ...), custom_call_target="tpu_custom_call" | custom-call | tf_op jit(solution)/shard_map/pallas_call | solution.py:33
  87.0 4.4 %collective-permute-done.21.refs_8_ = f32[264,128]{1,0:T(8,128)S(1)} collective-permute-done((f32[264,128]{1,0:T(8,128)S(1)}, f32[264,128]{1,0:T(8,128)S(1)}, u32[]{:S(2)}, u32[]{:S(2)}) %collective-permute-start.21) | collective-permute-done | bytes 135200 | tf_op jit(solution)/shard_map/ppermute | solution.py:572
  91.4 2.5 %shard_map.61 = (f32[1,23,64,256]{3,2,1,0:T(8,128)}, f32[23,1,64]{2,1,0:T(1,128)}, f32[8,128]{1,0:T(8,128)}) custom-call(s32[1]{0:T(128)} %bitcast.refs_1_.refs_0_, f32[23,64,256]{2,1,0:T(8,128)S(1)} %get-tuple-element.123.refs_1_, f32[4,23,128]{2,1,0:T(8,128)S(1)} %get-tuple-element.124.refs_2_, f32[784,128]{1,0:T(8,128)S(1)} %get-tuple-element.104.refs_1_.refs_3_, ...), custom_call_target="tpu_custom_call" | custom-call | tf_op jit(solution)/shard_map/pallas_call | solution.py:33
  (4 shorter events, 0.1 us)
Async XLA Ops:
  0.6 0.7 copy-start
  6.1 24.3 %collective-permute-start = (f32[976,128]{1,0:T(8,128)S(1)}, f32[976,128]{1,0:T(8,128)S(1)}, u32[]{:S(2)}, u32[]{:S(2)}) collective-permute-start(f32[976,128]{1,0:T(8,128)S(1)} %get-tuple-element.68), channel_id=1, source_target_pairs={{0,2},{6,4},{1,3},{7,5},{8,10},{14,12},{9,11},{15,13},{16,18},{22,... | collective-permute-start | bytes 1499144 | tf_op jit(solution)/shard_map/ppermute | solution.py:562
  15.6 18.1 %collective-permute-start.2 = (f32[1232,128]{1,0:T(8,128)S(1)}, f32[1232,128]{1,0:T(8,128)S(1)}, u32[]{:S(2)}, u32[]{:S(2)}) collective-permute-start(f32[1232,128]{1,0:T(8,128)S(1)} %get-tuple-element.75), channel_id=1, source_target_pairs={{0,2},{6,4},{1,3},{7,5},{8,10},{14,12},{9,11},{15,13},{16,18},{22,... | collective-permute-start | bytes 1892360 | tf_op jit(solution)/shard_map/ppermute | solution.py:562
  29.1 18.1 %collective-permute-start.4 = (f32[1232,128]{1,0:T(8,128)S(1)}, f32[1232,128]{1,0:T(8,128)S(1)}, u32[]{:S(2)}, u32[]{:S(2)}) collective-permute-start(f32[1232,128]{1,0:T(8,128)S(1)} %get-tuple-element.81), channel_id=1, source_target_pairs={{0,2},{6,4},{1,3},{7,5},{8,10},{14,12},{9,11},{15,13},{16,18},{22,... | collective-permute-start | bytes 1892360 | tf_op jit(solution)/shard_map/ppermute | solution.py:562
  30.8 10.6 %collective-permute-start.1 = (f32[784,128]{1,0:T(8,128)S(1)}, f32[784,128]{1,0:T(8,128)S(1)}, u32[]{:S(2)}, u32[]{:S(2)}) collective-permute-start(f32[784,128]{1,0:T(8,128)S(1)} %get-tuple-element.72.refs_1_), channel_id=1, source_target_pairs={{2,4},{4,2},{3,5},{5,3},{10,12},{12,10},{11,13},{13,11},{18,20},{2... | collective-permute-start | bytes 1204232 | tf_op jit(solution)/shard_map/ppermute | solution.py:567
  34.1 15.0 %collective-permute-start.6 = (f32[976,128]{1,0:T(8,128)S(1)}, f32[976,128]{1,0:T(8,128)S(1)}, u32[]{:S(2)}, u32[]{:S(2)}) collective-permute-start(f32[976,128]{1,0:T(8,128)S(1)} %get-tuple-element.85.refs_1_), channel_id=1, source_target_pairs={{2,4},{4,2},{3,5},{5,3},{10,12},{12,10},{11,13},{13,11},{18,20},{2... | collective-permute-start | bytes 1499144 | tf_op jit(solution)/shard_map/ppermute | solution.py:567
  34.8 23.2 %collective-permute-start.8 = (f32[976,128]{1,0:T(8,128)S(1)}, f32[976,128]{1,0:T(8,128)S(1)}, u32[]{:S(2)}, u32[]{:S(2)}) collective-permute-start(f32[976,128]{1,0:T(8,128)S(1)} %get-tuple-element.91), channel_id=1, source_target_pairs={{0,2},{6,4},{1,3},{7,5},{8,10},{14,12},{9,11},{15,13},{16,18},{22,... | collective-permute-start | bytes 1499144 | tf_op jit(solution)/shard_map/ppermute | solution.py:562
  41.8 7.2 %collective-permute-start.3 = (f32[528,128]{1,0:T(8,128)S(1)}, f32[528,128]{1,0:T(8,128)S(1)}, u32[]{:S(2)}, u32[]{:S(2)}) collective-permute-start(f32[528,128]{1,0:T(8,128)S(1)} %get-tuple-element.79), channel_id=1, source_target_pairs={{2,0},{4,6},{3,1},{5,7},{10,8},{12,14},{11,9},{13,15},{18,16},{20,... | collective-permute-start | bytes 811016 | tf_op jit(solution)/shard_map/ppermute | solution.py:572
  47.6 12.5 %collective-permute-start.10 = (f32[976,128]{1,0:T(8,128)S(1)}, f32[976,128]{1,0:T(8,128)S(1)}, u32[]{:S(2)}, u32[]{:S(2)}) collective-permute-start(f32[976,128]{1,0:T(8,128)S(1)} %get-tuple-element.95.refs_1_), channel_id=1, source_target_pairs={{2,4},{4,2},{3,5},{5,3},{10,12},{12,10},{11,13},{13,11},{18,20},{2... | collective-permute-start | bytes 1499144 | tf_op jit(solution)/shard_map/ppermute | solution.py:567
  49.6 10.5 %collective-permute-start.7 = (f32[656,128]{1,0:T(8,128)S(1)}, f32[656,128]{1,0:T(8,128)S(1)}, u32[]{:S(2)}, u32[]{:S(2)}) collective-permute-start(f32[656,128]{1,0:T(8,128)S(1)} %get-tuple-element.89), channel_id=1, source_target_pairs={{2,0},{4,6},{3,1},{5,7},{10,8},{12,14},{11,9},{13,15},{18,16},{20,... | collective-permute-start | bytes 1007624 | tf_op jit(solution)/shard_map/ppermute | solution.py:572
  50.9 16.7 %collective-permute-start.14 = (f32[752,128]{1,0:T(8,128)S(1)}, f32[752,128]{1,0:T(8,128)S(1)}, u32[]{:S(2)}, u32[]{:S(2)}) collective-permute-start(f32[752,128]{1,0:T(8,128)S(1)} %get-tuple-element.105), channel_id=1, source_target_pairs={{0,2},{6,4},{1,3},{7,5},{8,10},{14,12},{9,11},{15,13},{16,18},{22,... | collective-permute-start | bytes 1155080 | tf_op jit(solution)/shard_map/ppermute | solution.py:562
  58.3 10.1 %collective-permute-start.13 = (f32[784,128]{1,0:T(8,128)S(1)}, f32[784,128]{1,0:T(8,128)S(1)}, u32[]{:S(2)}, u32[]{:S(2)}) collective-permute-start(f32[784,128]{1,0:T(8,128)S(1)} %get-tuple-element.102.refs_1_), channel_id=1, source_target_pairs={{2,4},{4,2},{3,5},{5,3},{10,12},{12,10},{11,13},{13,11},{18,20},{2... | collective-permute-start | bytes 1204232 | tf_op jit(solution)/shard_map/ppermute | solution.py:567
  60.6 13.7 %collective-permute-start.11 = (f32[656,128]{1,0:T(8,128)S(1)}, f32[656,128]{1,0:T(8,128)S(1)}, u32[]{:S(2)}, u32[]{:S(2)}) collective-permute-start(f32[656,128]{1,0:T(8,128)S(1)} %get-tuple-element.99), channel_id=1, source_target_pairs={{2,0},{4,6},{3,1},{5,7},{10,8},{12,14},{11,9},{13,15},{18,16},{20,... | collective-permute-start | bytes 1007624 | tf_op jit(solution)/shard_map/ppermute | solution.py:572
  61.9 11.5 %collective-permute-start.12 = (f32[488,128]{1,0:T(8,128)S(1)}, f32[488,128]{1,0:T(8,128)S(1)}, u32[]{:S(2)}, u32[]{:S(2)}) collective-permute-start(f32[488,128]{1,0:T(8,128)S(1)} %get-tuple-element.101), channel_id=1, source_target_pairs={{0,2},{6,4},{1,3},{7,5},{8,10},{14,12},{9,11},{15,13},{16,18},{22,... | collective-permute-start | bytes 749576 | tf_op jit(solution)/shard_map/ppermute | solution.py:562
  67.7 8.9 %collective-permute-start.18 = (f32[592,128]{1,0:T(8,128)S(1)}, f32[592,128]{1,0:T(8,128)S(1)}, u32[]{:S(2)}, u32[]{:S(2)}) collective-permute-start(f32[592,128]{1,0:T(8,128)S(1)} %get-tuple-element.114.refs_1_), channel_id=1, source_target_pairs={{2,4},{4,2},{3,5},{5,3},{10,12},{12,10},{11,13},{13,11},{18,20},{2... | collective-permute-start | bytes 909320 | tf_op jit(solution)/shard_map/ppermute | solution.py:567
  68.8 8.5 %collective-permute-start.17 = (f32[528,128]{1,0:T(8,128)S(1)}, f32[528,128]{1,0:T(8,128)S(1)}, u32[]{:S(2)}, u32[]{:S(2)}) collective-permute-start(f32[528,128]{1,0:T(8,128)S(1)} %get-tuple-element.113), channel_id=1, source_target_pairs={{2,0},{4,6},{3,1},{5,7},{10,8},{12,14},{11,9},{13,15},{18,16},{20,... | collective-permute-start | bytes 811016 | tf_op jit(solution)/shard_map/ppermute | solution.py:572
  70.1 13.7 %collective-permute-start.5 = (f32[528,128]{1,0:T(8,128)S(1)}, f32[528,128]{1,0:T(8,128)S(1)}, u32[]{:S(2)}, u32[]{:S(2)}) collective-permute-start(f32[528,128]{1,0:T(8,128)S(1)} %get-tuple-element.84.refs_1_), channel_id=1, source_target_pairs={{8,0},{16,8},{24,16},{0,24},{9,1},{17,9},{25,17},{1,25},{10,2},{18... | collective-permute-start | bytes 811016 | tf_op jit(solution)/shard_map/ppermute | solution.py:581
  73.6 5.1 %collective-permute-start.19 = (f32[392,128]{1,0:T(8,128)S(1)}, f32[392,128]{1,0:T(8,128)S(1)}, u32[]{:S(2)}, u32[]{:S(2)}) collective-permute-start(f32[392,128]{1,0:T(8,128)S(1)} %get-tuple-element.119.refs_1_), channel_id=1, source_target_pairs={{2,4},{4,2},{3,5},{5,3},{10,12},{12,10},{11,13},{13,11},{18,20},{2... | collective-permute-start | bytes 602120 | tf_op jit(solution)/shard_map/ppermute | solution.py:567
  74.3 10.8 %collective-permute-start.9 = (f32[656,128]{1,0:T(8,128)S(1)}, f32[656,128]{1,0:T(8,128)S(1)}, u32[]{:S(2)}, u32[]{:S(2)}) collective-permute-start(f32[656,128]{1,0:T(8,128)S(1)} %get-tuple-element.94.refs_3_), channel_id=1, source_target_pairs={{0,8},{8,16},{16,24},{24,0},{1,9},{9,17},{17,25},{25,1},{2,10},{10... | collective-permute-start | bytes 1007624 | tf_op jit(solution)/shard_map/ppermute | solution.py:585
  76.6 9.0 %collective-permute-start.15 = (f32[400,128]{1,0:T(8,128)S(1)}, f32[400,128]{1,0:T(8,128)S(1)}, u32[]{:S(2)}, u32[]{:S(2)}) collective-permute-start(f32[400,128]{1,0:T(8,128)S(1)} %get-tuple-element.110.refs_5_), channel_id=1, source_target_pairs={{8,0},{16,8},{24,16},{0,24},{9,1},{17,9},{25,17},{1,25},{10,2},{18... | collective-permute-start | bytes 614408 | tf_op jit(solution)/shard_map/ppermute | solution.py:581
  77.3 14.1 %collective-permute-start.20 = (f32[400,128]{1,0:T(8,128)S(1)}, f32[400,128]{1,0:T(8,128)S(1)}, u32[]{:S(2)}, u32[]{:S(2)}) collective-permute-start(f32[400,128]{1,0:T(8,128)S(1)} %get-tuple-element.126), channel_id=1, source_target_pairs={{2,0},{4,6},{3,1},{5,7},{10,8},{12,14},{11,9},{13,15},{18,16},{20,... | collective-permute-start | bytes 614408 | tf_op jit(solution)/shard_map/ppermute | solution.py:572
  78.7 6.9 %collective-permute-start.16 = (f32[264,128]{1,0:T(8,128)S(1)}, f32[264,128]{1,0:T(8,128)S(1)}, u32[]{:S(2)}, u32[]{:S(2)}) collective-permute-start(f32[264,128]{1,0:T(8,128)S(1)} %get-tuple-element.111.refs_7_), channel_id=1, source_target_pairs={{0,8},{8,16},{16,24},{24,0},{1,9},{9,17},{17,25},{25,1},{2,10},{10... | collective-permute-start | bytes 405512 | tf_op jit(solution)/shard_map/ppermute | solution.py:585
  83.8 7.7 %collective-permute-start.21 = (f32[264,128]{1,0:T(8,128)S(1)}, f32[264,128]{1,0:T(8,128)S(1)}, u32[]{:S(2)}, u32[]{:S(2)}) collective-permute-start(f32[264,128]{1,0:T(8,128)S(1)} %get-tuple-element.128), channel_id=1, source_target_pairs={{2,0},{4,6},{3,1},{5,7},{10,8},{12,14},{11,9},{13,15},{18,16},{20,... | collective-permute-start | bytes 405512 | tf_op jit(solution)/shard_map/ppermute | solution.py:572

commit v4 on v3

--- a/solution.py
+++ b/solution.py
@@ -14,6 +14,7 @@
 FULL, CROSS, OWN = 4 * BLOCK, 3 * BLOCK, 2 * BLOCK
 PAIR = BLOCK + BLOCK // 2
 SMALL = 3
+AHEAD = 3
 TOKEN = (SUBLANES, LANES)
 SCALARS = pl.BlockSpec(memory_space=pltpu.SMEM)
 INSIDE = pl.BlockSpec(memory_space=pltpu.VMEM)
@@ -29,17 +30,16 @@
 
 
 def call(kernel, args, specs, shapes, scratch, flops, moved, mebibytes=16, outs=None):
-    *args, (after, *others) = args
     results = pl.pallas_call(
-        lambda *refs: kernel(*refs[len(others) :]),
-        in_specs=[ANYWHERE] * len(others) + list(specs),
+        kernel,
+        in_specs=list(specs),
         out_specs=(list(outs) if outs else [INSIDE] * len(shapes)) + [INSIDE],
         out_shape=[jax.ShapeDtypeStruct(shape, jnp.float32) for shape in list(shapes) + [TOKEN]],
         scratch_shapes=scratch,
         cost_estimate=pl.CostEstimate(flops=0, bytes_accessed=0, transcendentals=0),
         compiler_params=pltpu.CompilerParams(vmem_limit_bytes=mebibytes * 1024 * 1024),
-    )(*others, *args, after)
-    return results[:-1], results[-1:]
+    )(*args)
+    return results[:-1], results[-1]
 
 
 def sent_rows(days):
@@ -122,13 +122,24 @@
             for g in range(groups)
         ]
 
-    slot = 0
-    for runs in parts:
-        for start, number in runs:
-            for i in range(number):
-                for copy in copies(start + i, slot + i):
-                    copy.start()
-            slot += number
+    order = [start + i for runs in parts for start, number in runs for i in range(number)]
+    for slot in range(min(AHEAD, len(order))):
+        for copy in copies(order[slot], slot):
+            copy.start()
+
+    def later(slot):
+        day, at = jnp.int32(0), 0
+        for runs in parts:
+            for start, number in runs:
+                inside = (slot + AHEAD >= at) & (slot + AHEAD < at + number)
+                day = jnp.where(inside, start + slot + AHEAD - at, day)
+                at += number
+
+        @pl.when(slot + AHEAD < len(order))
+        def _():
+            for copy in copies(day, slot + AHEAD):
+                copy.start()
+
     slot = 0
     for runs, out_ref, sent_ref in zip(parts, outs, sents):
         days = length(runs)
@@ -141,6 +152,7 @@
             def day(i, numbers, start=start, at=at, slot=slot, out_ref=out_ref, small=small):
                 gram = jnp.zeros((width, width), jnp.float32)
                 total = jnp.zeros((1, width), jnp.float32)
+                later(slot + i)
                 for copy in copies(start + i, slot + i):
                     copy.wait()
                 for g in range(groups):
@@ -250,44 +262,54 @@
     return send, keep, token
 
 
-def cross_kernel(days, year_ref, mine_ref, keep_ref, came_ref, after_ref, send_ref, own_ref, token_ref):
+def own_size(days):
+    return days * OWN + small_rows(days)
+
+
+def cross_kernel(sizes, year_ref, *refs):
+    held, (_, send_ref, *owns, token_ref) = refs[: 3 * len(sizes)], refs[3 * len(sizes) :]
     low_half = year_ref[0] < 2
     token_ref[...] = jnp.zeros_like(token_ref)
     _, lane = iotas((BLOCK, LANES))
-
-    def day(i, carry):
-        src = pl.multiple_of(i * CROSS, CROSS)
-        own = pl.multiple_of(i * BLOCK, BLOCK)
-        dst = pl.multiple_of(i * OWN, OWN)
-        top = mine_ref[pl.ds(src, BLOCK)] + came_ref[pl.ds(src, BLOCK)]
-        bottom = mine_ref[pl.ds(src + BLOCK, BLOCK)] + came_ref[pl.ds(src + BLOCK, BLOCK)]
-        packed = keep_ref[pl.ds(own, BLOCK)] + came_ref[pl.ds(src + LANES, BLOCK)]
-        first = jnp.where(lane < BLOCK, top, swap(bottom))
-        second = jnp.where(lane < BLOCK, swap(top), bottom)
-        send_ref[pl.ds(dst, BLOCK)] = packed
-        own_ref[pl.ds(dst, BLOCK)] = packed
-        send_ref[pl.ds(dst + BLOCK, BLOCK)] = jnp.where(low_half, top, second)
-        own_ref[pl.ds(dst + BLOCK, BLOCK)] = jnp.where(low_half, bottom, first)
-        return carry
-
-    lax.fori_loop(0, days, day, 0)
-    small = mine_ref[days * CROSS :] + came_ref[days * CROSS :]
-    send_ref[days * OWN :] = small
-    own_ref[days * OWN :] = small
-
-
-def cross(year, mine, keep, came, days, after):
-    rows = days * OWN + small_rows(days)
-    (send, own), token = call(
-        functools.partial(cross_kernel, days),
-        (year, mine, keep, came, after),
-        (SCALARS, INSIDE, INSIDE, INSIDE, ANYWHERE),
-        [(rows, LANES)] * 2,
+    base = 0
+    for p, (days, own_ref) in enumerate(zip(sizes, owns)):
+        mine_ref, keep_ref, came_ref = held[3 * p : 3 * p + 3]
+
+        def day(i, carry, mine_ref=mine_ref, keep_ref=keep_ref, came_ref=came_ref, own_ref=own_ref, base=base):
+            src = pl.multiple_of(i * CROSS, CROSS)
+            own = pl.multiple_of(i * BLOCK, BLOCK)
+            dst = pl.multiple_of(i * OWN, OWN)
+            out = pl.multiple_of(base + i * OWN, SUBLANES)
+            top = mine_ref[pl.ds(src, BLOCK)] + came_ref[pl.ds(src, BLOCK)]
+            bottom = mine_ref[pl.ds(src + BLOCK, BLOCK)] + came_ref[pl.ds(src + BLOCK, BLOCK)]
+            packed = keep_ref[pl.ds(own, BLOCK)] + came_ref[pl.ds(src + LANES, BLOCK)]
+            first = jnp.where(lane < BLOCK, top, swap(bottom))
+            second = jnp.where(lane < BLOCK, swap(top), bottom)
+            send_ref[pl.ds(out, BLOCK)] = packed
+            own_ref[pl.ds(dst, BLOCK)] = packed
+            send_ref[pl.ds(out + BLOCK, BLOCK)] = jnp.where(low_half, top, second)
+            own_ref[pl.ds(dst + BLOCK, BLOCK)] = jnp.where(low_half, bottom, first)
+            return carry
+
+        lax.fori_loop(0, days, day, 0)
+        small = mine_ref[days * CROSS :] + came_ref[days * CROSS :]
+        send_ref[base + days * OWN : base + own_size(days)] = small
+        own_ref[days * OWN :] = small
+        base += own_size(days)
+
+
+def cross(year, held, sizes, after):
+    rows = [own_size(days) for days in sizes]
+    (send, *owns), token = call(
+        functools.partial(cross_kernel, sizes),
+        (year, *(array for arrays in held for array in arrays), after),
+        [SCALARS] + [INSIDE] * (3 * len(sizes)) + [ANYWHERE],
+        [(sum(rows), LANES)] + [(size, LANES) for size in rows],
         [],
-        days * CROSS * LANES,
-        3 * 4 * days * CROSS * LANES,
+        sum(sizes) * CROSS * LANES,
+        3 * 4 * sum(sizes) * CROSS * LANES,
     )
-    return send, own, token
+    return send, owns, token
 
 
 def is_outer(year):
@@ -314,34 +336,45 @@
     return jnp.where(is_outer(year), came_ref[at : at + 1], own_ref[at : at + 1])
 
 
-def pick_kernel(runs, year_ref, mine_ref, own_ref, came_ref, after_ref, *refs):
-    outs, token_ref = refs[:-1], refs[-1]
+def views(refs, bases, sizes):
+    held = []
+    for p, (base, size) in enumerate(zip(bases, sizes)):
+        mine_ref, own_ref, came_ref = refs[3 * p : 3 * p + 3]
+        held.append((mine_ref, own_ref, came_ref.at[pl.ds(base, own_size(size))]))
+    return held
+
+
+def pick_kernel(bases, sizes, moves, year_ref, *refs):
+    held = views(refs, bases, sizes)
+    (_, *outs, token_ref) = refs[3 * len(sizes) :]
     year = year_ref[0]
     token_ref[...] = jnp.zeros_like(token_ref)
-    days = length(runs)
-    counts = day_counts(year, days, own_ref, came_ref)
-    at = 0
-    for (_, number), out_ref in zip(runs, outs):
-        small = number * OWN
-        for i in range(number):
-            rows, *lines = day_rows(year, days, at + i, mine_ref, own_ref, came_ref)
-            out_ref[i * OWN : (i + 1) * OWN] = rows
-            for k, line in enumerate(lines):
-                out_ref[small + SMALL * i + k : small + SMALL * i + k + 1] = line
-        last = small + SMALL * number
-        out_ref[last : last + 1] = pltpu.roll(counts, (LANES - at) % LANES, 1)
-        at += number
-
-
-def pick(year, mine, own, came, runs, after):
+    lane = lax.broadcasted_iota(jnp.int32, (1, LANES), 1)
+    counts = [day_counts(year, size, *arrays[1:]) for size, arrays in zip(sizes, held)]
+    for stretch, out_ref in zip(moves, outs):
+        small = len(stretch) * OWN
+        numbers = jnp.zeros((1, LANES), jnp.float32)
+        for k, (p, i) in enumerate(stretch):
+            rows, *lines = day_rows(year, sizes[p], i, *held[p])
+            out_ref[k * OWN : (k + 1) * OWN] = rows
+            for l, line in enumerate(lines):
+                at = small + SMALL * k + l
+                out_ref[at : at + 1] = line
+            number = jnp.sum(jnp.where(lane == i, counts[p], 0.0), axis=1, keepdims=True)
+            numbers += jnp.where(lane == k, number, 0.0)
+        last = small + SMALL * len(stretch)
+        out_ref[last : last + 1] = numbers
+
+
+def pick(year, held, bases, sizes, moves, after):
     return call(
-        functools.partial(pick_kernel, runs),
-        (year, mine, own, came, after),
-        (SCALARS, INSIDE, INSIDE, INSIDE, ANYWHERE),
-        [(size * OWN + small_rows(size), LANES) for _, size in runs],
+        functools.partial(pick_kernel, bases, sizes, moves),
+        (year, *(array for arrays in held for array in arrays), after),
+        [SCALARS] + [INSIDE] * (3 * len(sizes)) + [ANYWHERE],
+        [(own_size(len(stretch)), LANES) for stretch in moves],
         [],
         0,
-        2 * 4 * own.size,
+        2 * 4 * sum(sizes) * OWN * LANES,
     )
 
 
@@ -439,8 +472,9 @@
     return win, small, token
 
 
-def finish_kernel(places, pieces, year_ref, win_ref, small_ref, *refs):
-    held, (after_ref, cov_ref, mean_ref, token_ref, formed, sent) = refs[: 3 * len(places)], refs[3 * len(places) :]
+def finish_kernel(bases, places, pieces, year_ref, win_ref, small_ref, *refs):
+    held = views(refs, bases, [number for _, number in places])
+    after_ref, cov_ref, mean_ref, token_ref, formed, sent = refs[3 * len(places) :]
     token_ref[...] = jnp.zeros_like(token_ref)
     year = year_ref[0]
     days = win_ref.shape[0]
@@ -449,7 +483,7 @@
     low, high, count = small_ref[1], small_ref[2], small_ref[SMALL]
     extras = []
     for p, (place, number) in enumerate(places):
-        arrays = held[3 * p : 3 * p + 3]
+        arrays = held[p]
         numbers = day_counts(year, number, *arrays[1:])
         for i in range(number):
             rows, diagonal, more_low, more_high = day_rows(year, number, i, *arrays)
@@ -487,13 +521,13 @@
         copy.wait()
 
 
-def finish(year, win, small, held, places, after):
+def finish(year, win, small, held, bases, places, after):
     days, _, width = win.shape
-    size = -(-days // 3)
+    size = -(-days // 6)
     pieces = tuple((first, min(size, days - first)) for first in range(0, days, size))
     flat = [array for arrays in held for array in arrays]
     (covariance, mean), _ = call(
-        functools.partial(finish_kernel, places, pieces),
+        functools.partial(finish_kernel, bases, places, pieces),
         (year, win, small, *flat, after),
         [SCALARS] + [INSIDE] * (2 + len(flat)) + [ANYWHERE],
         [(1, days, BLOCK, width), (days, 1, BLOCK)],
@@ -517,8 +551,9 @@
 ORDER = (
     ("gram", 0),
     ("gram", 1),
-    ("gram", 2, 3, 4, 5),
+    ("gram", 2),
     ("inner", 0),
+    ("gram", 3, 4, 5),
     ("inner", 1),
     ("cross", 0),
     ("inner", 2),
@@ -529,11 +564,11 @@
     ("cross", 2),
     ("inner", 4),
     ("cross", 3),
+    ("pick", 2),
     ("inner", 5),
-    ("pick", 2),
     ("cross", 4),
+    ("cross", 5),
     ("pick", 3),
-    ("cross", 5),
     ("windows",),
     ("finish", 4, 5),
 )
@@ -551,9 +586,9 @@
     left = [((i + 1) % day_size, i) for i in range(day_size)]
     counts = jnp.transpose(counts, (0, 2, 1))
     parts = plan(days)
-    token = [jnp.zeros(TOKEN, jnp.float32)]
+    token = jnp.zeros(TOKEN, jnp.float32)
     mine, sums, rows = {}, {}, {}
-    totals, places, halos = [], [], {}
+    totals, places, bases = [], [], {}
 
     def gram_step(*ks):
         nonlocal token
@@ -566,29 +601,42 @@
         send, keep, token = inner(year, *mine[k], length(parts[k]), token)
         sums[k] = (send, keep, lax.ppermute(send, "year", between))
 
-    def cross_step(k):
+    def cross_step(*ks):
         nonlocal token
-        send, own, token = cross(year, *sums[k], length(parts[k]), token)
-        rows[k] = (mine[k][0], own, lax.ppermute(send, "year", outward))
-
-    def pick_step(k):
+        sizes = [length(parts[k]) for k in ks]
+        send, owns, token = cross(year, [sums[k] for k in ks], sizes, token)
+        came = lax.ppermute(send, "year", outward)
+        base = 0
+        for k, own, size in zip(ks, owns, sizes):
+            rows[k] = (mine[k][0], own, came)
+            bases[k] = base
+            base += own_size(size)
+
+    def pick_step(*ks):
         nonlocal token
-        outs, token = pick(year, *rows[k], parts[k], token)
-        for (start, size), out in zip(parts[k], outs):
+        found = {}
+        for p, k in enumerate(ks):
+            at = 0
+            for start, size in parts[k]:
+                found.update({start + i: (p, at + i) for i in range(size)})
+                at += size
+        low = [day for day in sorted(found) if day < HALF]
+        high = [day for day in sorted(found) if day >= days - HALF]
+        inside = [day for day in sorted(found) if HALF <= day < days - HALF]
+        stretches = [stretch for stretch in (low, high, inside) if stretch]
+        moves = [[found[day] for day in stretch] for stretch in stretches]
+        sizes = [length(parts[k]) for k in ks]
+        outs, token = pick(year, [rows[k] for k in ks], [bases[k] for k in ks], sizes, moves, token)
+        for stretch, out in zip(stretches, outs):
+            start, size = stretch[0], len(stretch)
             totals.append(out)
             places.append((start + HALF, size))
             if start < HALF:
                 totals.append(lax.ppermute(out, "day", left))
                 places.append((start + HALF + days, size))
-                halos.setdefault(k, []).append(totals[-1])
             elif start >= days - HALF:
                 totals.append(lax.ppermute(out, "day", right))
                 places.append((start + HALF - days, size))
-                halos.setdefault(k, []).append(totals[-1])
-
-    def halo_step(k):
-        nonlocal token
-        token = [*token, *halos[k]]
 
     def windows_step():
         nonlocal token
@@ -597,14 +645,13 @@
 
     def finish_step(*ks):
         last = tuple(parts[k][0] for k in ks)
-        return finish(year, *held, [rows[k] for k in ks], last, token)
+        return finish(year, *held, [rows[k] for k in ks], [bases[k] for k in ks], last, token)
 
     steps = {
         "gram": gram_step,
         "inner": inner_step,
         "cross": cross_step,
         "pick": pick_step,
-        "halo": halo_step,
         "windows": windows_step,
         "finish": finish_step,
     }

time: 94.4 us -> 93.9 us (level)
  starting transfers between devices: 47.3 us -> 43.8 us
  Pallas kernels: 30.3 us -> 32.3 us
  waiting for transfers between devices: 14.6 us -> 15.7 us
    ppermute x2, starting transfers between devices: 7.13 us -> 3.78 us  [pick_step(): totals.append(lax.ppermute(out, 'day', right))]
    ppermute x6, waiting for transfers between devices: 6.65 us -> 8.95 us  [cross_step(): came = lax.ppermute(send, 'year', outward)]
    pallas_call x21 -> x22, Pallas kernels: 30.3 us -> 32.3 us  [call(): pl.pallas_call(kernel, in_specs=list(specs), out_specs=(list(outs) if out...]
    ppermute x6, waiting for transfers between devices: 7.45 us -> 5.64 us  [gram_step(): mine[k] = (out, lax.ppermute(sent, 'year', inward))]
  transfers between devices with their start and end apart: 22 -> 22, of which waited for: 8 -> 10; matrix products, arithmetic and copies ran while one was open for 0% -> 0% of each run, Pallas kernels for 25% -> 27%
where the time goes in v4:
time: 93.9 us; the launch traced here: 93.4 us
  starting transfers between devices  43.8 us (47%)
  Pallas kernels  32.3 us (34%)
  waiting for transfers between devices  15.7 us (17%)
  between operations  0.98 us (1%)
    pallas_call x22, Pallas kernels, call(): pl.pallas_call(kernel, in_specs=list(specs), out_specs=(list(outs) if out...  32.3 us
    ppermute x6, starting transfers between devices, gram_step(): mine[k] = (out, lax.ppermute(sent, 'year', inward))  24.9 us
    ppermute x6, waiting for transfers between devices, cross_step(): came = lax.ppermute(send, 'year', outward)  8.95 us
    ppermute x6, starting transfers between devices, cross_step(): came = lax.ppermute(send, 'year', outward)  7.73 us
    ppermute x6, waiting for transfers between devices, gram_step(): mine[k] = (out, lax.ppermute(sent, 'year', inward))  5.64 us
    ppermute x6, starting transfers between devices, inner_step(): sums[k] = (send, keep, lax.ppermute(send, 'year', between))  4.11 us
    ppermute x2, starting transfers between devices, pick_step(): totals.append(lax.ppermute(out, 'day', right))  3.78 us
    ppermute x2, starting transfers between devices, pick_step(): totals.append(lax.ppermute(out, 'day', left))  3.31 us
  transfers between devices with their start and end apart: 22, of which 10 were waited for; matrix products, arithmetic and copies ran while one was open for 0% of the time, Pallas kernels for 27%

profile of v4, /device:TPU:1, one launch (start us, length us, event | category | flops | bytes accessed | tf_op | source)
XLA Modules:
  0.0 93.4 jit_solution(2256882902048291569)
XLA Ops:
  0.6 0.0 copy-start
  0.7 0.7 copy-done
  1.3 4.8 %shard_map.41 = (f32[1040,128]{1,0:T(8,128)S(1)}, f32[976,128]{1,0:T(8,128)S(1)}, f32[8,128]{1,0:T(8,128)S(1)}) custom-call(s32[1,2,23]{2,1,0:T(2,128)S(1)} %bitcast.3, s32[1]{0:T(128)} %bitcast.year_ref, bf16[23,2,1000,256]{3,2,1,0:T(8,128)(2,1)} %samples_ref.7, f32[8,128]{1,0:T(8,128)S(1)} %broadcast_in_dim.7.after_ref), custom_call_target="tpu_custom_call" | custom-call | tf_op jit(solution)/shard_map/pallas_call | solution.py:33
  6.1 4.1 %collective-permute-start = (f32[976,128]{1,0:T(8,128)S(1)}, f32[976,128]{1,0:T(8,128)S(1)}, u32[]{:S(2)}, u32[]{:S(2)}) collective-permute-start(f32[976,128]{1,0:T(8,128)S(1)} %get-tuple-element.69), channel_id=1, source_target_pairs={{0,2},{6,4},{1,3},{7,5},{8,10},{14,12},{9,11},{15,13},{16,18},{22,... | collective-permute-start | bytes 1499144 | tf_op jit(solution)/shard_map/ppermute | solution.py:597
  10.2 5.4 %shard_map.42 = (f32[1296,128]{1,0:T(8,128)S(1)}, f32[1232,128]{1,0:T(8,128)S(1)}, f32[8,128]{1,0:T(8,128)S(1)}) custom-call(s32[1,2,23]{2,1,0:T(2,128)S(1)} %bitcast.4, s32[1]{0:T(128)} %bitcast.year_ref, bf16[23,2,1000,256]{3,2,1,0:T(8,128)(2,1)} %samples_ref.7, f32[8,128]{1,0:T(8,128)S(1)} %get-tuple-element.70.after_ref), custom_call_target="tpu_custom_call" | custom-call | tf_op jit(solution)/shard_map/pallas_call | solution.py:33
  15.6 1.3 %collective-permute-start.2 = (f32[1232,128]{1,0:T(8,128)S(1)}, f32[1232,128]{1,0:T(8,128)S(1)}, u32[]{:S(2)}, u32[]{:S(2)}) collective-permute-start(f32[1232,128]{1,0:T(8,128)S(1)} %get-tuple-element.76), channel_id=1, source_target_pairs={{0,2},{6,4},{1,3},{7,5},{8,10},{14,12},{9,11},{15,13},{16,18},{22,... | collective-permute-start | bytes 1892360 | tf_op jit(solution)/shard_map/ppermute | solution.py:597
  16.9 5.4 %shard_map.43 = (f32[1296,128]{1,0:T(8,128)S(1)}, f32[1232,128]{1,0:T(8,128)S(1)}, f32[8,128]{1,0:T(8,128)S(1)}) custom-call(s32[1,2,23]{2,1,0:T(2,128)S(1)} %bitcast.5, s32[1]{0:T(128)} %bitcast.year_ref, bf16[23,2,1000,256]{3,2,1,0:T(8,128)(2,1)} %samples_ref.7, f32[8,128]{1,0:T(8,128)S(1)} %get-tuple-element.71.after_ref), custom_call_target="tpu_custom_call" | custom-call | tf_op jit(solution)/shard_map/pallas_call | solution.py:33
  22.4 1.3 %collective-permute-start.4 = (f32[1232,128]{1,0:T(8,128)S(1)}, f32[1232,128]{1,0:T(8,128)S(1)}, u32[]{:S(2)}, u32[]{:S(2)}) collective-permute-start(f32[1232,128]{1,0:T(8,128)S(1)} %get-tuple-element.83), channel_id=1, source_target_pairs={{0,2},{6,4},{1,3},{7,5},{8,10},{14,12},{9,11},{15,13},{16,18},{22,... | collective-permute-start | bytes 1892360 | tf_op jit(solution)/shard_map/ppermute | solution.py:597
  23.7 0.4 shard_map.44
  24.1 0.7 collective-permute-start.1
  24.8 8.4 %shard_map.45 = (f32[1040,128]{1,0:T(8,128)S(1)}, f32[784,128]{1,0:T(8,128)S(1)}, f32[520,128]{1,0:T(8,128)S(1)}, f32[976,128]{1,0:T(8,128)S(1)}, f32[752,128]{1...) custom-call(s32[1,2,23]{2,1,0:T(2,128)S(1)} %bitcast.6, s32[1]{0:T(128)} %bitcast.year_ref, ...), custom_call_target="tpu_custom_call" | custom-call | tf_op jit(solution)/shard_map/pallas_call | solution.py:33
  33.2 0.5 collective-permute-done.2.came_ref
  33.7 0.4 shard_map.46
  34.1 0.7 collective-permute-start.6
  34.8 6.7 %collective-permute-start.8 = (f32[976,128]{1,0:T(8,128)S(1)}, f32[976,128]{1,0:T(8,128)S(1)}, u32[]{:S(2)}, u32[]{:S(2)}) collective-permute-start(f32[976,128]{1,0:T(8,128)S(1)} %get-tuple-element.93), channel_id=1, source_target_pairs={{0,2},{6,4},{1,3},{7,5},{8,10},{14,12},{9,11},{15,13},{16,18},{22,... | collective-permute-start | bytes 1499144 | tf_op jit(solution)/shard_map/ppermute | solution.py:597
  41.4 0.0 collective-permute-done.1.refs_2_
  41.5 0.4 shard_map.47
  41.8 1.3 %collective-permute-start.3 = (f32[528,128]{1,0:T(8,128)S(1)}, f32[528,128]{1,0:T(8,128)S(1)}, u32[]{:S(2)}, u32[]{:S(2)}) collective-permute-start(f32[528,128]{1,0:T(8,128)S(1)} %get-tuple-element.81), channel_id=1, source_target_pairs={{2,0},{4,6},{3,1},{5,7},{10,8},{12,14},{11,9},{13,15},{18,16},{20,... | collective-permute-start | bytes 811016 | tf_op jit(solution)/shard_map/ppermute | solution.py:608
  43.1 4.1 %collective-permute-done.4.came_ref = f32[1232,128]{1,0:T(8,128)S(1)} collective-permute-done((f32[1232,128]{1,0:T(8,128)S(1)}, f32[1232,128]{1,0:T(8,128)S(1)}, u32[]{:S(2)}, u32[]{:S(2)}) %collective-permute-start.4) | collective-permute-done | bytes 630816 | tf_op jit(solution)/shard_map/ppermute | solution.py:597
  47.2 0.4 shard_map.48
  47.6 0.7 collective-permute-start.10
  48.3 0.7 collective-permute-done.3.refs_2_
  49.0 0.1 shard_map.49
  49.1 0.0 collective-permute-done.6.refs_2_
  49.2 0.5 shard_map.50
  49.6 1.3 %collective-permute-start.7 = (f32[656,128]{1,0:T(8,128)S(1)}, f32[656,128]{1,0:T(8,128)S(1)}, u32[]{:S(2)}, u32[]{:S(2)}) collective-permute-start(f32[656,128]{1,0:T(8,128)S(1)} %get-tuple-element.91), channel_id=1, source_target_pairs={{2,0},{4,6},{3,1},{5,7},{10,8},{12,14},{11,9},{13,15},{18,16},{20,... | collective-permute-start | bytes 1007624 | tf_op jit(solution)/shard_map/ppermute | solution.py:608
  50.9 5.9 %collective-permute-start.13 = (f32[752,128]{1,0:T(8,128)S(1)}, f32[752,128]{1,0:T(8,128)S(1)}, u32[]{:S(2)}, u32[]{:S(2)}) collective-permute-start(f32[752,128]{1,0:T(8,128)S(1)} %get-tuple-element.105), channel_id=1, source_target_pairs={{0,2},{6,4},{1,3},{7,5},{8,10},{14,12},{9,11},{15,13},{16,18},{22,... | collective-permute-start | bytes 1155080 | tf_op jit(solution)/shard_map/ppermute | solution.py:597
  56.9 1.1 %collective-permute-done.8.came_ref = f32[976,128]{1,0:T(8,128)S(1)} collective-permute-done((f32[976,128]{1,0:T(8,128)S(1)}, f32[976,128]{1,0:T(8,128)S(1)}, u32[]{:S(2)}, u32[]{:S(2)}) %collective-permute-start.8) | collective-permute-done | bytes 499744 | tf_op jit(solution)/shard_map/ppermute | solution.py:597
  57.9 0.4 shard_map.51
  58.3 0.7 collective-permute-start.12
  59.0 1.1 %collective-permute-done.7.refs_2_ = f32[656,128]{1,0:T(8,128)S(1)} collective-permute-done((f32[656,128]{1,0:T(8,128)S(1)}, f32[656,128]{1,0:T(8,128)S(1)}, u32[]{:S(2)}, u32[]{:S(2)}) %collective-permute-start.7) | collective-permute-done | bytes 335904 | tf_op jit(solution)/shard_map/ppermute | solution.py:608
  60.1 0.1 shard_map.52
  60.2 0.5 shard_map.53
  60.7 1.3 %collective-permute-start.11 = (f32[656,128]{1,0:T(8,128)S(1)}, f32[656,128]{1,0:T(8,128)S(1)}, u32[]{:S(2)}, u32[]{:S(2)}) collective-permute-start(f32[656,128]{1,0:T(8,128)S(1)} %get-tuple-element.101), channel_id=1, source_target_pairs={{2,0},{4,6},{3,1},{5,7},{10,8},{12,14},{11,9},{13,15},{18,16},{20,... | collective-permute-start | bytes 1007624 | tf_op jit(solution)/shard_map/ppermute | solution.py:608
  62.0 5.6 %collective-permute-start.17 = (f32[488,128]{1,0:T(8,128)S(1)}, f32[488,128]{1,0:T(8,128)S(1)}, u32[]{:S(2)}, u32[]{:S(2)}) collective-permute-start(f32[488,128]{1,0:T(8,128)S(1)} %get-tuple-element.114), channel_id=1, source_target_pairs={{0,2},{6,4},{1,3},{7,5},{8,10},{14,12},{9,11},{15,13},{16,18},{22,... | collective-permute-start | bytes 749576 | tf_op jit(solution)/shard_map/ppermute | solution.py:597
  67.6 0.0 collective-permute-done.13.came_ref
  67.6 0.2 shard_map.54
  67.8 0.7 collective-permute-start.19
  68.5 3.3 %collective-permute-start.5 = (f32[528,128]{1,0:T(8,128)S(1)}, f32[528,128]{1,0:T(8,128)S(1)}, u32[]{:S(2)}, u32[]{:S(2)}) collective-permute-start(f32[528,128]{1,0:T(8,128)S(1)} %get-tuple-element.86.refs_0_), channel_id=1, source_target_pairs={{8,0},{16,8},{24,16},{0,24},{9,1},{17,9},{25,17},{1,25},{10,2},{18... | collective-permute-start | bytes 811016 | tf_op jit(solution)/shard_map/ppermute | solution.py:635
  71.8 0.0 collective-permute-done.12.refs_2_
  71.8 0.4 shard_map.55
  72.1 1.3 %collective-permute-start.16 = (f32[528,128]{1,0:T(8,128)S(1)}, f32[528,128]{1,0:T(8,128)S(1)}, u32[]{:S(2)}, u32[]{:S(2)}) collective-permute-start(f32[528,128]{1,0:T(8,128)S(1)} %get-tuple-element.112), channel_id=1, source_target_pairs={{2,0},{4,6},{3,1},{5,7},{10,8},{12,14},{11,9},{13,15},{18,16},{20,... | collective-permute-start | bytes 811016 | tf_op jit(solution)/shard_map/ppermute | solution.py:608
  73.4 0.0 collective-permute-done.11.refs_2_
  73.4 0.1 shard_map.56
  73.6 0.2 shard_map.57
  73.7 0.7 collective-permute-start.18
  74.4 2.1 %collective-permute-start.9 = (f32[656,128]{1,0:T(8,128)S(1)}, f32[656,128]{1,0:T(8,128)S(1)}, u32[]{:S(2)}, u32[]{:S(2)}) collective-permute-start(f32[656,128]{1,0:T(8,128)S(1)} %get-tuple-element.96.refs_2_), channel_id=1, source_target_pairs={{0,8},{8,16},{16,24},{24,0},{1,9},{9,17},{17,25},{25,1},{2,10},{10... | collective-permute-start | bytes 1007624 | tf_op jit(solution)/shard_map/ppermute | solution.py:638
  76.5 0.0 collective-permute-done.19.refs_2_
  76.5 0.0 collective-permute-start.14
  76.6 0.3 shard_map.58
  76.8 0.2 collective-permute-done.5.refs_1_
  77.0 1.3 %collective-permute-start.20 = (f32[400,128]{1,0:T(8,128)S(1)}, f32[400,128]{1,0:T(8,128)S(1)}, u32[]{:S(2)}, u32[]{:S(2)}) collective-permute-start(f32[400,128]{1,0:T(8,128)S(1)} %get-tuple-element.128), channel_id=1, source_target_pairs={{2,0},{4,6},{3,1},{5,7},{10,8},{12,14},{11,9},{13,15},{18,16},{20,... | collective-permute-start | bytes 614408 | tf_op jit(solution)/shard_map/ppermute | solution.py:608
  78.3 0.0 collective-permute-done.18.refs_2_
  78.3 1.6 %collective-permute-start.15 = (f32[264,128]{1,0:T(8,128)S(1)}, f32[264,128]{1,0:T(8,128)S(1)}, u32[]{:S(2)}, u32[]{:S(2)}) collective-permute-start(f32[264,128]{1,0:T(8,128)S(1)} %get-tuple-element.110.refs_6_), channel_id=1, source_target_pairs={{0,8},{8,16},{16,24},{24,0},{1,9},{9,17},{17,25},{25,1},{2,10},{10... | collective-permute-start | bytes 405512 | tf_op jit(solution)/shard_map/ppermute | solution.py:638
  79.9 0.2 shard_map.59
  80.1 1.8 %collective-permute-done.16.refs_2_ = f32[528,128]{1,0:T(8,128)S(1)} collective-permute-done((f32[528,128]{1,0:T(8,128)S(1)}, f32[528,128]{1,0:T(8,128)S(1)}, u32[]{:S(2)}, u32[]{:S(2)}) %collective-permute-start.16) | collective-permute-done | bytes 270368 | tf_op jit(solution)/shard_map/ppermute | solution.py:608
  81.9 1.3 %collective-permute-start.21 = (f32[264,128]{1,0:T(8,128)S(1)}, f32[264,128]{1,0:T(8,128)S(1)}, u32[]{:S(2)}, u32[]{:S(2)}) collective-permute-start(f32[264,128]{1,0:T(8,128)S(1)} %get-tuple-element.130), channel_id=1, source_target_pairs={{2,0},{4,6},{3,1},{5,7},{10,8},{12,14},{11,9},{13,15},{18,16},{20,... | collective-permute-start | bytes 405512 | tf_op jit(solution)/shard_map/ppermute | solution.py:608
  83.2 0.1 shard_map.60
  83.3 0.0 collective-permute-done.9.refs_3_
  83.3 1.0 %collective-permute-done.15.refs_7_ = f32[264,128]{1,0:T(8,128)S(1)} collective-permute-done((f32[264,128]{1,0:T(8,128)S(1)}, f32[264,128]{1,0:T(8,128)S(1)}, u32[]{:S(2)}, u32[]{:S(2)}) %collective-permute-start.15) | collective-permute-done | bytes 135200 | tf_op jit(solution)/shard_map/ppermute | solution.py:638
  84.3 1.4 %shard_map.61 = (f32[23,64,256]{2,1,0:T(8,128)S(1)}, f32[4,23,128]{2,1,0:T(8,128)S(1)}, f32[8,128]{1,0:T(8,128)S(1)}) custom-call(s32[1]{0:T(128)} %bitcast.year_ref, f32[528,128]{1,0:T(8,128)S(1)} %get-tuple-element.86.refs_0_, f32[528,128]{1,0:T(8,128)S(1)} %collective-permute-done.5.refs_1_, f32[656,128]{1,0:T(8,128)S(1)} %get-tuple-element.96.refs_2_, ...), custom_call_target="tpu_custom_call" | custom-call | tf_op jit(solution)/shard_map/pallas_call | solution.py:33
  85.7 1.9 %collective-permute-done.20.refs_2_ = f32[400,128]{1,0:T(8,128)S(1)} collective-permute-done((f32[400,128]{1,0:T(8,128)S(1)}, f32[400,128]{1,0:T(8,128)S(1)}, u32[]{:S(2)}, u32[]{:S(2)}) %collective-permute-start.20) | collective-permute-done | bytes 204832 | tf_op jit(solution)/shard_map/ppermute | solution.py:608
  87.6 3.4 %collective-permute-done.21.refs_5_ = f32[264,128]{1,0:T(8,128)S(1)} collective-permute-done((f32[264,128]{1,0:T(8,128)S(1)}, f32[264,128]{1,0:T(8,128)S(1)}, u32[]{:S(2)}, u32[]{:S(2)}) %collective-permute-start.21) | collective-permute-done | bytes 135200 | tf_op jit(solution)/shard_map/ppermute | solution.py:608
  91.0 2.4 %shard_map.62 = (f32[1,23,64,256]{3,2,1,0:T(8,128)}, f32[23,1,64]{2,1,0:T(1,128)}, f32[8,128]{1,0:T(8,128)}) custom-call(s32[1]{0:T(128)} %bitcast.year_ref, f32[23,64,256]{2,1,0:T(8,128)S(1)} %get-tuple-element.125.win_ref, f32[4,23,128]{2,1,0:T(8,128)S(1)} %get-tuple-element.126.small_ref, f32[784,128]{1,0:T(8,128)S(1)} %get-tuple-element.104.mine_ref.refs_0_, ...), custom_call_target="tpu_custom_call" | custom-call | tf_op jit(solution)/shard_map/pallas_call | solution.py:33
  (5 shorter events, 0.0 us)
Async XLA Ops:
  0.6 0.7 copy-start
  6.1 17.6 %collective-permute-start = (f32[976,128]{1,0:T(8,128)S(1)}, f32[976,128]{1,0:T(8,128)S(1)}, u32[]{:S(2)}, u32[]{:S(2)}) collective-permute-start(f32[976,128]{1,0:T(8,128)S(1)} %get-tuple-element.69), channel_id=1, source_target_pairs={{0,2},{6,4},{1,3},{7,5},{8,10},{14,12},{9,11},{15,13},{16,18},{22,... | collective-permute-start | bytes 1499144 | tf_op jit(solution)/shard_map/ppermute | solution.py:597
  15.6 18.1 %collective-permute-start.2 = (f32[1232,128]{1,0:T(8,128)S(1)}, f32[1232,128]{1,0:T(8,128)S(1)}, u32[]{:S(2)}, u32[]{:S(2)}) collective-permute-start(f32[1232,128]{1,0:T(8,128)S(1)} %get-tuple-element.76), channel_id=1, source_target_pairs={{0,2},{6,4},{1,3},{7,5},{8,10},{14,12},{9,11},{15,13},{16,18},{22,... | collective-permute-start | bytes 1892360 | tf_op jit(solution)/shard_map/ppermute | solution.py:597
  22.4 24.8 %collective-permute-start.4 = (f32[1232,128]{1,0:T(8,128)S(1)}, f32[1232,128]{1,0:T(8,128)S(1)}, u32[]{:S(2)}, u32[]{:S(2)}) collective-permute-start(f32[1232,128]{1,0:T(8,128)S(1)} %get-tuple-element.83), channel_id=1, source_target_pairs={{0,2},{6,4},{1,3},{7,5},{8,10},{14,12},{9,11},{15,13},{16,18},{22,... | collective-permute-start | bytes 1892360 | tf_op jit(solution)/shard_map/ppermute | solution.py:597
  24.1 17.3 %collective-permute-start.1 = (f32[784,128]{1,0:T(8,128)S(1)}, f32[784,128]{1,0:T(8,128)S(1)}, u32[]{:S(2)}, u32[]{:S(2)}) collective-permute-start(f32[784,128]{1,0:T(8,128)S(1)} %get-tuple-element.73.refs_0_), channel_id=1, source_target_pairs={{2,4},{4,2},{3,5},{5,3},{10,12},{12,10},{11,13},{13,11},{18,20},{2... | collective-permute-start | bytes 1204232 | tf_op jit(solution)/shard_map/ppermute | solution.py:602
  34.1 15.1 %collective-permute-start.6 = (f32[976,128]{1,0:T(8,128)S(1)}, f32[976,128]{1,0:T(8,128)S(1)}, u32[]{:S(2)}, u32[]{:S(2)}) collective-permute-start(f32[976,128]{1,0:T(8,128)S(1)} %get-tuple-element.87.refs_0_), channel_id=1, source_target_pairs={{2,4},{4,2},{3,5},{5,3},{10,12},{12,10},{11,13},{13,11},{18,20},{2... | collective-permute-start | bytes 1499144 | tf_op jit(solution)/shard_map/ppermute | solution.py:602
  34.8 23.2 %collective-permute-start.8 = (f32[976,128]{1,0:T(8,128)S(1)}, f32[976,128]{1,0:T(8,128)S(1)}, u32[]{:S(2)}, u32[]{:S(2)}) collective-permute-start(f32[976,128]{1,0:T(8,128)S(1)} %get-tuple-element.93), channel_id=1, source_target_pairs={{0,2},{6,4},{1,3},{7,5},{8,10},{14,12},{9,11},{15,13},{16,18},{22,... | collective-permute-start | bytes 1499144 | tf_op jit(solution)/shard_map/ppermute | solution.py:597
  41.8 7.2 %collective-permute-start.3 = (f32[528,128]{1,0:T(8,128)S(1)}, f32[528,128]{1,0:T(8,128)S(1)}, u32[]{:S(2)}, u32[]{:S(2)}) collective-permute-start(f32[528,128]{1,0:T(8,128)S(1)} %get-tuple-element.81), channel_id=1, source_target_pairs={{2,0},{4,6},{3,1},{5,7},{10,8},{12,14},{11,9},{13,15},{18,16},{20,... | collective-permute-start | bytes 811016 | tf_op jit(solution)/shard_map/ppermute | solution.py:608
  47.6 12.6 %collective-permute-start.10 = (f32[976,128]{1,0:T(8,128)S(1)}, f32[976,128]{1,0:T(8,128)S(1)}, u32[]{:S(2)}, u32[]{:S(2)}) collective-permute-start(f32[976,128]{1,0:T(8,128)S(1)} %get-tuple-element.97.refs_0_), channel_id=1, source_target_pairs={{2,4},{4,2},{3,5},{5,3},{10,12},{12,10},{11,13},{13,11},{18,20},{2... | collective-permute-start | bytes 1499144 | tf_op jit(solution)/shard_map/ppermute | solution.py:602
  49.6 10.5 %collective-permute-start.7 = (f32[656,128]{1,0:T(8,128)S(1)}, f32[656,128]{1,0:T(8,128)S(1)}, u32[]{:S(2)}, u32[]{:S(2)}) collective-permute-start(f32[656,128]{1,0:T(8,128)S(1)} %get-tuple-element.91), channel_id=1, source_target_pairs={{2,0},{4,6},{3,1},{5,7},{10,8},{12,14},{11,9},{13,15},{18,16},{20,... | collective-permute-start | bytes 1007624 | tf_op jit(solution)/shard_map/ppermute | solution.py:608
  50.9 16.6 %collective-permute-start.13 = (f32[752,128]{1,0:T(8,128)S(1)}, f32[752,128]{1,0:T(8,128)S(1)}, u32[]{:S(2)}, u32[]{:S(2)}) collective-permute-start(f32[752,128]{1,0:T(8,128)S(1)} %get-tuple-element.105), channel_id=1, source_target_pairs={{0,2},{6,4},{1,3},{7,5},{8,10},{14,12},{9,11},{15,13},{16,18},{22,... | collective-permute-start | bytes 1155080 | tf_op jit(solution)/shard_map/ppermute | solution.py:597
  58.3 13.5 %collective-permute-start.12 = (f32[784,128]{1,0:T(8,128)S(1)}, f32[784,128]{1,0:T(8,128)S(1)}, u32[]{:S(2)}, u32[]{:S(2)}) collective-permute-start(f32[784,128]{1,0:T(8,128)S(1)} %get-tuple-element.102.refs_0_), channel_id=1, source_target_pairs={{2,4},{4,2},{3,5},{5,3},{10,12},{12,10},{11,13},{13,11},{18,20},{2... | collective-permute-start | bytes 1204232 | tf_op jit(solution)/shard_map/ppermute | solution.py:602
  60.7 12.7 %collective-permute-start.11 = (f32[656,128]{1,0:T(8,128)S(1)}, f32[656,128]{1,0:T(8,128)S(1)}, u32[]{:S(2)}, u32[]{:S(2)}) collective-permute-start(f32[656,128]{1,0:T(8,128)S(1)} %get-tuple-element.101), channel_id=1, source_target_pairs={{2,0},{4,6},{3,1},{5,7},{10,8},{12,14},{11,9},{13,15},{18,16},{20,... | collective-permute-start | bytes 1007624 | tf_op jit(solution)/shard_map/ppermute | solution.py:608
  62.0 11.6 %collective-permute-start.17 = (f32[488,128]{1,0:T(8,128)S(1)}, f32[488,128]{1,0:T(8,128)S(1)}, u32[]{:S(2)}, u32[]{:S(2)}) collective-permute-start(f32[488,128]{1,0:T(8,128)S(1)} %get-tuple-element.114), channel_id=1, source_target_pairs={{0,2},{6,4},{1,3},{7,5},{8,10},{14,12},{9,11},{15,13},{16,18},{22,... | collective-permute-start | bytes 749576 | tf_op jit(solution)/shard_map/ppermute | solution.py:597
  67.8 8.8 %collective-permute-start.19 = (f32[592,128]{1,0:T(8,128)S(1)}, f32[592,128]{1,0:T(8,128)S(1)}, u32[]{:S(2)}, u32[]{:S(2)}) collective-permute-start(f32[592,128]{1,0:T(8,128)S(1)} %get-tuple-element.118.refs_0_), channel_id=1, source_target_pairs={{2,4},{4,2},{3,5},{5,3},{10,12},{12,10},{11,13},{13,11},{18,20},{2... | collective-permute-start | bytes 909320 | tf_op jit(solution)/shard_map/ppermute | solution.py:602
  68.5 8.5 %collective-permute-start.5 = (f32[528,128]{1,0:T(8,128)S(1)}, f32[528,128]{1,0:T(8,128)S(1)}, u32[]{:S(2)}, u32[]{:S(2)}) collective-permute-start(f32[528,128]{1,0:T(8,128)S(1)} %get-tuple-element.86.refs_0_), channel_id=1, source_target_pairs={{8,0},{16,8},{24,16},{0,24},{9,1},{17,9},{25,17},{1,25},{10,2},{18... | collective-permute-start | bytes 811016 | tf_op jit(solution)/shard_map/ppermute | solution.py:635
  72.1 9.8 %collective-permute-start.16 = (f32[528,128]{1,0:T(8,128)S(1)}, f32[528,128]{1,0:T(8,128)S(1)}, u32[]{:S(2)}, u32[]{:S(2)}) collective-permute-start(f32[528,128]{1,0:T(8,128)S(1)} %get-tuple-element.112), channel_id=1, source_target_pairs={{2,0},{4,6},{3,1},{5,7},{10,8},{12,14},{11,9},{13,15},{18,16},{20,... | collective-permute-start | bytes 811016 | tf_op jit(solution)/shard_map/ppermute | solution.py:608
  73.7 4.6 %collective-permute-start.18 = (f32[392,128]{1,0:T(8,128)S(1)}, f32[392,128]{1,0:T(8,128)S(1)}, u32[]{:S(2)}, u32[]{:S(2)}) collective-permute-start(f32[392,128]{1,0:T(8,128)S(1)} %get-tuple-element.116.refs_0_), channel_id=1, source_target_pairs={{2,4},{4,2},{3,5},{5,3},{10,12},{12,10},{11,13},{13,11},{18,20},{2... | collective-permute-start | bytes 602120 | tf_op jit(solution)/shard_map/ppermute | solution.py:602
  74.4 8.9 %collective-permute-start.9 = (f32[656,128]{1,0:T(8,128)S(1)}, f32[656,128]{1,0:T(8,128)S(1)}, u32[]{:S(2)}, u32[]{:S(2)}) collective-permute-start(f32[656,128]{1,0:T(8,128)S(1)} %get-tuple-element.96.refs_2_), channel_id=1, source_target_pairs={{0,8},{8,16},{16,24},{24,0},{1,9},{9,17},{17,25},{25,1},{2,10},{10... | collective-permute-start | bytes 1007624 | tf_op jit(solution)/shard_map/ppermute | solution.py:638
  76.5 7.7 %collective-permute-start.14 = (f32[400,128]{1,0:T(8,128)S(1)}, f32[400,128]{1,0:T(8,128)S(1)}, u32[]{:S(2)}, u32[]{:S(2)}) collective-permute-start(f32[400,128]{1,0:T(8,128)S(1)} %get-tuple-element.109.refs_4_), channel_id=1, source_target_pairs={{8,0},{16,8},{24,16},{0,24},{9,1},{17,9},{25,17},{1,25},{10,2},{18... | collective-permute-start | bytes 614408 | tf_op jit(solution)/shard_map/ppermute | solution.py:635
  77.0 10.6 %collective-permute-start.20 = (f32[400,128]{1,0:T(8,128)S(1)}, f32[400,128]{1,0:T(8,128)S(1)}, u32[]{:S(2)}, u32[]{:S(2)}) collective-permute-start(f32[400,128]{1,0:T(8,128)S(1)} %get-tuple-element.128), channel_id=1, source_target_pairs={{2,0},{4,6},{3,1},{5,7},{10,8},{12,14},{11,9},{13,15},{18,16},{20,... | collective-permute-start | bytes 614408 | tf_op jit(solution)/shard_map/ppermute | solution.py:608
  78.3 6.0 %collective-permute-start.15 = (f32[264,128]{1,0:T(8,128)S(1)}, f32[264,128]{1,0:T(8,128)S(1)}, u32[]{:S(2)}, u32[]{:S(2)}) collective-permute-start(f32[264,128]{1,0:T(8,128)S(1)} %get-tuple-element.110.refs_6_), channel_id=1, source_target_pairs={{0,8},{8,16},{16,24},{24,0},{1,9},{9,17},{17,25},{25,1},{2,10},{10... | collective-permute-start | bytes 405512 | tf_op jit(solution)/shard_map/ppermute | solution.py:638
  81.9 9.1 %collective-permute-start.21 = (f32[264,128]{1,0:T(8,128)S(1)}, f32[264,128]{1,0:T(8,128)S(1)}, u32[]{:S(2)}, u32[]{:S(2)}) collective-permute-start(f32[264,128]{1,0:T(8,128)S(1)} %get-tuple-element.130), channel_id=1, source_target_pairs={{2,0},{4,6},{3,1},{5,7},{10,8},{12,14},{11,9},{13,15},{18,16},{20,... | collective-permute-start | bytes 405512 | tf_op jit(solution)/shard_map/ppermute | solution.py:608

commit v5 on v4

--- a/solution.py
+++ b/solution.py
@@ -107,9 +107,9 @@
         sent_ref[last : last + BLOCK] = jnp.where(own, 0.0, half_rows(mine_ref, days - 1, low_half))
 
 
-def gram_kernel(parts, counts_ref, year_ref, samples_ref, after_ref, *refs):
+def gram_kernel(parts, counts_from, year_ref, samples_ref, after_ref, *refs):
     outs, sents = refs[: len(parts)], refs[len(parts) : 2 * len(parts)]
-    token_ref, held, arrived = refs[2 * len(parts) :]
+    token_ref, held, arrived, counts_ref, counted = refs[2 * len(parts) :]
     low_half = year_ref[0] < 2
     groups, slots, width = held.shape[1:]
     lane = lax.broadcasted_iota(jnp.int32, (1, LANES), 1)
@@ -126,6 +126,10 @@
     for slot in range(min(AHEAD, len(order))):
         for copy in copies(order[slot], slot):
             copy.start()
+
+    counting = pltpu.make_async_copy(counts_from, counts_ref, counted)
+    counting.start()
+    counting.wait()
 
     def later(slot):
         day, at = jnp.int32(0), 0
@@ -192,11 +196,13 @@
     outs, token = call(
         functools.partial(gram_kernel, parts),
         (counts, year, samples, after),
-        (SCALARS, SCALARS, ANYWHERE, ANYWHERE),
+        (ANYWHERE, SCALARS, ANYWHERE, ANYWHERE),
         [(size, LANES) for size in rows],
         [
             pltpu.VMEM((days, groups, slots, width), samples.dtype),
             pltpu.SemaphoreType.DMA((days, groups)),
+            pltpu.SMEM(counts.shape, counts.dtype),
+            pltpu.SemaphoreType.DMA(()),
         ],
         2 * days * groups * slots * width * width,
         2 * days * groups * slots * width + 4 * sum(rows) * LANES,

time: 93.9 us -> 93.4 us (level)
  Pallas kernels: 32.3 us -> 30.1 us
  waiting for transfers between devices: 15.7 us -> 17.3 us
    pallas_call x22, Pallas kernels: 32.3 us -> 30.1 us  [call(): pl.pallas_call(kernel, in_specs=list(specs), out_specs=(list(outs) if out...]
    ppermute x6, waiting for transfers between devices: 5.64 us -> 7.24 us  [gram_step(): mine[k] = (out, lax.ppermute(sent, 'year', inward))]
  transfers between devices with their start and end apart: 22 -> 22, of which waited for: 10 -> 10; matrix products, arithmetic and copies ran while one was open for 0% -> 0% of each run, Pallas kernels for 27% -> 25%
where the time goes in v5:
time: 93.4 us; the launch traced here: 92.9 us
  starting transfers between devices  43.8 us (47%)
  Pallas kernels  30.1 us (32%)
  waiting for transfers between devices  17.3 us (19%)
  between operations  0.98 us (1%)
    pallas_call x22, Pallas kernels, call(): pl.pallas_call(kernel, in_specs=list(specs), out_specs=(list(outs) if out...  30.1 us
    ppermute x6, starting transfers between devices, gram_step(): mine[k] = (out, lax.ppermute(sent, 'year', inward))  24.9 us
    ppermute x6, waiting for transfers between devices, cross_step(): came = lax.ppermute(send, 'year', outward)  8.95 us
    ppermute x6, starting transfers between devices, cross_step(): came = lax.ppermute(send, 'year', outward)  7.73 us
    ppermute x6, waiting for transfers between devices, gram_step(): mine[k] = (out, lax.ppermute(sent, 'year', inward))  7.24 us
    ppermute x6, starting transfers between devices, inner_step(): sums[k] = (send, keep, lax.ppermute(send, 'year', between))  4.11 us
    ppermute x2, starting transfers between devices, pick_step(): totals.append(lax.ppermute(out, 'day', right))  3.78 us
    ppermute x2, starting transfers between devices, pick_step(): totals.append(lax.ppermute(out, 'day', left))  3.31 us
  transfers between devices with their start and end apart: 22, of which 10 were waited for; matrix products, arithmetic and copies ran while one was open for 0% of the time, Pallas kernels for 25%

profile of v5, /device:TPU:1, one launch (start us, length us, event | category | flops | bytes accessed | tf_op | source)
XLA Modules:
  0.0 92.9 jit_solution(4165677177067014919)
XLA Ops:
  0.6 0.0 copy-start
  0.7 0.7 copy-done
  1.3 4.2 %shard_map.41 = (f32[1040,128]{1,0:T(8,128)S(1)}, f32[976,128]{1,0:T(8,128)S(1)}, f32[8,128]{1,0:T(8,128)S(1)}) custom-call(s32[1,2,23]{2,1,0:T(2,128)S(1)} %bitcast.3, s32[1]{0:T(128)} %bitcast.year_ref, bf16[23,2,1000,256]{3,2,1,0:T(8,128)(2,1)} %samples_ref.7, f32[8,128]{1,0:T(8,128)S(1)} %broadcast_in_dim.7.after_ref), custom_call_target="tpu_custom_call" | custom-call | tf_op jit(solution)/shard_map/pallas_call | solution.py:33
  5.6 4.1 %collective-permute-start = (f32[976,128]{1,0:T(8,128)S(1)}, f32[976,128]{1,0:T(8,128)S(1)}, u32[]{:S(2)}, u32[]{:S(2)}) collective-permute-start(f32[976,128]{1,0:T(8,128)S(1)} %get-tuple-element.69), channel_id=1, source_target_pairs={{0,2},{6,4},{1,3},{7,5},{8,10},{14,12},{9,11},{15,13},{16,18},{22,... | collective-permute-start | bytes 1499144 | tf_op jit(solution)/shard_map/ppermute | solution.py:603
  9.6 4.9 %shard_map.42 = (f32[1296,128]{1,0:T(8,128)S(1)}, f32[1232,128]{1,0:T(8,128)S(1)}, f32[8,128]{1,0:T(8,128)S(1)}) custom-call(s32[1,2,23]{2,1,0:T(2,128)S(1)} %bitcast.4, s32[1]{0:T(128)} %bitcast.year_ref, bf16[23,2,1000,256]{3,2,1,0:T(8,128)(2,1)} %samples_ref.7, f32[8,128]{1,0:T(8,128)S(1)} %get-tuple-element.70.after_ref), custom_call_target="tpu_custom_call" | custom-call | tf_op jit(solution)/shard_map/pallas_call | solution.py:33
  14.5 1.3 %collective-permute-start.2 = (f32[1232,128]{1,0:T(8,128)S(1)}, f32[1232,128]{1,0:T(8,128)S(1)}, u32[]{:S(2)}, u32[]{:S(2)}) collective-permute-start(f32[1232,128]{1,0:T(8,128)S(1)} %get-tuple-element.76), channel_id=1, source_target_pairs={{0,2},{6,4},{1,3},{7,5},{8,10},{14,12},{9,11},{15,13},{16,18},{22,... | collective-permute-start | bytes 1892360 | tf_op jit(solution)/shard_map/ppermute | solution.py:603
  15.9 4.9 %shard_map.43 = (f32[1296,128]{1,0:T(8,128)S(1)}, f32[1232,128]{1,0:T(8,128)S(1)}, f32[8,128]{1,0:T(8,128)S(1)}) custom-call(s32[1,2,23]{2,1,0:T(2,128)S(1)} %bitcast.5, s32[1]{0:T(128)} %bitcast.year_ref, bf16[23,2,1000,256]{3,2,1,0:T(8,128)(2,1)} %samples_ref.7, f32[8,128]{1,0:T(8,128)S(1)} %get-tuple-element.71.after_ref), custom_call_target="tpu_custom_call" | custom-call | tf_op jit(solution)/shard_map/pallas_call | solution.py:33
  20.8 1.3 %collective-permute-start.4 = (f32[1232,128]{1,0:T(8,128)S(1)}, f32[1232,128]{1,0:T(8,128)S(1)}, u32[]{:S(2)}, u32[]{:S(2)}) collective-permute-start(f32[1232,128]{1,0:T(8,128)S(1)} %get-tuple-element.83), channel_id=1, source_target_pairs={{0,2},{6,4},{1,3},{7,5},{8,10},{14,12},{9,11},{15,13},{16,18},{22,... | collective-permute-start | bytes 1892360 | tf_op jit(solution)/shard_map/ppermute | solution.py:603
  22.1 0.0 collective-permute-done.came_ref
  22.1 0.4 shard_map.44
  22.5 0.7 collective-permute-start.1
  23.2 7.9 %shard_map.45 = (f32[1040,128]{1,0:T(8,128)S(1)}, f32[784,128]{1,0:T(8,128)S(1)}, f32[520,128]{1,0:T(8,128)S(1)}, f32[976,128]{1,0:T(8,128)S(1)}, f32[752,128]{1...) custom-call(s32[1,2,23]{2,1,0:T(2,128)S(1)} %bitcast.6, s32[1]{0:T(128)} %bitcast.year_ref, ...), custom_call_target="tpu_custom_call" | custom-call | tf_op jit(solution)/shard_map/pallas_call | solution.py:33
  31.1 2.1 %collective-permute-done.2.came_ref = f32[1232,128]{1,0:T(8,128)S(1)} collective-permute-done((f32[1232,128]{1,0:T(8,128)S(1)}, f32[1232,128]{1,0:T(8,128)S(1)}, u32[]{:S(2)}, u32[]{:S(2)}) %collective-permute-start.2) | collective-permute-done | bytes 630816 | tf_op jit(solution)/shard_map/ppermute | solution.py:603
  33.2 0.4 shard_map.46
  33.5 0.7 collective-permute-start.6
  34.2 6.7 %collective-permute-start.8 = (f32[976,128]{1,0:T(8,128)S(1)}, f32[976,128]{1,0:T(8,128)S(1)}, u32[]{:S(2)}, u32[]{:S(2)}) collective-permute-start(f32[976,128]{1,0:T(8,128)S(1)} %get-tuple-element.93), channel_id=1, source_target_pairs={{0,2},{6,4},{1,3},{7,5},{8,10},{14,12},{9,11},{15,13},{16,18},{22,... | collective-permute-start | bytes 1499144 | tf_op jit(solution)/shard_map/ppermute | solution.py:603
  40.9 0.0 collective-permute-done.1.refs_2_
  40.9 0.4 shard_map.47
  41.3 1.3 %collective-permute-start.3 = (f32[528,128]{1,0:T(8,128)S(1)}, f32[528,128]{1,0:T(8,128)S(1)}, u32[]{:S(2)}, u32[]{:S(2)}) collective-permute-start(f32[528,128]{1,0:T(8,128)S(1)} %get-tuple-element.81), channel_id=1, source_target_pairs={{2,0},{4,6},{3,1},{5,7},{10,8},{12,14},{11,9},{13,15},{18,16},{20,... | collective-permute-start | bytes 811016 | tf_op jit(solution)/shard_map/ppermute | solution.py:614
  42.6 4.1 %collective-permute-done.4.came_ref = f32[1232,128]{1,0:T(8,128)S(1)} collective-permute-done((f32[1232,128]{1,0:T(8,128)S(1)}, f32[1232,128]{1,0:T(8,128)S(1)}, u32[]{:S(2)}, u32[]{:S(2)}) %collective-permute-start.4) | collective-permute-done | bytes 630816 | tf_op jit(solution)/shard_map/ppermute | solution.py:603
  46.7 0.4 shard_map.48
  47.1 0.7 collective-permute-start.10
  47.8 0.7 collective-permute-done.3.refs_2_
  48.5 0.1 shard_map.49
  48.6 0.0 collective-permute-done.6.refs_2_
  48.6 0.5 shard_map.50
  49.1 1.3 %collective-permute-start.7 = (f32[656,128]{1,0:T(8,128)S(1)}, f32[656,128]{1,0:T(8,128)S(1)}, u32[]{:S(2)}, u32[]{:S(2)}) collective-permute-start(f32[656,128]{1,0:T(8,128)S(1)} %get-tuple-element.91), channel_id=1, source_target_pairs={{2,0},{4,6},{3,1},{5,7},{10,8},{12,14},{11,9},{13,15},{18,16},{20,... | collective-permute-start | bytes 1007624 | tf_op jit(solution)/shard_map/ppermute | solution.py:614
  50.4 5.9 %collective-permute-start.13 = (f32[752,128]{1,0:T(8,128)S(1)}, f32[752,128]{1,0:T(8,128)S(1)}, u32[]{:S(2)}, u32[]{:S(2)}) collective-permute-start(f32[752,128]{1,0:T(8,128)S(1)} %get-tuple-element.105), channel_id=1, source_target_pairs={{0,2},{6,4},{1,3},{7,5},{8,10},{14,12},{9,11},{15,13},{16,18},{22,... | collective-permute-start | bytes 1155080 | tf_op jit(solution)/shard_map/ppermute | solution.py:603
  56.3 1.1 %collective-permute-done.8.came_ref = f32[976,128]{1,0:T(8,128)S(1)} collective-permute-done((f32[976,128]{1,0:T(8,128)S(1)}, f32[976,128]{1,0:T(8,128)S(1)}, u32[]{:S(2)}, u32[]{:S(2)}) %collective-permute-start.8) | collective-permute-done | bytes 499744 | tf_op jit(solution)/shard_map/ppermute | solution.py:603
  57.4 0.4 shard_map.51
  57.8 0.7 collective-permute-start.12
  58.5 1.1 %collective-permute-done.7.refs_2_ = f32[656,128]{1,0:T(8,128)S(1)} collective-permute-done((f32[656,128]{1,0:T(8,128)S(1)}, f32[656,128]{1,0:T(8,128)S(1)}, u32[]{:S(2)}, u32[]{:S(2)}) %collective-permute-start.7) | collective-permute-done | bytes 335904 | tf_op jit(solution)/shard_map/ppermute | solution.py:614
  59.6 0.1 shard_map.52
  59.7 0.0 collective-permute-done.10.refs_2_
  59.7 0.5 shard_map.53
  60.2 1.3 %collective-permute-start.11 = (f32[656,128]{1,0:T(8,128)S(1)}, f32[656,128]{1,0:T(8,128)S(1)}, u32[]{:S(2)}, u32[]{:S(2)}) collective-permute-start(f32[656,128]{1,0:T(8,128)S(1)} %get-tuple-element.101), channel_id=1, source_target_pairs={{2,0},{4,6},{3,1},{5,7},{10,8},{12,14},{11,9},{13,15},{18,16},{20,... | collective-permute-start | bytes 1007624 | tf_op jit(solution)/shard_map/ppermute | solution.py:614
  61.5 5.6 %collective-permute-start.17 = (f32[488,128]{1,0:T(8,128)S(1)}, f32[488,128]{1,0:T(8,128)S(1)}, u32[]{:S(2)}, u32[]{:S(2)}) collective-permute-start(f32[488,128]{1,0:T(8,128)S(1)} %get-tuple-element.114), channel_id=1, source_target_pairs={{0,2},{6,4},{1,3},{7,5},{8,10},{14,12},{9,11},{15,13},{16,18},{22,... | collective-permute-start | bytes 749576 | tf_op jit(solution)/shard_map/ppermute | solution.py:603
  67.0 0.0 collective-permute-done.13.came_ref
  67.0 0.2 shard_map.54
  67.2 0.7 collective-permute-start.19
  67.9 3.3 %collective-permute-start.5 = (f32[528,128]{1,0:T(8,128)S(1)}, f32[528,128]{1,0:T(8,128)S(1)}, u32[]{:S(2)}, u32[]{:S(2)}) collective-permute-start(f32[528,128]{1,0:T(8,128)S(1)} %get-tuple-element.86.refs_0_), channel_id=1, source_target_pairs={{8,0},{16,8},{24,16},{0,24},{9,1},{17,9},{25,17},{1,25},{10,2},{18... | collective-permute-start | bytes 811016 | tf_op jit(solution)/shard_map/ppermute | solution.py:641
  71.2 0.0 collective-permute-done.12.refs_2_
  71.2 0.4 shard_map.55
  71.6 1.3 %collective-permute-start.16 = (f32[528,128]{1,0:T(8,128)S(1)}, f32[528,128]{1,0:T(8,128)S(1)}, u32[]{:S(2)}, u32[]{:S(2)}) collective-permute-start(f32[528,128]{1,0:T(8,128)S(1)} %get-tuple-element.112), channel_id=1, source_target_pairs={{2,0},{4,6},{3,1},{5,7},{10,8},{12,14},{11,9},{13,15},{18,16},{20,... | collective-permute-start | bytes 811016 | tf_op jit(solution)/shard_map/ppermute | solution.py:614
  72.9 0.0 collective-permute-done.11.refs_2_
  72.9 0.1 shard_map.56
  73.0 0.0 collective-permute-done.17.came_ref
  73.0 0.2 shard_map.57
  73.2 0.7 collective-permute-start.18
  73.9 2.1 %collective-permute-start.9 = (f32[656,128]{1,0:T(8,128)S(1)}, f32[656,128]{1,0:T(8,128)S(1)}, u32[]{:S(2)}, u32[]{:S(2)}) collective-permute-start(f32[656,128]{1,0:T(8,128)S(1)} %get-tuple-element.96.refs_2_), channel_id=1, source_target_pairs={{0,8},{8,16},{16,24},{24,0},{1,9},{9,17},{17,25},{25,1},{2,10},{10... | collective-permute-start | bytes 1007624 | tf_op jit(solution)/shard_map/ppermute | solution.py:644
  76.0 0.0 collective-permute-done.19.refs_2_
  76.0 0.3 shard_map.58
  76.3 0.2 collective-permute-done.5.refs_1_
  76.5 1.3 %collective-permute-start.20 = (f32[400,128]{1,0:T(8,128)S(1)}, f32[400,128]{1,0:T(8,128)S(1)}, u32[]{:S(2)}, u32[]{:S(2)}) collective-permute-start(f32[400,128]{1,0:T(8,128)S(1)} %get-tuple-element.128), channel_id=1, source_target_pairs={{2,0},{4,6},{3,1},{5,7},{10,8},{12,14},{11,9},{13,15},{18,16},{20,... | collective-permute-start | bytes 614408 | tf_op jit(solution)/shard_map/ppermute | solution.py:614
  77.8 1.6 %collective-permute-start.15 = (f32[264,128]{1,0:T(8,128)S(1)}, f32[264,128]{1,0:T(8,128)S(1)}, u32[]{:S(2)}, u32[]{:S(2)}) collective-permute-start(f32[264,128]{1,0:T(8,128)S(1)} %get-tuple-element.110.refs_6_), channel_id=1, source_target_pairs={{0,8},{8,16},{16,24},{24,0},{1,9},{9,17},{17,25},{25,1},{2,10},{10... | collective-permute-start | bytes 405512 | tf_op jit(solution)/shard_map/ppermute | solution.py:644
  79.4 0.2 shard_map.59
  79.6 1.8 %collective-permute-done.16.refs_2_ = f32[528,128]{1,0:T(8,128)S(1)} collective-permute-done((f32[528,128]{1,0:T(8,128)S(1)}, f32[528,128]{1,0:T(8,128)S(1)}, u32[]{:S(2)}, u32[]{:S(2)}) %collective-permute-start.16) | collective-permute-done | bytes 270368 | tf_op jit(solution)/shard_map/ppermute | solution.py:614
  81.4 1.3 %collective-permute-start.21 = (f32[264,128]{1,0:T(8,128)S(1)}, f32[264,128]{1,0:T(8,128)S(1)}, u32[]{:S(2)}, u32[]{:S(2)}) collective-permute-start(f32[264,128]{1,0:T(8,128)S(1)} %get-tuple-element.130), channel_id=1, source_target_pairs={{2,0},{4,6},{3,1},{5,7},{10,8},{12,14},{11,9},{13,15},{18,16},{20,... | collective-permute-start | bytes 405512 | tf_op jit(solution)/shard_map/ppermute | solution.py:614
  82.7 0.1 shard_map.60
  82.8 1.0 %collective-permute-done.15.refs_7_ = f32[264,128]{1,0:T(8,128)S(1)} collective-permute-done((f32[264,128]{1,0:T(8,128)S(1)}, f32[264,128]{1,0:T(8,128)S(1)}, u32[]{:S(2)}, u32[]{:S(2)}) %collective-permute-start.15) | collective-permute-done | bytes 135200 | tf_op jit(solution)/shard_map/ppermute | solution.py:644
  83.8 1.4 %shard_map.61 = (f32[23,64,256]{2,1,0:T(8,128)S(1)}, f32[4,23,128]{2,1,0:T(8,128)S(1)}, f32[8,128]{1,0:T(8,128)S(1)}) custom-call(s32[1]{0:T(128)} %bitcast.year_ref, f32[528,128]{1,0:T(8,128)S(1)} %get-tuple-element.86.refs_0_, f32[528,128]{1,0:T(8,128)S(1)} %collective-permute-done.5.refs_1_, f32[656,128]{1,0:T(8,128)S(1)} %get-tuple-element.96.refs_2_, ...), custom_call_target="tpu_custom_call" | custom-call | tf_op jit(solution)/shard_map/pallas_call | solution.py:33
  85.2 1.9 %collective-permute-done.20.refs_2_ = f32[400,128]{1,0:T(8,128)S(1)} collective-permute-done((f32[400,128]{1,0:T(8,128)S(1)}, f32[400,128]{1,0:T(8,128)S(1)}, u32[]{:S(2)}, u32[]{:S(2)}) %collective-permute-start.20) | collective-permute-done | bytes 204832 | tf_op jit(solution)/shard_map/ppermute | solution.py:614
  87.1 3.4 %collective-permute-done.21.refs_5_ = f32[264,128]{1,0:T(8,128)S(1)} collective-permute-done((f32[264,128]{1,0:T(8,128)S(1)}, f32[264,128]{1,0:T(8,128)S(1)}, u32[]{:S(2)}, u32[]{:S(2)}) %collective-permute-start.21) | collective-permute-done | bytes 135200 | tf_op jit(solution)/shard_map/ppermute | solution.py:614
  90.5 2.4 %shard_map.62 = (f32[1,23,64,256]{3,2,1,0:T(8,128)}, f32[23,1,64]{2,1,0:T(1,128)}, f32[8,128]{1,0:T(8,128)}) custom-call(s32[1]{0:T(128)} %bitcast.year_ref, f32[23,64,256]{2,1,0:T(8,128)S(1)} %get-tuple-element.125.win_ref, f32[4,23,128]{2,1,0:T(8,128)S(1)} %get-tuple-element.126.small_ref, f32[784,128]{1,0:T(8,128)S(1)} %get-tuple-element.104.mine_ref.refs_0_, ...), custom_call_target="tpu_custom_call" | custom-call | tf_op jit(solution)/shard_map/pallas_call | solution.py:33
  (5 shorter events, 0.0 us)
Async XLA Ops:
  0.6 0.7 copy-start
  5.6 16.5 %collective-permute-start = (f32[976,128]{1,0:T(8,128)S(1)}, f32[976,128]{1,0:T(8,128)S(1)}, u32[]{:S(2)}, u32[]{:S(2)}) collective-permute-start(f32[976,128]{1,0:T(8,128)S(1)} %get-tuple-element.69), channel_id=1, source_target_pairs={{0,2},{6,4},{1,3},{7,5},{8,10},{14,12},{9,11},{15,13},{16,18},{22,... | collective-permute-start | bytes 1499144 | tf_op jit(solution)/shard_map/ppermute | solution.py:603
  14.5 18.6 %collective-permute-start.2 = (f32[1232,128]{1,0:T(8,128)S(1)}, f32[1232,128]{1,0:T(8,128)S(1)}, u32[]{:S(2)}, u32[]{:S(2)}) collective-permute-start(f32[1232,128]{1,0:T(8,128)S(1)} %get-tuple-element.76), channel_id=1, source_target_pairs={{0,2},{6,4},{1,3},{7,5},{8,10},{14,12},{9,11},{15,13},{16,18},{22,... | collective-permute-start | bytes 1892360 | tf_op jit(solution)/shard_map/ppermute | solution.py:603
  20.8 25.9 %collective-permute-start.4 = (f32[1232,128]{1,0:T(8,128)S(1)}, f32[1232,128]{1,0:T(8,128)S(1)}, u32[]{:S(2)}, u32[]{:S(2)}) collective-permute-start(f32[1232,128]{1,0:T(8,128)S(1)} %get-tuple-element.83), channel_id=1, source_target_pairs={{0,2},{6,4},{1,3},{7,5},{8,10},{14,12},{9,11},{15,13},{16,18},{22,... | collective-permute-start | bytes 1892360 | tf_op jit(solution)/shard_map/ppermute | solution.py:603
  22.5 18.4 %collective-permute-start.1 = (f32[784,128]{1,0:T(8,128)S(1)}, f32[784,128]{1,0:T(8,128)S(1)}, u32[]{:S(2)}, u32[]{:S(2)}) collective-permute-start(f32[784,128]{1,0:T(8,128)S(1)} %get-tuple-element.73.refs_0_), channel_id=1, source_target_pairs={{2,4},{4,2},{3,5},{5,3},{10,12},{12,10},{11,13},{13,11},{18,20},{2... | collective-permute-start | bytes 1204232 | tf_op jit(solution)/shard_map/ppermute | solution.py:608
  33.5 15.1 %collective-permute-start.6 = (f32[976,128]{1,0:T(8,128)S(1)}, f32[976,128]{1,0:T(8,128)S(1)}, u32[]{:S(2)}, u32[]{:S(2)}) collective-permute-start(f32[976,128]{1,0:T(8,128)S(1)} %get-tuple-element.87.refs_0_), channel_id=1, source_target_pairs={{2,4},{4,2},{3,5},{5,3},{10,12},{12,10},{11,13},{13,11},{18,20},{2... | collective-permute-start | bytes 1499144 | tf_op jit(solution)/shard_map/ppermute | solution.py:608
  34.2 23.2 %collective-permute-start.8 = (f32[976,128]{1,0:T(8,128)S(1)}, f32[976,128]{1,0:T(8,128)S(1)}, u32[]{:S(2)}, u32[]{:S(2)}) collective-permute-start(f32[976,128]{1,0:T(8,128)S(1)} %get-tuple-element.93), channel_id=1, source_target_pairs={{0,2},{6,4},{1,3},{7,5},{8,10},{14,12},{9,11},{15,13},{16,18},{22,... | collective-permute-start | bytes 1499144 | tf_op jit(solution)/shard_map/ppermute | solution.py:603
  41.3 7.2 %collective-permute-start.3 = (f32[528,128]{1,0:T(8,128)S(1)}, f32[528,128]{1,0:T(8,128)S(1)}, u32[]{:S(2)}, u32[]{:S(2)}) collective-permute-start(f32[528,128]{1,0:T(8,128)S(1)} %get-tuple-element.81), channel_id=1, source_target_pairs={{2,0},{4,6},{3,1},{5,7},{10,8},{12,14},{11,9},{13,15},{18,16},{20,... | collective-permute-start | bytes 811016 | tf_op jit(solution)/shard_map/ppermute | solution.py:614
  47.1 12.6 %collective-permute-start.10 = (f32[976,128]{1,0:T(8,128)S(1)}, f32[976,128]{1,0:T(8,128)S(1)}, u32[]{:S(2)}, u32[]{:S(2)}) collective-permute-start(f32[976,128]{1,0:T(8,128)S(1)} %get-tuple-element.97.refs_0_), channel_id=1, source_target_pairs={{2,4},{4,2},{3,5},{5,3},{10,12},{12,10},{11,13},{13,11},{18,20},{2... | collective-permute-start | bytes 1499144 | tf_op jit(solution)/shard_map/ppermute | solution.py:608
  49.1 10.5 %collective-permute-start.7 = (f32[656,128]{1,0:T(8,128)S(1)}, f32[656,128]{1,0:T(8,128)S(1)}, u32[]{:S(2)}, u32[]{:S(2)}) collective-permute-start(f32[656,128]{1,0:T(8,128)S(1)} %get-tuple-element.91), channel_id=1, source_target_pairs={{2,0},{4,6},{3,1},{5,7},{10,8},{12,14},{11,9},{13,15},{18,16},{20,... | collective-permute-start | bytes 1007624 | tf_op jit(solution)/shard_map/ppermute | solution.py:614
  50.4 16.6 %collective-permute-start.13 = (f32[752,128]{1,0:T(8,128)S(1)}, f32[752,128]{1,0:T(8,128)S(1)}, u32[]{:S(2)}, u32[]{:S(2)}) collective-permute-start(f32[752,128]{1,0:T(8,128)S(1)} %get-tuple-element.105), channel_id=1, source_target_pairs={{0,2},{6,4},{1,3},{7,5},{8,10},{14,12},{9,11},{15,13},{16,18},{22,... | collective-permute-start | bytes 1155080 | tf_op jit(solution)/shard_map/ppermute | solution.py:603
  57.8 13.5 %collective-permute-start.12 = (f32[784,128]{1,0:T(8,128)S(1)}, f32[784,128]{1,0:T(8,128)S(1)}, u32[]{:S(2)}, u32[]{:S(2)}) collective-permute-start(f32[784,128]{1,0:T(8,128)S(1)} %get-tuple-element.102.refs_0_), channel_id=1, source_target_pairs={{2,4},{4,2},{3,5},{5,3},{10,12},{12,10},{11,13},{13,11},{18,20},{2... | collective-permute-start | bytes 1204232 | tf_op jit(solution)/shard_map/ppermute | solution.py:608
  60.2 12.7 %collective-permute-start.11 = (f32[656,128]{1,0:T(8,128)S(1)}, f32[656,128]{1,0:T(8,128)S(1)}, u32[]{:S(2)}, u32[]{:S(2)}) collective-permute-start(f32[656,128]{1,0:T(8,128)S(1)} %get-tuple-element.101), channel_id=1, source_target_pairs={{2,0},{4,6},{3,1},{5,7},{10,8},{12,14},{11,9},{13,15},{18,16},{20,... | collective-permute-start | bytes 1007624 | tf_op jit(solution)/shard_map/ppermute | solution.py:614
  61.5 11.6 %collective-permute-start.17 = (f32[488,128]{1,0:T(8,128)S(1)}, f32[488,128]{1,0:T(8,128)S(1)}, u32[]{:S(2)}, u32[]{:S(2)}) collective-permute-start(f32[488,128]{1,0:T(8,128)S(1)} %get-tuple-element.114), channel_id=1, source_target_pairs={{0,2},{6,4},{1,3},{7,5},{8,10},{14,12},{9,11},{15,13},{16,18},{22,... | collective-permute-start | bytes 749576 | tf_op jit(solution)/shard_map/ppermute | solution.py:603
  67.2 8.8 %collective-permute-start.19 = (f32[592,128]{1,0:T(8,128)S(1)}, f32[592,128]{1,0:T(8,128)S(1)}, u32[]{:S(2)}, u32[]{:S(2)}) collective-permute-start(f32[592,128]{1,0:T(8,128)S(1)} %get-tuple-element.118.refs_0_), channel_id=1, source_target_pairs={{2,4},{4,2},{3,5},{5,3},{10,12},{12,10},{11,13},{13,11},{18,20},{2... | collective-permute-start | bytes 909320 | tf_op jit(solution)/shard_map/ppermute | solution.py:608
  67.9 8.5 %collective-permute-start.5 = (f32[528,128]{1,0:T(8,128)S(1)}, f32[528,128]{1,0:T(8,128)S(1)}, u32[]{:S(2)}, u32[]{:S(2)}) collective-permute-start(f32[528,128]{1,0:T(8,128)S(1)} %get-tuple-element.86.refs_0_), channel_id=1, source_target_pairs={{8,0},{16,8},{24,16},{0,24},{9,1},{17,9},{25,17},{1,25},{10,2},{18... | collective-permute-start | bytes 811016 | tf_op jit(solution)/shard_map/ppermute | solution.py:641
  71.6 9.8 %collective-permute-start.16 = (f32[528,128]{1,0:T(8,128)S(1)}, f32[528,128]{1,0:T(8,128)S(1)}, u32[]{:S(2)}, u32[]{:S(2)}) collective-permute-start(f32[528,128]{1,0:T(8,128)S(1)} %get-tuple-element.112), channel_id=1, source_target_pairs={{2,0},{4,6},{3,1},{5,7},{10,8},{12,14},{11,9},{13,15},{18,16},{20,... | collective-permute-start | bytes 811016 | tf_op jit(solution)/shard_map/ppermute | solution.py:614
  73.2 4.6 %collective-permute-start.18 = (f32[392,128]{1,0:T(8,128)S(1)}, f32[392,128]{1,0:T(8,128)S(1)}, u32[]{:S(2)}, u32[]{:S(2)}) collective-permute-start(f32[392,128]{1,0:T(8,128)S(1)} %get-tuple-element.116.refs_0_), channel_id=1, source_target_pairs={{2,4},{4,2},{3,5},{5,3},{10,12},{12,10},{11,13},{13,11},{18,20},{2... | collective-permute-start | bytes 602120 | tf_op jit(solution)/shard_map/ppermute | solution.py:608
  73.9 8.9 %collective-permute-start.9 = (f32[656,128]{1,0:T(8,128)S(1)}, f32[656,128]{1,0:T(8,128)S(1)}, u32[]{:S(2)}, u32[]{:S(2)}) collective-permute-start(f32[656,128]{1,0:T(8,128)S(1)} %get-tuple-element.96.refs_2_), channel_id=1, source_target_pairs={{0,8},{8,16},{16,24},{24,0},{1,9},{9,17},{17,25},{25,1},{2,10},{10... | collective-permute-start | bytes 1007624 | tf_op jit(solution)/shard_map/ppermute | solution.py:644
  76.0 7.7 %collective-permute-start.14 = (f32[400,128]{1,0:T(8,128)S(1)}, f32[400,128]{1,0:T(8,128)S(1)}, u32[]{:S(2)}, u32[]{:S(2)}) collective-permute-start(f32[400,128]{1,0:T(8,128)S(1)} %get-tuple-element.109.refs_4_), channel_id=1, source_target_pairs={{8,0},{16,8},{24,16},{0,24},{9,1},{17,9},{25,17},{1,25},{10,2},{18... | collective-permute-start | bytes 614408 | tf_op jit(solution)/shard_map/ppermute | solution.py:641
  76.5 10.6 %collective-permute-start.20 = (f32[400,128]{1,0:T(8,128)S(1)}, f32[400,128]{1,0:T(8,128)S(1)}, u32[]{:S(2)}, u32[]{:S(2)}) collective-permute-start(f32[400,128]{1,0:T(8,128)S(1)} %get-tuple-element.128), channel_id=1, source_target_pairs={{2,0},{4,6},{3,1},{5,7},{10,8},{12,14},{11,9},{13,15},{18,16},{20,... | collective-permute-start | bytes 614408 | tf_op jit(solution)/shard_map/ppermute | solution.py:614
  77.8 6.0 %collective-permute-start.15 = (f32[264,128]{1,0:T(8,128)S(1)}, f32[264,128]{1,0:T(8,128)S(1)}, u32[]{:S(2)}, u32[]{:S(2)}) collective-permute-start(f32[264,128]{1,0:T(8,128)S(1)} %get-tuple-element.110.refs_6_), channel_id=1, source_target_pairs={{0,8},{8,16},{16,24},{24,0},{1,9},{9,17},{17,25},{25,1},{2,10},{10... | collective-permute-start | bytes 405512 | tf_op jit(solution)/shard_map/ppermute | solution.py:644
  81.4 9.1 %collective-permute-start.21 = (f32[264,128]{1,0:T(8,128)S(1)}, f32[264,128]{1,0:T(8,128)S(1)}, u32[]{:S(2)}, u32[]{:S(2)}) collective-permute-start(f32[264,128]{1,0:T(8,128)S(1)} %get-tuple-element.130), channel_id=1, source_target_pairs={{2,0},{4,6},{3,1},{5,7},{10,8},{12,14},{11,9},{13,15},{18,16},{20,... | collective-permute-start | bytes 405512 | tf_op jit(solution)/shard_map/ppermute | solution.py:614
